TPU v7x, 32 devices: a whole 2x2x4 slice. The times are simulated.
32 devices in a mesh: sec: 2 (over x), gx: 4 (over y, core), gy: 4 (over z).
Axes of the slice: x: 2, y: 2, z: 4, core: 2. Of those that a mesh axis runs over, the one named last changes fastest.
Arguments:
- fields: float32 [2, 5, 128, 1024], P('sec', None, 'gx', 'gy'), may hold values from -1.5 to 6, as said below
- stored_rates: bfloat16 [2, 3, 5, 128, 1024], P('sec', None, None, 'gx', 'gy'), may hold values from -6 to 6
Outputs:
- advanced: float32 [2, 5, 128, 1024], P('sec', None, 'gx', 'gy')
Inputs may be any that keep to these rules, and one draw needn't show every extreme that they name: `fields`: for every level and cell: density in [0.6, 1.4], every velocity component within 0.9 in magnitude, pressure in [0.6, 1.4]; momenta are density times velocity and energy is pressure / 0.4 plus density times kinetic energy.
All inputs are finite; a program needn't handle non-finite values.
Results may differ from a plain program's by a relative error of at most 0.0005.
Values may be sent and summed in bfloat16 or wider, within the bound.
No kernel may reach another device: no remote copies, remote signals or barrier semaphores. Data moves between devices by JAX's collectives and lax.ppermute only.
A program may use at most 64 MiB of HBM per device.

v0:
```python
import jax
import jax.numpy as jnp
from jax import lax
from jax.sharding import PartitionSpec as P

NZ = 32
TICKS = 3


TIME_STEP = 0.04
DYNAMIC_FRICTION = 0.4
CONDUCTIVITY = 0.5
GAMMA_LESS = 0.4
QUAD_WEIGHTS = (1.0 / 24.0, -5.0 / 24.0, 19.0 / 24.0, 9.0 / 24.0)


def with_halo(block, sides, width):
    for axis, dim in sides:
        count = lax.axis_size(axis)
        forward = [(i, i + 1) for i in range(count - 1)]
        forward.append((count - 1, 0))
        backward = [(target, source) for source, target in forward]
        low = lax.ppermute(
            lax.slice_in_dim(block, block.shape[dim] - width, None, axis=dim), axis, forward
        )
        high = lax.ppermute(lax.slice_in_dim(block, 0, width, axis=dim), axis, backward)
        block = jnp.concatenate([low, block, high], axis=dim)
    return block


def shifted(block, axis, distance):
    devices = range(lax.axis_size(axis))
    route = [(i - distance, i) for i in devices if i - distance in devices]
    return lax.ppermute(block, axis, route)


def shift_z(values, step, depth):
    column = lax.broadcasted_iota(jnp.int32, values.shape, values.ndim - 1) % depth
    unwrapped = jnp.roll(values, -step, axis=-1)
    if step > 0:
        wrapped = jnp.roll(values, depth - step, axis=-1)
        inside = column + step < depth
    else:
        wrapped = jnp.roll(values, -step - depth, axis=-1)
        inside = column + step >= 0
    return jnp.where(inside, unwrapped, wrapped)


def rates(matter_per_volume, mom_x, mom_y, mom_z, energy, window, depth):
    vel_x = mom_x / matter_per_volume
    vel_y = mom_y / matter_per_volume
    vel_z = mom_z / matter_per_volume
    motion_half_square = 0.5 * (vel_x * vel_x + vel_y * vel_y + vel_z * vel_z)
    normal_stress_scalar = GAMMA_LESS * (energy - matter_per_volume * motion_half_square)
    gas_warmth_field = normal_stress_scalar / matter_per_volume
    enthalpy = energy + normal_stress_scalar

    def diff_x(values):
        return (window(values, 1, 0) - window(values, -1, 0)) * 0.5

    def diff_y(values):
        return (window(values, 0, 1) - window(values, 0, -1)) * 0.5

    def diff_z(values):
        center = window(values, 0, 0)
        return (shift_z(center, 1, depth) - shift_z(center, -1, depth)) * 0.5

    def middle_sweep_tier(values):
        center = window(values, 0, 0)
        along_x = window(values, 2, 0) - 2.0 * center + window(values, -2, 0)
        along_y = window(values, 0, 2) - 2.0 * center + window(values, 0, -2)
        along_z = shift_z(center, 2, depth) - 2.0 * center + shift_z(center, -2, depth)
        return (along_x + along_y + along_z) * 0.25

    mass = -(diff_x(mom_x) + diff_y(mom_y) + diff_z(mom_z))
    flow_x = -(
        diff_x(mom_x * vel_x + normal_stress_scalar) + diff_y(mom_x * vel_y) + diff_z(mom_x * vel_z)
    ) + DYNAMIC_FRICTION * middle_sweep_tier(vel_x)
    flow_y = -(
        diff_x(mom_y * vel_x) + diff_y(mom_y * vel_y + normal_stress_scalar) + diff_z(mom_y * vel_z)
    ) + DYNAMIC_FRICTION * middle_sweep_tier(vel_y)
    flow_z = -(
        diff_x(mom_z * vel_x) + diff_y(mom_z * vel_y) + diff_z(mom_z * vel_z + normal_stress_scalar)
    ) + DYNAMIC_FRICTION * middle_sweep_tier(vel_z)
    conducted_warmth_current = -(
        diff_x(enthalpy * vel_x) + diff_y(enthalpy * vel_y) + diff_z(enthalpy * vel_z)
    )
    conducted_warmth_current = (
        conducted_warmth_current
        + DYNAMIC_FRICTION * middle_sweep_tier(motion_half_square)
        + CONDUCTIVITY * middle_sweep_tier(gas_warmth_field)
    )
    return jnp.stack([mass, flow_x, flow_y, flow_z, conducted_warmth_current])


def padded_rates(block):
    rows_x = block.shape[1]
    cols_yz = block.shape[2]
    x_padded = with_halo(block.astype(jnp.bfloat16), (("gx", 1),), 2).astype(block.dtype)
    xy_padded = with_halo(x_padded.astype(jnp.bfloat16), (("gy", 2),), 2 * NZ).astype(
        x_padded.dtype
    )

    def window(values, across, along):
        return values[
            2 + across : 2 + across + rows_x, (2 + along) * NZ : (2 + along) * NZ + cols_yz
        ]

    return rates(xy_padded[0], xy_padded[1], xy_padded[2], xy_padded[3], xy_padded[4], window, NZ)


def per_device(fields, stored_rates):
    levels = min(4, lax.axis_size("sec"))
    level_zero = lax.axis_index("sec") % levels == 0
    current = fields[0]
    stored = stored_rates[0]
    for tick_count in range(TICKS):
        own_rates = padded_rates(current)
        arrived_rates = shifted(own_rates.astype(jnp.bfloat16), "sec", 1)
        fresh_rates = jnp.where(level_zero, jnp.zeros_like(arrived_rates), arrived_rates)
        quadrature = (
            QUAD_WEIGHTS[0] * stored[0].astype(jnp.float32)
            + QUAD_WEIGHTS[1] * stored[1].astype(jnp.float32)
            + QUAD_WEIGHTS[2] * stored[2].astype(jnp.float32)
            + QUAD_WEIGHTS[3] * fresh_rates.astype(jnp.float32)
        )
        correction = quadrature - stored[2].astype(jnp.float32)
        current = current + TIME_STEP * (
            own_rates + jnp.where(level_zero, jnp.float32(0.0), correction)
        )
        stored = jnp.concatenate([stored[1:], fresh_rates[None]], axis=0)
    return current[None]


def solution(mesh):
    return jax.shard_map(
        per_device,
        mesh=mesh,
        in_specs=(P("sec", None, "gx", "gy"), P("sec", None, None, "gx", "gy")),
        out_specs=P("sec", None, "gx", "gy"),
        check_vma=False,
    )
```

profile of v0, /device:TPU:0, one launch (start us, length us, event | category | flops | bytes accessed | tf_op | source)
XLA Modules:
  0.0 67.4 jit_solution(14832244294111676582)
XLA Ops:
  0.0 0.9 %bitcast_convert_fusion = bf16[5,32,256]{2,1,0:T(8,128)(2,1)S(1)} fusion(f32[1,5,32,256]{3,2,1,0:T(8,128)} %param.2), kind=kLoop, calls=%fused_computation.37 | loop fusion | flops 40960 | bytes 245760 | tf_op jit(solution)/shard_map/convert_element_type | solution.py:99
  0.9 2.5 %collective-permute-start.1 = (bf16[5,2,256]{2,1,0:T(2,128)(2,1)S(1)}, bf16[5,2,256]{2,1,0:T(2,128)(2,1)S(1)}, u32[]{:S(2)}, u32[]{:S(2)}) collective-permute-start(bf16[5,2,256]{2,1,0:T(2,128)(2,1)S(1)} %get-tuple-element.89), channel_id=1, source_target_pairs={{4,0},{8,4},{12,8},{0,12},{5,1},{9,5},{13,9},{1,13},{6,2},{10,6},{... | collective-permute-start | bytes 15368 | tf_op jit(solution)/shard_map/ppermute | solution.py:26
  3.4 1.3 %collective-permute-done.1 = bf16[5,2,256]{2,1,0:T(2,128)(2,1)S(1)} collective-permute-done((bf16[5,2,256]{2,1,0:T(2,128)(2,1)S(1)}, bf16[5,2,256]{2,1,0:T(2,128)(2,1)S(1)}, u32[]{:S(2)}, u32[]{:S(2)}) %collective-permute-start.1) | collective-permute-done | bytes 5152 | tf_op jit(solution)/shard_map/ppermute | solution.py:26
  4.7 1.7 %collective-permute-done = bf16[5,2,256]{2,1,0:T(2,128)(2,1)S(1)} collective-permute-done((bf16[5,2,256]{2,1,0:T(2,128)(2,1)S(1)}, bf16[5,2,256]{2,1,0:T(2,128)(2,1)S(1)}, u32[]{:S(2)}, u32[]{:S(2)}) %collective-permute-start) | collective-permute-done | bytes 5152 | tf_op jit(solution)/shard_map/ppermute | solution.py:23
  6.6 3.7 %collective-permute-start.3 = (bf16[5,36,64]{2,1,0:T(8,128)(2,1)S(1)}, bf16[5,36,64]{2,1,0:T(8,128)(2,1)S(1)}, u32[]{:S(2)}, u32[]{:S(2)}) collective-permute-start(bf16[5,36,64]{2,1,0:T(8,128)(2,1)S(1)} %get-tuple-element.83), channel_id=1, source_target_pairs={{1,0},{2,1},{3,2},{0,3},{5,4},{6,5},{7,6},{4,7},{9,8},{10,9},{11,1... | collective-permute-start | bytes 69128 | tf_op jit(solution)/shard_map/ppermute | solution.py:26
  10.2 1.8 %collective-permute-done.3 = bf16[5,36,64]{2,1,0:T(8,128)(2,1)S(1)} collective-permute-done((bf16[5,36,64]{2,1,0:T(8,128)(2,1)S(1)}, bf16[5,36,64]{2,1,0:T(8,128)(2,1)S(1)}, u32[]{:S(2)}, u32[]{:S(2)}) %collective-permute-start.3) | collective-permute-done | bytes 23072 | tf_op jit(solution)/shard_map/ppermute | solution.py:26
  12.0 4.1 %collective-permute-done.2 = bf16[5,36,64]{2,1,0:T(8,128)(2,1)S(1)} collective-permute-done((bf16[5,36,64]{2,1,0:T(8,128)(2,1)S(1)}, bf16[5,36,64]{2,1,0:T(8,128)(2,1)S(1)}, u32[]{:S(2)}, u32[]{:S(2)}) %collective-permute-start.2) | collective-permute-done | bytes 23072 | tf_op jit(solution)/shard_map/ppermute | solution.py:23
  16.1 0.1 maximum_convert_fusion
  17.6 0.1 fusion.384
  17.7 0.1 fusion.381
  19.0 0.1 fusion.192
  19.1 0.2 fusion.182
  19.3 0.2 fusion.172
  19.5 0.2 fusion.162
  19.7 0.3 fusion.148
  20.0 3.5 %collective-permute-start.4 = (bf16[5,32,256]{2,1,0:T(8,128)(2,1)S(1)}, bf16[5,32,256]{2,1,0:T(8,128)(2,1)S(1)}, u32[]{:S(2)}, u32[]{:S(2)}) collective-permute-start(bf16[5,32,256]{2,1,0:T(8,128)(2,1)S(1)} %convert_element_type.71), channel_id=1, source_target_pairs={{0,16},{1,17},{2,18},{3,19},{4,20},{5,21},{6,22},{7,23},{8,24},{9,... | collective-permute-start | bytes 245768 | tf_op jit(solution)/shard_map/ppermute | solution.py:34
  23.6 2.0 %collective-permute-done.4 = bf16[5,32,256]{2,1,0:T(8,128)(2,1)S(1)} collective-permute-done((bf16[5,32,256]{2,1,0:T(8,128)(2,1)S(1)}, bf16[5,32,256]{2,1,0:T(8,128)(2,1)S(1)}, u32[]{:S(2)}, u32[]{:S(2)}) %collective-permute-start.4) | collective-permute-done | bytes 81952 | tf_op jit(solution)/shard_map/ppermute | solution.py:34
  25.8 0.5 collective-permute-start.5
  26.3 0.8 %collective-permute-done.6 = bf16[5,2,256]{2,1,0:T(2,128)(2,1)S(1)} collective-permute-done((bf16[5,2,256]{2,1,0:T(2,128)(2,1)S(1)}, bf16[5,2,256]{2,1,0:T(2,128)(2,1)S(1)}, u32[]{:S(2)}, u32[]{:S(2)}) %collective-permute-start.6) | collective-permute-done | bytes 5152 | tf_op jit(solution)/shard_map/ppermute | solution.py:26
  27.1 1.8 %collective-permute-done.5 = bf16[5,2,256]{2,1,0:T(2,128)(2,1)S(1)} collective-permute-done((bf16[5,2,256]{2,1,0:T(2,128)(2,1)S(1)}, bf16[5,2,256]{2,1,0:T(2,128)(2,1)S(1)}, u32[]{:S(2)}, u32[]{:S(2)}) %collective-permute-start.5) | collective-permute-done | bytes 5152 | tf_op jit(solution)/shard_map/ppermute | solution.py:23
  29.1 2.0 %collective-permute-start.7 = (bf16[5,36,64]{2,1,0:T(8,128)(2,1)S(1)}, bf16[5,36,64]{2,1,0:T(8,128)(2,1)S(1)}, u32[]{:S(2)}, u32[]{:S(2)}) collective-permute-start(bf16[5,36,64]{2,1,0:T(8,128)(2,1)S(1)} %get-tuple-element.80), channel_id=1, source_target_pairs={{0,1},{1,2},{2,3},{3,0},{4,5},{5,6},{6,7},{7,4},{8,9},{9,10},{10,1... | collective-permute-start | bytes 69128 | tf_op jit(solution)/shard_map/ppermute | solution.py:23
  31.1 2.5 %collective-permute-done.8 = bf16[5,36,64]{2,1,0:T(8,128)(2,1)S(1)} collective-permute-done((bf16[5,36,64]{2,1,0:T(8,128)(2,1)S(1)}, bf16[5,36,64]{2,1,0:T(8,128)(2,1)S(1)}, u32[]{:S(2)}, u32[]{:S(2)}) %collective-permute-start.8) | collective-permute-done | bytes 23072 | tf_op jit(solution)/shard_map/ppermute | solution.py:26
  33.6 1.5 %collective-permute-done.7 = bf16[5,36,64]{2,1,0:T(8,128)(2,1)S(1)} collective-permute-done((bf16[5,36,64]{2,1,0:T(8,128)(2,1)S(1)}, bf16[5,36,64]{2,1,0:T(8,128)(2,1)S(1)}, u32[]{:S(2)}, u32[]{:S(2)}) %collective-permute-start.7) | collective-permute-done | bytes 23072 | tf_op jit(solution)/shard_map/ppermute | solution.py:23
  35.1 0.1 maximum_convert_fusion.1
  38.7 0.1 fusion.142
  38.8 0.2 fusion.132
  39.0 0.2 fusion.122
  39.2 0.2 fusion.112
  39.4 0.3 fusion.98
  39.7 4.3 %collective-permute-start.9 = (bf16[5,32,256]{2,1,0:T(8,128)(2,1)S(1)}, bf16[5,32,256]{2,1,0:T(8,128)(2,1)S(1)}, u32[]{:S(2)}, u32[]{:S(2)}) collective-permute-start(bf16[5,32,256]{2,1,0:T(8,128)(2,1)S(1)} %convert_element_type.75), channel_id=1, source_target_pairs={{0,16},{1,17},{2,18},{3,19},{4,20},{5,21},{6,22},{7,23},{8,24},{9,... | collective-permute-start | bytes 245768 | tf_op jit(solution)/shard_map/ppermute | solution.py:34
  44.0 2.0 %collective-permute-done.9 = bf16[5,32,256]{2,1,0:T(8,128)(2,1)S(1)} collective-permute-done((bf16[5,32,256]{2,1,0:T(8,128)(2,1)S(1)}, bf16[5,32,256]{2,1,0:T(8,128)(2,1)S(1)}, u32[]{:S(2)}, u32[]{:S(2)}) %collective-permute-start.9) | collective-permute-done | bytes 81952 | tf_op jit(solution)/shard_map/ppermute | solution.py:34
  46.1 0.1 fusion.269
  46.3 0.5 collective-permute-start.10
  46.8 0.8 %collective-permute-done.11 = bf16[5,2,256]{2,1,0:T(2,128)(2,1)S(1)} collective-permute-done((bf16[5,2,256]{2,1,0:T(2,128)(2,1)S(1)}, bf16[5,2,256]{2,1,0:T(2,128)(2,1)S(1)}, u32[]{:S(2)}, u32[]{:S(2)}) %collective-permute-start.11) | collective-permute-done | bytes 5152 | tf_op jit(solution)/shard_map/ppermute | solution.py:26
  47.6 1.8 %collective-permute-done.10 = bf16[5,2,256]{2,1,0:T(2,128)(2,1)S(1)} collective-permute-done((bf16[5,2,256]{2,1,0:T(2,128)(2,1)S(1)}, bf16[5,2,256]{2,1,0:T(2,128)(2,1)S(1)}, u32[]{:S(2)}, u32[]{:S(2)}) %collective-permute-start.10) | collective-permute-done | bytes 5152 | tf_op jit(solution)/shard_map/ppermute | solution.py:23
  49.5 0.3 collective-permute-start.13
  49.8 1.8 %collective-permute-start.12 = (bf16[5,36,64]{2,1,0:T(8,128)(2,1)S(1)}, bf16[5,36,64]{2,1,0:T(8,128)(2,1)S(1)}, u32[]{:S(2)}, u32[]{:S(2)}) collective-permute-start(bf16[5,36,64]{2,1,0:T(8,128)(2,1)S(1)} %get-tuple-element.78), channel_id=1, source_target_pairs={{0,1},{1,2},{2,3},{3,0},{4,5},{5,6},{6,7},{7,4},{8,9},{9,10},{10,1... | collective-permute-start | bytes 69128 | tf_op jit(solution)/shard_map/ppermute | solution.py:23
  51.6 2.6 %collective-permute-done.13 = bf16[5,36,64]{2,1,0:T(8,128)(2,1)S(1)} collective-permute-done((bf16[5,36,64]{2,1,0:T(8,128)(2,1)S(1)}, bf16[5,36,64]{2,1,0:T(8,128)(2,1)S(1)}, u32[]{:S(2)}, u32[]{:S(2)}) %collective-permute-start.13) | collective-permute-done | bytes 23072 | tf_op jit(solution)/shard_map/ppermute | solution.py:26
  54.1 1.5 %collective-permute-done.12 = bf16[5,36,64]{2,1,0:T(8,128)(2,1)S(1)} collective-permute-done((bf16[5,36,64]{2,1,0:T(8,128)(2,1)S(1)}, bf16[5,36,64]{2,1,0:T(8,128)(2,1)S(1)}, u32[]{:S(2)}, u32[]{:S(2)}) %collective-permute-start.12) | collective-permute-done | bytes 23072 | tf_op jit(solution)/shard_map/ppermute | solution.py:23
  55.7 0.1 maximum_convert_fusion.2
  59.3 0.1 fusion.92
  59.4 0.2 fusion.82
  59.6 0.2 fusion.72
  59.8 0.2 fusion.62
  60.0 0.3 fusion.48
  60.3 4.3 %collective-permute-start.14 = (bf16[5,32,256]{2,1,0:T(8,128)(2,1)S(1)}, bf16[5,32,256]{2,1,0:T(8,128)(2,1)S(1)}, u32[]{:S(2)}, u32[]{:S(2)}) collective-permute-start(bf16[5,32,256]{2,1,0:T(8,128)(2,1)S(1)} %convert_element_type.79), channel_id=1, source_target_pairs={{0,16},{1,17},{2,18},{3,19},{4,20},{5,21},{6,22},{7,23},{8,24},{9,... | collective-permute-start | bytes 245768 | tf_op jit(solution)/shard_map/ppermute | solution.py:34
  64.6 2.0 %collective-permute-done.14 = bf16[5,32,256]{2,1,0:T(8,128)(2,1)S(1)} collective-permute-done((bf16[5,32,256]{2,1,0:T(8,128)(2,1)S(1)}, bf16[5,32,256]{2,1,0:T(8,128)(2,1)S(1)}, u32[]{:S(2)}, u32[]{:S(2)}) %collective-permute-start.14) | collective-permute-done | bytes 81952 | tf_op jit(solution)/shard_map/ppermute | solution.py:34
  66.7 0.8 %fusion.14 = f32[1,5,32,256]{3,2,1,0:T(8,128)} fusion(f32[5,32,256]{2,1,0:T(8,128)S(1)} %get-tuple-element.12, f32[5,32,256]{2,1,0:T(8,128)S(1)} %fusion.48, bf16[5,32,256]{2,1,0:T(8,128)(2,1)S(1)} %collective-permute-done.14, pred[]{:T(512)S(6)} %eq.66, bf16[5,32,256]{2,1,0:T(8,128)(2,1)S(1)} %collective-permute-done.9, ...), kind=kLoop, calls=%fused_computation.27 | loop fusion | flops 778240 | bytes 819201 | tf_op jit(solution)/shard_map/broadcast_in_dim | solution.py:132
  (139 shorter events, 9.9 us)
Async XLA Ops:
  0.9 3.8 %collective-permute-start.1 = (bf16[5,2,256]{2,1,0:T(2,128)(2,1)S(1)}, bf16[5,2,256]{2,1,0:T(2,128)(2,1)S(1)}, u32[]{:S(2)}, u32[]{:S(2)}) collective-permute-start(bf16[5,2,256]{2,1,0:T(2,128)(2,1)S(1)} %get-tuple-element.89), channel_id=1, source_target_pairs={{4,0},{8,4},{12,8},{0,12},{5,1},{9,5},{13,9},{1,13},{6,2},{10,6},{... | collective-permute-start | bytes 15368 | tf_op jit(solution)/shard_map/ppermute | solution.py:26
  3.4 3.0 %collective-permute-start = (bf16[5,2,256]{2,1,0:T(2,128)(2,1)S(1)}, bf16[5,2,256]{2,1,0:T(2,128)(2,1)S(1)}, u32[]{:S(2)}, u32[]{:S(2)}) collective-permute-start(bf16[5,2,256]{2,1,0:T(2,128)(2,1)S(1)} %get-tuple-element.88), channel_id=1, source_target_pairs={{0,4},{4,8},{8,12},{12,0},{1,5},{5,9},{9,13},{13,1},{2,6},{6,10},{... | collective-permute-start | bytes 15368 | tf_op jit(solution)/shard_map/ppermute | solution.py:23
  6.6 5.4 %collective-permute-start.3 = (bf16[5,36,64]{2,1,0:T(8,128)(2,1)S(1)}, bf16[5,36,64]{2,1,0:T(8,128)(2,1)S(1)}, u32[]{:S(2)}, u32[]{:S(2)}) collective-permute-start(bf16[5,36,64]{2,1,0:T(8,128)(2,1)S(1)} %get-tuple-element.83), channel_id=1, source_target_pairs={{1,0},{2,1},{3,2},{0,3},{5,4},{6,5},{7,6},{4,7},{9,8},{10,9},{11,1... | collective-permute-start | bytes 69128 | tf_op jit(solution)/shard_map/ppermute | solution.py:26
  10.2 5.9 %collective-permute-start.2 = (bf16[5,36,64]{2,1,0:T(8,128)(2,1)S(1)}, bf16[5,36,64]{2,1,0:T(8,128)(2,1)S(1)}, u32[]{:S(2)}, u32[]{:S(2)}) collective-permute-start(bf16[5,36,64]{2,1,0:T(8,128)(2,1)S(1)} %get-tuple-element.82), channel_id=1, source_target_pairs={{0,1},{1,2},{2,3},{3,0},{4,5},{5,6},{6,7},{7,4},{8,9},{9,10},{10,1... | collective-permute-start | bytes 69128 | tf_op jit(solution)/shard_map/ppermute | solution.py:23
  19.7 5.9 %copy-start.1 = (f32[1,5,32,256]{3,2,1,0:T(8,128)S(1)}, f32[1,5,32,256]{3,2,1,0:T(8,128)}, u32[]{:S(2)}) copy-start(f32[1,5,32,256]{3,2,1,0:T(8,128)} %param.2) | copy-start | bytes 491524
  20.0 5.6 %copy-start = (bf16[1,3,5,32,256]{4,3,2,1,0:T(8,128)(2,1)S(1)}, bf16[1,3,5,32,256]{4,3,2,1,0:T(8,128)(2,1)}, u32[]{:S(2)}) copy-start(bf16[1,3,5,32,256]{4,3,2,1,0:T(8,128)(2,1)} %param.3) | copy-start | bytes 737284
  20.0 5.6 %collective-permute-start.4 = (bf16[5,32,256]{2,1,0:T(8,128)(2,1)S(1)}, bf16[5,32,256]{2,1,0:T(8,128)(2,1)S(1)}, u32[]{:S(2)}, u32[]{:S(2)}) collective-permute-start(bf16[5,32,256]{2,1,0:T(8,128)(2,1)S(1)} %convert_element_type.71), channel_id=1, source_target_pairs={{0,16},{1,17},{2,18},{3,19},{4,20},{5,21},{6,22},{7,23},{8,24},{9,... | collective-permute-start | bytes 245768 | tf_op jit(solution)/shard_map/ppermute | solution.py:34
  25.7 1.4 %collective-permute-start.6 = (bf16[5,2,256]{2,1,0:T(2,128)(2,1)S(1)}, bf16[5,2,256]{2,1,0:T(2,128)(2,1)S(1)}, u32[]{:S(2)}, u32[]{:S(2)}) collective-permute-start(bf16[5,2,256]{2,1,0:T(2,128)(2,1)S(1)} %get-tuple-element.87), channel_id=1, source_target_pairs={{4,0},{8,4},{12,8},{0,12},{5,1},{9,5},{13,9},{1,13},{6,2},{10,6},{... | collective-permute-start | bytes 15368 | tf_op jit(solution)/shard_map/ppermute | solution.py:26
  25.8 3.1 %collective-permute-start.5 = (bf16[5,2,256]{2,1,0:T(2,128)(2,1)S(1)}, bf16[5,2,256]{2,1,0:T(2,128)(2,1)S(1)}, u32[]{:S(2)}, u32[]{:S(2)}) collective-permute-start(bf16[5,2,256]{2,1,0:T(2,128)(2,1)S(1)} %get-tuple-element.86), channel_id=1, source_target_pairs={{0,4},{4,8},{8,12},{12,0},{1,5},{5,9},{9,13},{13,1},{2,6},{6,10},{... | collective-permute-start | bytes 15368 | tf_op jit(solution)/shard_map/ppermute | solution.py:23
  29.0 4.5 %collective-permute-start.8 = (bf16[5,36,64]{2,1,0:T(8,128)(2,1)S(1)}, bf16[5,36,64]{2,1,0:T(8,128)(2,1)S(1)}, u32[]{:S(2)}, u32[]{:S(2)}) collective-permute-start(bf16[5,36,64]{2,1,0:T(8,128)(2,1)S(1)} %get-tuple-element.81), channel_id=1, source_target_pairs={{1,0},{2,1},{3,2},{0,3},{5,4},{6,5},{7,6},{4,7},{9,8},{10,9},{11,1... | collective-permute-start | bytes 69128 | tf_op jit(solution)/shard_map/ppermute | solution.py:26
  29.1 6.0 %collective-permute-start.7 = (bf16[5,36,64]{2,1,0:T(8,128)(2,1)S(1)}, bf16[5,36,64]{2,1,0:T(8,128)(2,1)S(1)}, u32[]{:S(2)}, u32[]{:S(2)}) collective-permute-start(bf16[5,36,64]{2,1,0:T(8,128)(2,1)S(1)} %get-tuple-element.80), channel_id=1, source_target_pairs={{0,1},{1,2},{2,3},{3,0},{4,5},{5,6},{6,7},{7,4},{8,9},{9,10},{10,1... | collective-permute-start | bytes 69128 | tf_op jit(solution)/shard_map/ppermute | solution.py:23
  39.7 6.3 %collective-permute-start.9 = (bf16[5,32,256]{2,1,0:T(8,128)(2,1)S(1)}, bf16[5,32,256]{2,1,0:T(8,128)(2,1)S(1)}, u32[]{:S(2)}, u32[]{:S(2)}) collective-permute-start(bf16[5,32,256]{2,1,0:T(8,128)(2,1)S(1)} %convert_element_type.75), channel_id=1, source_target_pairs={{0,16},{1,17},{2,18},{3,19},{4,20},{5,21},{6,22},{7,23},{8,24},{9,... | collective-permute-start | bytes 245768 | tf_op jit(solution)/shard_map/ppermute | solution.py:34
  46.2 1.4 %collective-permute-start.11 = (bf16[5,2,256]{2,1,0:T(2,128)(2,1)S(1)}, bf16[5,2,256]{2,1,0:T(2,128)(2,1)S(1)}, u32[]{:S(2)}, u32[]{:S(2)}) collective-permute-start(bf16[5,2,256]{2,1,0:T(2,128)(2,1)S(1)} %get-tuple-element.85), channel_id=1, source_target_pairs={{4,0},{8,4},{12,8},{0,12},{5,1},{9,5},{13,9},{1,13},{6,2},{10,6},{... | collective-permute-start | bytes 15368 | tf_op jit(solution)/shard_map/ppermute | solution.py:26
  46.3 3.1 %collective-permute-start.10 = (bf16[5,2,256]{2,1,0:T(2,128)(2,1)S(1)}, bf16[5,2,256]{2,1,0:T(2,128)(2,1)S(1)}, u32[]{:S(2)}, u32[]{:S(2)}) collective-permute-start(bf16[5,2,256]{2,1,0:T(2,128)(2,1)S(1)} %get-tuple-element.84), channel_id=1, source_target_pairs={{0,4},{4,8},{8,12},{12,0},{1,5},{5,9},{9,13},{13,1},{2,6},{6,10},{... | collective-permute-start | bytes 15368 | tf_op jit(solution)/shard_map/ppermute | solution.py:23
  49.5 4.7 %collective-permute-start.13 = (bf16[5,36,64]{2,1,0:T(8,128)(2,1)S(1)}, bf16[5,36,64]{2,1,0:T(8,128)(2,1)S(1)}, u32[]{:S(2)}, u32[]{:S(2)}) collective-permute-start(bf16[5,36,64]{2,1,0:T(8,128)(2,1)S(1)} %get-tuple-element.79), channel_id=1, source_target_pairs={{1,0},{2,1},{3,2},{0,3},{5,4},{6,5},{7,6},{4,7},{9,8},{10,9},{11,1... | collective-permute-start | bytes 69128 | tf_op jit(solution)/shard_map/ppermute | solution.py:26
  49.8 5.9 %collective-permute-start.12 = (bf16[5,36,64]{2,1,0:T(8,128)(2,1)S(1)}, bf16[5,36,64]{2,1,0:T(8,128)(2,1)S(1)}, u32[]{:S(2)}, u32[]{:S(2)}) collective-permute-start(bf16[5,36,64]{2,1,0:T(8,128)(2,1)S(1)} %get-tuple-element.78), channel_id=1, source_target_pairs={{0,1},{1,2},{2,3},{3,0},{4,5},{5,6},{6,7},{7,4},{8,9},{9,10},{10,1... | collective-permute-start | bytes 69128 | tf_op jit(solution)/shard_map/ppermute | solution.py:23
  60.3 6.3 %collective-permute-start.14 = (bf16[5,32,256]{2,1,0:T(8,128)(2,1)S(1)}, bf16[5,32,256]{2,1,0:T(8,128)(2,1)S(1)}, u32[]{:S(2)}, u32[]{:S(2)}) collective-permute-start(bf16[5,32,256]{2,1,0:T(8,128)(2,1)S(1)} %convert_element_type.79), channel_id=1, source_target_pairs={{0,16},{1,17},{2,18},{3,19},{4,20},{5,21},{6,22},{7,23},{8,24},{9,... | collective-permute-start | bytes 245768 | tf_op jit(solution)/shard_map/ppermute | solution.py:34
where the time goes:
time: 67.6 us; the launch traced here: 67.4 us
  waiting for transfers between devices  28.3 us (42%)
  starting transfers between devices  23.5 us (35%)
  local copies, waits for them, and re-layouts  9.34 us (14%)
  other arithmetic  5.86 us (9%)
    ppermute x6, waiting for transfers between devices, with_halo(): lax.ppermute(lax.slice_in_dim(block, block.shape[dim] - width, None, axis...  12.4 us
    ppermute x3, starting transfers between devices, shifted(): return lax.ppermute(block, axis, route)  12.1 us
    ppermute x6, waiting for transfers between devices, with_halo(): lax.ppermute(lax.slice_in_dim(block, 0, width, axis=dim), axis, backward)  9.8 us
    ppermute x6, starting transfers between devices, with_halo(): lax.ppermute(lax.slice_in_dim(block, 0, width, axis=dim), axis, backward)  6.57 us
    ppermute x3, waiting for transfers between devices, shifted(): return lax.ppermute(block, axis, route)  6.1 us
    ppermute x6, starting transfers between devices, with_halo(): lax.ppermute(lax.slice_in_dim(block, block.shape[dim] - width, None, axis...  4.81 us
    slice x54, local copies, waits for them, and re-layouts, shift_z(): wrapped = jnp.roll(values, -step - depth, axis=-1)  4.58 us
    slice x54, local copies, waits for them, and re-layouts, shift_z(): unwrapped = jnp.roll(values, -step, axis=-1)  4.41 us
  transfers between devices with their start and end apart: 15, of which 15 were waited for; matrix products, arithmetic and copies ran while one was open for 0% of the time, Pallas kernels for 0%

commit v1 on v0

v1 whole, which is shorter than its diff:
```python
import functools

import jax
import jax.numpy as jnp
import numpy as np
from jax import lax
from jax.experimental import pallas as pl
from jax.experimental.pallas import tpu as pltpu
from jax.sharding import PartitionSpec as P

NZ = 32
TICKS = 3


TIME_STEP = 0.04
DYNAMIC_FRICTION = 0.4
CONDUCTIVITY = 0.5
GAMMA_LESS = 0.4
QUAD_WEIGHTS = (1.0 / 24.0, -5.0 / 24.0, 19.0 / 24.0, 9.0 / 24.0)

LANES = 128
EDGE = 8
FIELDS = 5


def neighbours(axis, even, low_edge, high_edge):
    count = lax.axis_size(axis)
    if count % 2:
        from_next = lax.ppermute(low_edge, axis, [(i, (i - 1) % count) for i in range(count)])
        from_last = lax.ppermute(high_edge, axis, [(i, (i + 1) % count) for i in range(count)])
        return from_next, from_last
    if low_edge is high_edge:
        outward = inward = low_edge
    else:
        outward = jnp.where(even, high_edge, low_edge)
        inward = jnp.where(even, low_edge, high_edge)
    far = [(i, (i + 1) % count if i % 2 else (i - 1) % count) for i in range(count)]
    near = [(i, i + 1 if i % 2 == 0 else i - 1) for i in range(count)]
    second = lax.ppermute(inward, axis, far)
    first = lax.ppermute(outward, axis, near)
    return first, second


def from_lower(block, levels, distance):
    count = lax.axis_size("sec")
    route = []
    for start in range(0, count, levels):
        route += [(start + i, start + (i + distance) % levels) for i in range(levels)]
    return lax.ppermute(block, "sec", route)


def stencil_matrix():
    per_tile = LANES // NZ
    out = 2 * LANES
    d_y = np.zeros((4 * LANES, out), np.float32)
    d_z = np.zeros((out, out), np.float32)
    sweep = np.zeros((4 * LANES, out), np.float32)
    for y in range(2 * per_tile):
        for z in range(NZ):
            column = y * NZ + z
            here = (y + per_tile) * NZ + z
            d_y[here + NZ, column] += 0.5
            d_y[here - NZ, column] -= 0.5
            d_z[y * NZ + (z + 1) % NZ, column] += 0.5
            d_z[y * NZ + (z - 1) % NZ, column] -= 0.5
            sweep[here, column] -= 1.0
            sweep[here + 2 * NZ, column] += 0.25
            sweep[here - 2 * NZ, column] += 0.25
            base = (y + per_tile) * NZ
            sweep[base + (z + 2) % NZ, column] += 0.25
            sweep[base + (z - 2) % NZ, column] += 0.25
    return np.concatenate([d_y, d_z, sweep], axis=0)


def advance_kernel(chain, corrected, rows, *refs):
    flags = refs[0]
    matrix = refs[1]
    refs = list(refs[2:])
    even_x = flags[0] == 1
    even_y = flags[1] == 1
    position = flags[2]
    inputs = []
    for link in range(chain):
        state = refs[:5]
        refs = refs[5:]
        extra = None
        if corrected[link]:
            extra = refs[:5]
            refs = refs[5:]
        inputs.append((state, extra))
    out, state_s, term_s, fresh_s, flow_x, slow, flow_y, flow_z, slow_yz = refs
    high = rows + 2 * EDGE

    def lanes(tile):
        return pl.ds(tile * LANES, LANES)

    for link in range(chain):
        (center, y_first, y_second, x_first, x_second), extra = inputs[link]
        for field in range(FIELDS):
            for tile in range(6):
                if tile in (2, 3):
                    middle = center[field, :, lanes(tile - 2)].astype(jnp.float32)
                else:
                    one = y_first[field, :, lanes(tile % 2)].astype(jnp.float32)
                    two = y_second[field, :, lanes(tile % 2)].astype(jnp.float32)
                    middle = jnp.where(even_y, two, one) if tile < 2 else jnp.where(even_y, one, two)
                one = x_first[field, :, lanes(tile)]
                two = x_second[field, :, lanes(tile)]
                state_s[link, field, tile, pl.ds(EDGE, rows), :] = middle
                state_s[link, field, tile, pl.ds(0, EDGE), :] = jnp.where(even_x, two, one)
                state_s[link, field, tile, pl.ds(EDGE + rows, EDGE), :] = jnp.where(even_x, one, two)
        if extra is not None:
            stored, y_first, y_second, x_first, x_second = extra
            for field in range(FIELDS):
                for tile in (2, 3):
                    old = [stored[age, field, :, lanes(tile - 2)].astype(jnp.float32) for age in range(3)]
                    terms = kept_terms(old)
                    for tick in range(TICKS):
                        term_s[link, tick, field, tile - 1, pl.ds(EDGE, rows), :] = terms[tick]
                for tick in range(2):
                    plane = tick * FIELDS + field
                    one = y_first[plane].astype(jnp.float32)
                    two = y_second[plane].astype(jnp.float32)
                    term_s[link, tick, field, 0, pl.ds(EDGE, rows), :] = jnp.where(even_y, two, one)
                    term_s[link, tick, field, 3, pl.ds(EDGE, rows), :] = jnp.where(even_y, one, two)
                    for tile in range(4):
                        one = x_first[plane, :, lanes(tile)]
                        two = x_second[plane, :, lanes(tile)]
                        term_s[link, tick, field, tile, pl.ds(0, EDGE), :] = jnp.where(even_x, two, one)
                        term_s[link, tick, field, tile, pl.ds(EDGE + rows, EDGE), :] = jnp.where(
                            even_x, one, two
                        )

    def pointwise(link, tile):
        density, mom_x, mom_y, mom_z, energy = [state_s[link, field, tile] for field in range(FIELDS)]
        inverse = 1.0 / density
        vel_x = mom_x * inverse
        vel_y = mom_y * inverse
        vel_z = mom_z * inverse
        kinetic = 0.5 * (vel_x * vel_x + vel_y * vel_y + vel_z * vel_z)
        pressure = GAMMA_LESS * (energy - density * kinetic)
        enthalpy = energy + pressure
        heat = DYNAMIC_FRICTION * kinetic + CONDUCTIVITY * (pressure * inverse)
        xy = mom_x * vel_y
        xz = mom_x * vel_z
        yz = mom_y * vel_z
        along_x = (mom_x, mom_x * vel_x + pressure, xy, xz, enthalpy * vel_x)
        along_y = (mom_y, xy, mom_y * vel_y + pressure, yz, enthalpy * vel_y)
        along_z = (mom_z, xz, yz, mom_z * vel_z + pressure, enthalpy * vel_z)
        spread = (
            DYNAMIC_FRICTION * vel_x,
            DYNAMIC_FRICTION * vel_y,
            DYNAMIC_FRICTION * vel_z,
            heat,
        )
        for field in range(FIELDS):
            flow_y[pl.ds(field * high, high), lanes(tile)] = (-along_y[field]).astype(jnp.bfloat16)
            if 1 <= tile <= 4:
                flow_z[pl.ds(field * high, high), lanes(tile - 1)] = (-along_z[field]).astype(jnp.bfloat16)
                flow_x[field, tile - 1, pl.ds(EDGE, high), :] = along_x[field]
            if field:
                slow_yz[pl.ds(field * high, high), lanes(tile)] = spread[field - 1].astype(jnp.bfloat16)
                if 1 <= tile <= 4:
                    slow[field - 1, tile - 1, pl.ds(EDGE, high), :] = spread[field - 1]

    slow_yz[pl.ds(0, high), :] = jnp.zeros((high, 6 * LANES), jnp.bfloat16)

    def rates(link, tick):
        for tile in range(6) if tick == 0 else range(1, 5):
            pointwise(link, tile)
        groups = ((1, 2), (3, 4)) if tick < TICKS - 1 else ((2, 3),)
        found = [{} for _ in range(FIELDS)]
        for group in groups:
            around = pl.ds((group[0] - 1) * LANES, 4 * LANES)
            inner = pl.ds((group[0] - 1) * LANES, 2 * LANES)
            left = jnp.concatenate([flow_y[:, around], flow_z[:, inner], slow_yz[:, around]], axis=1)
            product = jnp.dot(left, matrix[...], preferred_element_type=jnp.float32)
            for field in range(FIELDS):
                for place, tile in enumerate(group):
                    total = product[field * high : (field + 1) * high, place * LANES : (place + 1) * LANES]

                    def shifted(ref, index, step):
                        return ref[index, tile - 1, pl.ds(EDGE + step, high), :]

                    total = total - 0.5 * (shifted(flow_x, field, 1) - shifted(flow_x, field, -1))
                    if field:
                        total = total + (
                            0.25 * (shifted(slow, field - 1, 2) + shifted(slow, field - 1, -2))
                            - 0.5 * shifted(slow, field - 1, 0)
                        )
                    found[field][tile] = total
        return found

    for tick in range(TICKS):
        for link in reversed(range(chain)):
            if link > TICKS - tick:
                continue
            found = rates(link, tick)
            last = tick == TICKS - 1
            for field in range(FIELDS):
                for tile, rate in found[field].items():
                    if link:
                        fresh_s[link - 1, tick, field, tile - 1] = rate.astype(jnp.bfloat16).astype(jnp.float32)
                    if link + tick >= TICKS:
                        continue
                    step = rate
                    if corrected[link]:
                        extra = term_s[link, tick, field, tile - 1] + QUAD_WEIGHTS[3] * fresh_s[
                            link, tick, field, tile - 1
                        ]
                        for age in range(tick):
                            weight = QUAD_WEIGHTS[3 - tick + age] - (1.0 if age == tick - 1 else 0.0)
                            extra = extra + weight * fresh_s[link, age, field, tile - 1]
                        step = rate + jnp.where(position > link, extra, 0.0)
                    state = state_s[link, field, tile] + TIME_STEP * step
                    if last:
                        out[field, :, lanes(tile - 2)] = state[EDGE : EDGE + rows]
                    else:
                        state_s[link, field, tile] = state


def kept_terms(old):
    first, second, third, _ = QUAD_WEIGHTS
    return (
        first * old[0] + second * old[1] + (third - 1.0) * old[2],
        first * old[1] + second * old[2],
        first * old[2],
    )


def per_device(fields, stored_rates):
    levels = min(4, lax.axis_size("sec"))
    position = lax.axis_index("sec") % levels
    even_x = lax.axis_index("gx") % 2 == 0 if lax.axis_size("gx") % 2 == 0 else jnp.bool_(True)
    even_y = lax.axis_index("gy") % 2 == 0 if lax.axis_size("gy") % 2 == 0 else jnp.bool_(True)
    block = fields[0]
    stored = stored_rates[0]
    rows, columns = block.shape[1:]
    chain = min(levels, TICKS + 1)
    corrected = [link < levels - 1 and link < TICKS for link in range(chain)]
    sent = block.astype(jnp.bfloat16)

    def ordered_y(pair):
        first, second = pair
        return jnp.where(even_y, second, first), jnp.where(even_y, first, second)

    def edges_x(padded):
        return padded[:, :EDGE], padded[:, -EDGE:]

    own_y = neighbours("gy", even_y, sent, sent)
    centers = [sent] + [from_lower(sent, levels, link) for link in range(1, chain)]
    old = stored.astype(jnp.float32)
    kept = jnp.concatenate(kept_terms(old)[:2], axis=0).astype(jnp.bfloat16)
    kept_y = neighbours("gy", even_y, kept[:, :, :LANES], kept[:, :, -LANES:])
    low, top = ordered_y(own_y)
    padded = jnp.concatenate([low, sent, top], axis=2)
    own_x = neighbours("gx", even_x, *edges_x(padded))
    both = jnp.concatenate(own_y, axis=0)
    low, top = ordered_y(kept_y)
    kept_padded = jnp.concatenate([low, kept, top], axis=2)

    states = [(block, *own_y, *own_x)]
    extras = [None] * chain
    late = []
    for link in range(chain):
        if link:
            arrived = from_lower(both, levels, link)
            link_y = (arrived[:FIELDS], arrived[FIELDS:])
            low, top = ordered_y(link_y)
            late.append(jnp.concatenate([low, centers[link], top], axis=2))
            states.append((centers[link], *link_y))
        if corrected[link]:
            if link:
                link_stored = from_lower(stored, levels, link)
                link_y = tuple(from_lower(half, levels, link) for half in kept_y)
                link_padded = from_lower(kept_padded, levels, link)
            else:
                link_stored, link_y, link_padded = stored, kept_y, kept_padded
            extras[link] = (link_stored, *link_y)
            late += [link_padded[:FIELDS], link_padded[FIELDS:]]
    late_x = neighbours("gx", even_x, *edges_x(jnp.concatenate(late, axis=2)))

    operands = []
    start = 0
    for link in range(chain):
        if link:
            width = columns + 4 * LANES
            operands += [*states[link], *(half[:, :, start : start + width] for half in late_x)]
            start += width
        else:
            operands += states[0]
        if corrected[link]:
            width = columns + 2 * LANES
            operands += extras[link]
            operands += [
                jnp.concatenate(
                    [half[:, :, start : start + width], half[:, :, start + width : start + 2 * width]], axis=0
                )
                for half in late_x
            ]
            start += 2 * width
    operands = [
        part.astype(jnp.float32) if part.ndim == 3 and part.shape[1] == EDGE else part for part in operands
    ]
    flags = jnp.stack([even_x.astype(jnp.int32), even_y.astype(jnp.int32), position])
    matrix = jnp.asarray(stencil_matrix(), jnp.bfloat16)
    high = rows + 2 * EDGE
    tall = high + 2 * EDGE
    vmem = pl.BlockSpec(memory_space=pltpu.VMEM)
    result = pl.pallas_call(
        functools.partial(advance_kernel, chain, corrected, rows),
        out_shape=jax.ShapeDtypeStruct((FIELDS, rows, columns), jnp.float32),
        in_specs=[pl.BlockSpec(memory_space=pltpu.SMEM)] + [vmem] * (len(operands) + 1),
        out_specs=vmem,
        scratch_shapes=[
            pltpu.VMEM((chain, FIELDS, 6, high, LANES), jnp.float32),
            pltpu.VMEM((chain, TICKS, FIELDS, 4, high, LANES), jnp.float32),
            pltpu.VMEM((chain, TICKS, FIELDS, 4, high, LANES), jnp.float32),
            pltpu.VMEM((FIELDS, 4, tall, LANES), jnp.float32),
            pltpu.VMEM((FIELDS - 1, 4, tall, LANES), jnp.float32),
            pltpu.VMEM((FIELDS * high, 6 * LANES), jnp.bfloat16),
            pltpu.VMEM((FIELDS * high, 4 * LANES), jnp.bfloat16),
            pltpu.VMEM((FIELDS * high, 6 * LANES), jnp.bfloat16),
        ],
        compiler_params=pltpu.CompilerParams(vmem_limit_bytes=48 * 1024 * 1024),
    )(flags, matrix, *operands)
    return result[None]


def solution(mesh):
    return jax.shard_map(
        per_device,
        mesh=mesh,
        in_specs=(P("sec", None, "gx", "gy"), P("sec", None, None, "gx", "gy")),
        out_specs=P("sec", None, "gx", "gy"),
        check_vma=False,
    )
```

time: 67.6 us -> 35.5 us (0.53)
  waiting for transfers between devices: 28.3 us -> 14.7 us
  starting transfers between devices: 23.5 us -> 12.4 us
  local copies, waits for them, and re-layouts: 9.34 us -> 0.95 us
  Pallas kernels: 0 us -> 5.64 us
  other arithmetic: 5.86 us -> 1.44 us
    ppermute x15 -> x10, waiting for transfers between devices: 28.3 us -> 14.7 us  [the longest x4 8.81 us: neighbours(): second = lax.ppermute(inward, axis, far)]
    ppermute x15 -> x10, starting transfers between devices: 23.5 us -> 12.4 us  [the longest x4 5.69 us: neighbours(): first = lax.ppermute(outward, axis, near)]
    slice x114 -> x2, local copies, waits for them, and re-layouts: 9.28 us -> 0.01 us  [per_device(): half[:, :, start:start + width]]
    pallas_call x0 -> x1, Pallas kernels: none -> 5.64 us  [per_device(): pl.pallas_call(functools.partial(advance_kernel, chain, corrected, rows),...]
    unnamed x12 -> x0, other arithmetic: 2.13 us -> none
    unnamed x4 -> x9, local copies, waits for them, and re-layouts: 0.01 us -> 0.94 us
    another operation x3 -> x1, other arithmetic: 0.86 us -> 0.08 us  [per_device(): jnp.stack([even_x.astype(jnp.int32), even_y.astype(jnp.int32), position])]
    broadcast_in_dim x1 -> x0, other arithmetic: 0.78 us -> none  [per_device(): return current[None]]
  transfers between devices with their start and end apart: 15 -> 10, of which waited for: 15 -> 7; matrix products, arithmetic and copies ran while one was open for 0% -> 1% of each run, Pallas kernels for 0% -> 0%
where the time goes in v1:
time: 35.5 us; the launch traced here: 35.3 us
  waiting for transfers between devices  14.7 us (41%)
  starting transfers between devices  12.4 us (35%)
  Pallas kernels  5.64 us (16%)
  other arithmetic  1.44 us (4%)
  local copies, waits for them, and re-layouts  0.95 us (3%)
    ppermute x4, waiting for transfers between devices, neighbours(): second = lax.ppermute(inward, axis, far)  8.81 us
    ppermute x4, starting transfers between devices, neighbours(): first = lax.ppermute(outward, axis, near)  5.69 us
    pallas_call x1, Pallas kernels, per_device(): pl.pallas_call(functools.partial(advance_kernel, chain, corrected, rows),...  5.64 us
    ppermute x2, waiting for transfers between devices, from_lower(): return lax.ppermute(block, 'sec', route)  3.78 us
    ppermute x4, starting transfers between devices, neighbours(): second = lax.ppermute(inward, axis, far)  3.64 us
    ppermute x2, starting transfers between devices, from_lower(): return lax.ppermute(block, 'sec', route)  3.05 us
    ppermute x4, waiting for transfers between devices, neighbours(): first = lax.ppermute(outward, axis, near)  2.11 us
    convert_element_type x1, other arithmetic, per_device(): old = stored.astype(jnp.float32)  0.98 us
  transfers between devices with their start and end apart: 10, of which 7 were waited for; matrix products, arithmetic and copies ran while one was open for 1% of the time, Pallas kernels for 0%

profile of v1, /device:TPU:0, one launch (start us, length us, event | category | flops | bytes accessed | tf_op | source)
XLA Modules:
  0.0 35.3 jit_solution(6923073140472926817)
XLA Ops:
  0.0 1.0 %bitcast_convert_fusion = f32[3,5,32,256]{3,2,1,0:T(8,128)S(1)} fusion(bf16[1,3,5,32,256]{4,3,2,1,0:T(8,128)(2,1)} %param.4), kind=kLoop, calls=%fused_computation.37 | loop fusion | flops 122880 | bytes 737280 | tf_op jit(solution)/shard_map/convert_element_type | solution.py:252
  1.0 0.1 fusion.5
  1.0 0.0 copy-start.1
  1.1 3.1 %collective-permute-start.4 = (bf16[10,32,128]{2,1,0:T(8,128)(2,1)S(1)}, bf16[10,32,128]{2,1,0:T(8,128)(2,1)S(1)}, u32[]{:S(2)}, u32[]{:S(2)}) collective-permute-start(bf16[10,32,128]{2,1,0:T(8,128)(2,1)S(1)} %get-tuple-element.18), channel_id=1, source_target_pairs={{0,1},{1,0},{2,3},{3,2},{4,5},{5,4},{6,7},{7,6},{8,9},{9,8},{10,11... | collective-permute-start | bytes 245768 | tf_op jit(solution)/shard_map/ppermute | solution.py:40
  4.2 2.5 %collective-permute-start.5 = (bf16[10,32,128]{2,1,0:T(8,128)(2,1)S(1)}, bf16[10,32,128]{2,1,0:T(8,128)(2,1)S(1)}, u32[]{:S(2)}, u32[]{:S(2)}) collective-permute-start(bf16[10,32,128]{2,1,0:T(8,128)(2,1)S(1)} %get-tuple-element.17), channel_id=1, source_target_pairs={{0,3},{1,2},{2,1},{3,0},{4,7},{5,6},{6,5},{7,4},{8,11},{9,10},{10,... | collective-permute-start | bytes 245768 | tf_op jit(solution)/shard_map/ppermute | solution.py:39
  6.7 0.0 copy-done.1
  6.7 0.7 %collective-permute-start = (bf16[5,32,256]{2,1,0:T(8,128)(2,1)S(1)}, bf16[5,32,256]{2,1,0:T(8,128)(2,1)S(1)}, u32[]{:S(2)}, u32[]{:S(2)}) collective-permute-start(bf16[5,32,256]{2,1,0:T(8,128)(2,1)S(1)} %bitcast_convert_fusion.1), channel_id=1, source_target_pairs={{0,1},{1,0},{2,3},{3,2},{4,5},{5,4},{6,7},{7,6},{8,9},{9,8},{10,11... | collective-permute-start | bytes 245768 | tf_op jit(solution)/shard_map/ppermute | solution.py:40
  7.4 0.9 %collective-permute-start.1 = (bf16[5,32,256]{2,1,0:T(8,128)(2,1)S(1)}, bf16[5,32,256]{2,1,0:T(8,128)(2,1)S(1)}, u32[]{:S(2)}, u32[]{:S(2)}) collective-permute-start(bf16[5,32,256]{2,1,0:T(8,128)(2,1)S(1)} %bitcast_convert_fusion.1), channel_id=1, source_target_pairs={{0,3},{1,2},{2,1},{3,0},{4,7},{5,6},{6,5},{7,4},{8,11},{9,10},{10,... | collective-permute-start | bytes 245768 | tf_op jit(solution)/shard_map/ppermute | solution.py:39
  8.3 1.5 %collective-permute-start.7 = (bf16[5,32,256]{2,1,0:T(8,128)(2,1)S(1)}, bf16[5,32,256]{2,1,0:T(8,128)(2,1)S(1)}, u32[]{:S(2)}, u32[]{:S(2)}) collective-permute-start(bf16[5,32,256]{2,1,0:T(8,128)(2,1)S(1)} %bitcast_convert_fusion.1), channel_id=1, source_target_pairs={{0,16},{16,0},{1,17},{17,1},{2,18},{18,2},{3,19},{19,3},{4,20},{20... | collective-permute-start | bytes 245768 | tf_op jit(solution)/shard_map/ppermute | solution.py:49
  9.8 0.0 collective-permute-done.4.refs_8_
  9.8 2.0 %collective-permute-done.5.refs_9_ = bf16[10,32,128]{2,1,0:T(8,128)(2,1)S(1)} collective-permute-done((bf16[10,32,128]{2,1,0:T(8,128)(2,1)S(1)}, bf16[10,32,128]{2,1,0:T(8,128)(2,1)S(1)}, u32[]{:S(2)}, u32[]{:S(2)}) %collective-permute-start.5) | collective-permute-done | bytes 81952 | tf_op jit(solution)/shard_map/ppermute | solution.py:39
  11.9 0.3 collective-permute-done.refs_3_
  12.2 2.1 %collective-permute-done.1.refs_4_ = bf16[5,32,256]{2,1,0:T(8,128)(2,1)S(1)} collective-permute-done((bf16[5,32,256]{2,1,0:T(8,128)(2,1)S(1)}, bf16[5,32,256]{2,1,0:T(8,128)(2,1)S(1)}, u32[]{:S(2)}, u32[]{:S(2)}) %collective-permute-start.1) | collective-permute-done | bytes 81952 | tf_op jit(solution)/shard_map/ppermute | solution.py:39
  14.4 1.6 %collective-permute-start.6 = (bf16[10,32,256]{2,1,0:T(8,128)(2,1)S(1)}, bf16[10,32,256]{2,1,0:T(8,128)(2,1)S(1)}, u32[]{:S(2)}, u32[]{:S(2)}) collective-permute-start(bf16[10,32,256]{2,1,0:T(8,128)(2,1)S(1)} %pad_maximum_fusion.1), channel_id=1, source_target_pairs={{0,16},{16,0},{1,17},{17,1},{2,18},{18,2},{3,19},{19,3},{4,20},{20... | collective-permute-start | bytes 491528 | tf_op jit(solution)/shard_map/ppermute | solution.py:49
  16.0 3.8 %collective-permute-done.6 = bf16[10,32,256]{2,1,0:T(8,128)(2,1)S(1)} collective-permute-done((bf16[10,32,256]{2,1,0:T(8,128)(2,1)S(1)}, bf16[10,32,256]{2,1,0:T(8,128)(2,1)S(1)}, u32[]{:S(2)}, u32[]{:S(2)}) %collective-permute-start.6) | collective-permute-done | bytes 163872 | tf_op jit(solution)/shard_map/ppermute | solution.py:49
  19.8 0.0 collective-permute-done.7.refs_12_
  19.9 0.1 collective-permute-start.9
  20.0 1.7 %collective-permute-start.2 = (bf16[5,8,768]{2,1,0:T(8,128)(2,1)S(1)}, bf16[5,8,768]{2,1,0:T(8,128)(2,1)S(1)}, u32[]{:S(2)}, u32[]{:S(2)}) collective-permute-start(bf16[5,8,768]{2,1,0:T(8,128)(2,1)S(1)} %broadcast_select_fusion.9), channel_id=1, source_target_pairs={{0,4},{4,0},{8,12},{12,8},{1,5},{5,1},{9,13},{13,9},{2,6},{6,2},{1... | collective-permute-start | bytes 184328 | tf_op jit(solution)/shard_map/ppermute | solution.py:40
  21.7 0.2 collective-permute-start.3
  21.8 0.1 pad_add_fusion.refs_0_
  21.9 0.6 %collective-permute-done.2 = bf16[5,8,768]{2,1,0:T(8,128)(2,1)S(1)} collective-permute-done((bf16[5,8,768]{2,1,0:T(8,128)(2,1)S(1)}, bf16[5,8,768]{2,1,0:T(8,128)(2,1)S(1)}, u32[]{:S(2)}, u32[]{:S(2)}) %collective-permute-start.2) | collective-permute-done | bytes 61472 | tf_op jit(solution)/shard_map/ppermute | solution.py:40
  22.6 0.0 copy-start.2
  22.6 4.7 %collective-permute-done.3 = bf16[5,8,768]{2,1,0:T(8,128)(2,1)S(1)} collective-permute-done((bf16[5,8,768]{2,1,0:T(8,128)(2,1)S(1)}, bf16[5,8,768]{2,1,0:T(8,128)(2,1)S(1)}, u32[]{:S(2)}, u32[]{:S(2)}) %collective-permute-start.3) | collective-permute-done | bytes 61472 | tf_op jit(solution)/shard_map/ppermute | solution.py:39
  27.3 0.2 collective-permute-start.8
  27.4 0.0 collective-permute-done.9
  27.5 1.2 %collective-permute-done.8 = bf16[5,8,1792]{2,1,0:T(8,128)(2,1)S(1)} collective-permute-done((bf16[5,8,1792]{2,1,0:T(8,128)(2,1)S(1)}, bf16[5,8,1792]{2,1,0:T(8,128)(2,1)S(1)}, u32[]{:S(2)}, u32[]{:S(2)}) %collective-permute-start.8) | collective-permute-done | bytes 143392 | tf_op jit(solution)/shard_map/ppermute | solution.py:40
  28.7 0.0 copy-start
  28.8 0.0 copy-done.2
  28.8 0.9 %copy-done = bf16[1,3,5,32,256]{4,3,2,1,0:T(8,128)(2,1)S(1)} copy-done((bf16[1,3,5,32,256]{4,3,2,1,0:T(8,128)(2,1)S(1)}, bf16[1,3,5,32,256]{4,3,2,1,0:T(8,128)(2,1)}, u32[]{:S(2)}) %copy-start) | copy-done | bytes 245784
  29.7 5.6 %shard_map.37 = f32[5,32,256]{2,1,0:T(8,128)} custom-call(s32[3]{0:T(128)S(1)} %pad_add_fusion.refs_0_, bf16[1280,256]{1,0:T(8,128)(2,1)S(1)} %copy-done.2, f32[5,32,256]{2,1,0:T(8,128)S(1)} %bitcast.13, bf16[5,32,256]{2,1,0:T(8,128)(2,1)S(1)} %collective-permute-done.refs_3_, bf16[5,32,256]{2,1,0:T(8,128)(2,1)S(1)} %collective-permute-done.1.refs_4_, ...), custom_call_target="tpu_custom_call" | custom-call | tf_op jit(solution)/shard_map/pallas_call | solution.py:310
  (22 shorter events, 0.4 us)
Async XLA Ops:
  1.0 5.6 %copy-start.1 = (f32[1,5,32,256]{3,2,1,0:T(8,128)S(1)}, f32[1,5,32,256]{3,2,1,0:T(8,128)}, u32[]{:S(2)}) copy-start(f32[1,5,32,256]{3,2,1,0:T(8,128)} %param.3) | copy-start | bytes 491524
  1.1 8.7 %collective-permute-start.4 = (bf16[10,32,128]{2,1,0:T(8,128)(2,1)S(1)}, bf16[10,32,128]{2,1,0:T(8,128)(2,1)S(1)}, u32[]{:S(2)}, u32[]{:S(2)}) collective-permute-start(bf16[10,32,128]{2,1,0:T(8,128)(2,1)S(1)} %get-tuple-element.18), channel_id=1, source_target_pairs={{0,1},{1,0},{2,3},{3,2},{4,5},{5,4},{6,7},{7,6},{8,9},{9,8},{10,11... | collective-permute-start | bytes 245768 | tf_op jit(solution)/shard_map/ppermute | solution.py:40
  4.2 7.6 %collective-permute-start.5 = (bf16[10,32,128]{2,1,0:T(8,128)(2,1)S(1)}, bf16[10,32,128]{2,1,0:T(8,128)(2,1)S(1)}, u32[]{:S(2)}, u32[]{:S(2)}) collective-permute-start(bf16[10,32,128]{2,1,0:T(8,128)(2,1)S(1)} %get-tuple-element.17), channel_id=1, source_target_pairs={{0,3},{1,2},{2,1},{3,0},{4,7},{5,6},{6,5},{7,4},{8,11},{9,10},{10,... | collective-permute-start | bytes 245768 | tf_op jit(solution)/shard_map/ppermute | solution.py:39
  6.7 5.5 %collective-permute-start = (bf16[5,32,256]{2,1,0:T(8,128)(2,1)S(1)}, bf16[5,32,256]{2,1,0:T(8,128)(2,1)S(1)}, u32[]{:S(2)}, u32[]{:S(2)}) collective-permute-start(bf16[5,32,256]{2,1,0:T(8,128)(2,1)S(1)} %bitcast_convert_fusion.1), channel_id=1, source_target_pairs={{0,1},{1,0},{2,3},{3,2},{4,5},{5,4},{6,7},{7,6},{8,9},{9,8},{10,11... | collective-permute-start | bytes 245768 | tf_op jit(solution)/shard_map/ppermute | solution.py:40
  7.4 6.9 %collective-permute-start.1 = (bf16[5,32,256]{2,1,0:T(8,128)(2,1)S(1)}, bf16[5,32,256]{2,1,0:T(8,128)(2,1)S(1)}, u32[]{:S(2)}, u32[]{:S(2)}) collective-permute-start(bf16[5,32,256]{2,1,0:T(8,128)(2,1)S(1)} %bitcast_convert_fusion.1), channel_id=1, source_target_pairs={{0,3},{1,2},{2,1},{3,0},{4,7},{5,6},{6,5},{7,4},{8,11},{9,10},{10,... | collective-permute-start | bytes 245768 | tf_op jit(solution)/shard_map/ppermute | solution.py:39
  8.3 11.5 %collective-permute-start.7 = (bf16[5,32,256]{2,1,0:T(8,128)(2,1)S(1)}, bf16[5,32,256]{2,1,0:T(8,128)(2,1)S(1)}, u32[]{:S(2)}, u32[]{:S(2)}) collective-permute-start(bf16[5,32,256]{2,1,0:T(8,128)(2,1)S(1)} %bitcast_convert_fusion.1), channel_id=1, source_target_pairs={{0,16},{16,0},{1,17},{17,1},{2,18},{18,2},{3,19},{19,3},{4,20},{20... | collective-permute-start | bytes 245768 | tf_op jit(solution)/shard_map/ppermute | solution.py:49
  14.4 5.4 %collective-permute-start.6 = (bf16[10,32,256]{2,1,0:T(8,128)(2,1)S(1)}, bf16[10,32,256]{2,1,0:T(8,128)(2,1)S(1)}, u32[]{:S(2)}, u32[]{:S(2)}) collective-permute-start(bf16[10,32,256]{2,1,0:T(8,128)(2,1)S(1)} %pad_maximum_fusion.1), channel_id=1, source_target_pairs={{0,16},{16,0},{1,17},{17,1},{2,18},{18,2},{3,19},{19,3},{4,20},{20... | collective-permute-start | bytes 491528 | tf_op jit(solution)/shard_map/ppermute | solution.py:49
  19.9 7.6 %collective-permute-start.9 = (bf16[5,8,1792]{2,1,0:T(8,128)(2,1)S(1)}, bf16[5,8,1792]{2,1,0:T(8,128)(2,1)S(1)}, u32[]{:S(2)}, u32[]{:S(2)}) collective-permute-start(bf16[5,8,1792]{2,1,0:T(8,128)(2,1)S(1)} %get-tuple-element.8), channel_id=1, source_target_pairs={{0,12},{4,8},{8,4},{12,0},{1,13},{5,9},{9,5},{13,1},{2,14},{6,10},... | collective-permute-start | bytes 430088 | tf_op jit(solution)/shard_map/ppermute | solution.py:39
  20.0 2.6 %collective-permute-start.2 = (bf16[5,8,768]{2,1,0:T(8,128)(2,1)S(1)}, bf16[5,8,768]{2,1,0:T(8,128)(2,1)S(1)}, u32[]{:S(2)}, u32[]{:S(2)}) collective-permute-start(bf16[5,8,768]{2,1,0:T(8,128)(2,1)S(1)} %broadcast_select_fusion.9), channel_id=1, source_target_pairs={{0,4},{4,0},{8,12},{12,8},{1,5},{5,1},{9,13},{13,9},{2,6},{6,2},{1... | collective-permute-start | bytes 184328 | tf_op jit(solution)/shard_map/ppermute | solution.py:40
  21.7 5.6 %collective-permute-start.3 = (bf16[5,8,768]{2,1,0:T(8,128)(2,1)S(1)}, bf16[5,8,768]{2,1,0:T(8,128)(2,1)S(1)}, u32[]{:S(2)}, u32[]{:S(2)}) collective-permute-start(bf16[5,8,768]{2,1,0:T(8,128)(2,1)S(1)} %get-tuple-element.5), channel_id=1, source_target_pairs={{0,12},{4,8},{8,4},{12,0},{1,13},{5,9},{9,5},{13,1},{2,14},{6,10},... | collective-permute-start | bytes 184328 | tf_op jit(solution)/shard_map/ppermute | solution.py:39
  22.6 6.2 %copy-start.2 = (bf16[1280,256]{1,0:T(8,128)(2,1)S(1)}, bf16[1280,256]{1,0:T(8,128)(2,1)}, u32[]{:S(2)}) copy-start(bf16[1280,256]{1,0:T(8,128)(2,1)} %constant.41.clone.refs_1_) | copy-start | bytes 1966084
  27.3 1.4 %collective-permute-start.8 = (bf16[5,8,1792]{2,1,0:T(8,128)(2,1)S(1)}, bf16[5,8,1792]{2,1,0:T(8,128)(2,1)S(1)}, u32[]{:S(2)}, u32[]{:S(2)}) collective-permute-start(bf16[5,8,1792]{2,1,0:T(8,128)(2,1)S(1)} %get-tuple-element.9), channel_id=1, source_target_pairs={{0,4},{4,0},{8,12},{12,8},{1,5},{5,1},{9,13},{13,9},{2,6},{6,2},{1... | collective-permute-start | bytes 430088 | tf_op jit(solution)/shard_map/ppermute | solution.py:40
  28.7 0.9 %copy-start = (bf16[1,3,5,32,256]{4,3,2,1,0:T(8,128)(2,1)S(1)}, bf16[1,3,5,32,256]{4,3,2,1,0:T(8,128)(2,1)}, u32[]{:S(2)}) copy-start(bf16[1,3,5,32,256]{4,3,2,1,0:T(8,128)(2,1)} %param.4) | copy-start | bytes 737284

commit v2 on v1

v2 whole, which is shorter than its diff:
```python
import functools

import jax
import jax.numpy as jnp
import numpy as np
from jax import lax
from jax.experimental import pallas as pl
from jax.experimental.pallas import tpu as pltpu
from jax.sharding import PartitionSpec as P

NZ = 32
TICKS = 3


TIME_STEP = 0.04
DYNAMIC_FRICTION = 0.4
CONDUCTIVITY = 0.5
GAMMA_LESS = 0.4
QUAD_WEIGHTS = (1.0 / 24.0, -5.0 / 24.0, 19.0 / 24.0, 9.0 / 24.0)

LANES = 128
EDGE = 8
FIELDS = 5


def neighbours(axis, even, low_edge, high_edge):
    count = lax.axis_size(axis)
    if count % 2:
        from_next = lax.ppermute(low_edge, axis, [(i, (i - 1) % count) for i in range(count)])
        from_last = lax.ppermute(high_edge, axis, [(i, (i + 1) % count) for i in range(count)])
        return from_next, from_last
    if low_edge is high_edge:
        outward = inward = low_edge
    else:
        outward = jnp.where(even, high_edge, low_edge)
        inward = jnp.where(even, low_edge, high_edge)
    far = [(i, (i + 1) % count if i % 2 else (i - 1) % count) for i in range(count)]
    near = [(i, i + 1 if i % 2 == 0 else i - 1) for i in range(count)]
    second = lax.ppermute(inward, axis, far)
    first = lax.ppermute(outward, axis, near)
    return first, second


def from_lower(block, levels, distance):
    count = lax.axis_size("sec")
    route = []
    for start in range(0, count, levels):
        route += [(start + i, start + (i + distance) % levels) for i in range(levels)]
    return lax.ppermute(block, "sec", route)


def stencil_matrix():
    per_tile = LANES // NZ
    out = 2 * LANES
    d_y = np.zeros((4 * LANES, out), np.float32)
    d_z = np.zeros((out, out), np.float32)
    sweep = np.zeros((4 * LANES, out), np.float32)
    for y in range(2 * per_tile):
        for z in range(NZ):
            column = y * NZ + z
            here = (y + per_tile) * NZ + z
            d_y[here + NZ, column] -= 0.5
            d_y[here - NZ, column] += 0.5
            d_z[y * NZ + (z + 1) % NZ, column] -= 0.5
            d_z[y * NZ + (z - 1) % NZ, column] += 0.5
            sweep[here, column] -= 1.0
            sweep[here + 2 * NZ, column] += 0.25
            sweep[here - 2 * NZ, column] += 0.25
            base = (y + per_tile) * NZ
            sweep[base + (z + 2) % NZ, column] += 0.25
            sweep[base + (z - 2) % NZ, column] += 0.25
    return np.concatenate([d_y, d_z, sweep], axis=0)


def advance_kernel(chain, corrected, rows, *refs):
    flags, matrix, x_first, x_second = refs[:4]
    refs = list(refs[4:])
    even_x = flags[0] == 1
    even_y = flags[1] == 1
    position = flags[2]
    inputs = []
    for link in range(chain):
        state, refs = refs[:3], refs[3:]
        extra = None
        if corrected[link]:
            extra, refs = refs[:3], refs[3:]
        inputs.append((state, extra))
    out, own, state_s, term_s, fresh_s, flow_x, slow, flow_y, flow_z, slow_yz, edges, arrival = refs
    high = rows + 2 * EDGE
    block = FIELDS * high
    load_own = pltpu.make_async_copy(inputs[0][0][0], own, arrival)
    load_own.start()

    def lanes(tile):
        return pl.ds(tile * LANES, LANES)

    taken = x_first.shape[1]
    for field in range(FIELDS):
        for tile in range(4):
            one = x_first[field, :, lanes(tile)]
            two = x_second[field, :, lanes(tile)]
            edges[0, field, tile, pl.ds(0, taken), :] = jnp.where(even_x, two, one)
            edges[1, field, tile, pl.ds(0, taken), :] = jnp.where(even_x, one, two)
    sources, _ = edge_layout(chain, corrected)

    def place(target, index, kind):
        for distance, count, tiles, row, first_tile in sources[kind]:
            for tile in range(tiles):
                start = (4 - tiles) // 2 + tile
                low = edges[0, index[-1], first_tile + tile, pl.ds(row, count), :]
                top = edges[1, index[-1], first_tile + tile, pl.ds(row, count), :]
                target(start)[pl.ds(EDGE - distance - count, count), :] = low
                target(start)[pl.ds(EDGE + rows + distance, count), :] = top

    for link in reversed(range(chain)):
        (center, y_first, y_second), extra = inputs[link]
        if link == 0:
            load_own.wait()
            center = own
        for field in range(FIELDS):
            rest = jnp.full((EDGE, LANES), (1.0, 0.0, 0.0, 0.0, 2.5)[field], jnp.float32)
            for tile in range(6):
                if tile in (2, 3):
                    middle = center[field, :, lanes(tile - 2)].astype(jnp.float32)
                else:
                    one = y_first[field, :, lanes(tile % 2)].astype(jnp.float32)
                    two = y_second[field, :, lanes(tile % 2)].astype(jnp.float32)
                    middle = jnp.where(even_y, two, one) if tile < 2 else jnp.where(even_y, one, two)
                state_s[link, field, tile, pl.ds(EDGE, rows), :] = middle
                state_s[link, field, tile, pl.ds(0, EDGE), :] = rest
                state_s[link, field, tile, pl.ds(EDGE + rows, EDGE), :] = rest
            place(lambda tile: state_s.at[link, field, tile + 1], (field,), ("state", link))
        if extra is not None:
            stored, y_first, y_second = extra
            none = jnp.zeros((EDGE, LANES), jnp.float32)
            for field in range(FIELDS):
                for tile in (2, 3):
                    old = [stored[age, field, :, lanes(tile - 2)].astype(jnp.float32) for age in range(3)]
                    terms = kept_terms(old)
                    for tick in range(TICKS):
                        term_s[link, tick, field, tile - 1, pl.ds(EDGE, rows), :] = terms[tick]
                for tick in range(2):
                    plane = tick * FIELDS + field
                    one = y_first[plane].astype(jnp.float32)
                    two = y_second[plane].astype(jnp.float32)
                    term_s[link, tick, field, 0, pl.ds(EDGE, rows), :] = jnp.where(even_y, two, one)
                    term_s[link, tick, field, 3, pl.ds(EDGE, rows), :] = jnp.where(even_y, one, two)
                    for tile in range(4):
                        term_s[link, tick, field, tile, pl.ds(0, EDGE), :] = none
                        term_s[link, tick, field, tile, pl.ds(EDGE + rows, EDGE), :] = none
                    place(lambda tile: term_s.at[link, tick, field, tile], (field,), ("kept", link, tick))

    def pointwise(link, tile):
        density, mom_x, mom_y, mom_z, energy = [state_s[link, field, tile] for field in range(FIELDS)]
        inverse = 1.0 / density
        vel_x = mom_x * inverse
        vel_y = mom_y * inverse
        vel_z = mom_z * inverse
        kinetic = 0.5 * (vel_x * vel_x + vel_y * vel_y + vel_z * vel_z)
        pressure = GAMMA_LESS * (energy - density * kinetic)
        enthalpy = energy + pressure
        heat = DYNAMIC_FRICTION * kinetic + CONDUCTIVITY * (pressure * inverse)
        xy = mom_x * vel_y
        xz = mom_x * vel_z
        yz = mom_y * vel_z
        along_x = (mom_x, mom_x * vel_x + pressure, xy, xz, enthalpy * vel_x)
        along_y = (mom_y, xy, mom_y * vel_y + pressure, yz, enthalpy * vel_y)
        along_z = (mom_z, xz, yz, mom_z * vel_z + pressure, enthalpy * vel_z)
        spread = (
            DYNAMIC_FRICTION * vel_x,
            DYNAMIC_FRICTION * vel_y,
            DYNAMIC_FRICTION * vel_z,
            heat,
        )
        for field in range(FIELDS):
            place = pl.ds(link * block + field * high, high)
            flow_y[place, lanes(tile)] = along_y[field].astype(jnp.bfloat16)
            if 1 <= tile <= 4:
                flow_z[place, lanes(tile - 1)] = along_z[field].astype(jnp.bfloat16)
                flow_x[link, field, tile - 1, pl.ds(EDGE, high), :] = along_x[field]
            if field:
                slow_yz[place, lanes(tile)] = spread[field - 1].astype(jnp.bfloat16)
                if 1 <= tile <= 4:
                    slow[link, field - 1, tile - 1, pl.ds(EDGE, high), :] = spread[field - 1]

    for link in range(chain):
        slow_yz[pl.ds(link * block, high), :] = jnp.zeros((high, 6 * LANES), jnp.bfloat16)

    def along_x(link, field, tile):
        def shifted(ref, index, step):
            return ref[link, index, tile - 1, pl.ds(EDGE + step, high), :]

        total = 0.5 * (shifted(flow_x, field, -1) - shifted(flow_x, field, 1))
        if field:
            total = total + (
                0.25 * (shifted(slow, field - 1, 2) + shifted(slow, field - 1, -2))
                - 0.5 * shifted(slow, field - 1, 0)
            )
        return total

    for tick in range(TICKS):
        last = tick == TICKS - 1
        active = min(chain, TICKS - tick + 1)
        for link in reversed(range(active)):
            for tile in range(6) if tick == 0 else range(1, 5):
                pointwise(link, tile)
        tall = pl.ds(0, active * block)
        for group in ((2, 3),) if last else ((1, 2), (3, 4)):
            around = pl.ds((group[0] - 1) * LANES, 4 * LANES)
            inner = pl.ds((group[0] - 1) * LANES, 2 * LANES)
            left = jnp.concatenate([flow_y[tall, around], flow_z[tall, inner], slow_yz[tall, around]], axis=1)
            product = jnp.dot(left, matrix[...], preferred_element_type=jnp.float32)
            for link in reversed(range(active)):
                for field in range(FIELDS):
                    for side, tile in enumerate(group):
                        start = link * block + field * high
                        rate = product[start : start + high, side * LANES : (side + 1) * LANES]
                        rate = rate + along_x(link, field, tile)
                        if link:
                            fresh_s[link - 1, tick, field, tile - 1] = rate.astype(jnp.bfloat16).astype(
                                jnp.float32
                            )
                        if link + tick >= TICKS:
                            continue
                        step = rate
                        if corrected[link]:
                            extra = term_s[link, tick, field, tile - 1] + QUAD_WEIGHTS[3] * fresh_s[
                                link, tick, field, tile - 1
                            ]
                            for age in range(tick):
                                weight = QUAD_WEIGHTS[3 - tick + age] - (1.0 if age == tick - 1 else 0.0)
                                extra = extra + weight * fresh_s[link, age, field, tile - 1]
                            step = rate + jnp.where(position > link, extra, 0.0)
                        state = state_s[link, field, tile] + TIME_STEP * step
                        if not last:
                            state_s[link, field, tile] = state
                        elif link == 0:
                            out[field, :, lanes(tile - 2)] = state[EDGE : EDGE + rows]


def edge_layout(chain, corrected):
    sources = {}
    wide = []
    narrow = []
    for link in range(chain):
        wide.append((("state", link), 0, 4))
        narrow.append((("state", link), 4))
        if corrected[link]:
            wide.append((("kept", link, 0), 0, 2))
            narrow.append((("kept", link, 0), 2))
            narrow.append((("kept", link, 1), 0))
    row = 0
    for kind, distance, count in wide:
        sources.setdefault(kind, []).append((distance, count, 4, row, 0))
        row += count
    for place, (kind, distance) in enumerate(narrow):
        sources.setdefault(kind, []).append((distance, 2, 2, row + 2 * (place // 2), 2 * (place % 2)))
    return sources, row + 2 * ((len(narrow) + 1) // 2)


def kept_terms(old):
    first, second, third, _ = QUAD_WEIGHTS
    return (
        first * old[0] + second * old[1] + (third - 1.0) * old[2],
        first * old[1] + second * old[2],
        first * old[2],
    )


def per_device(fields, stored_rates):
    levels = min(4, lax.axis_size("sec"))
    position = lax.axis_index("sec") % levels
    even_x = lax.axis_index("gx") % 2 == 0 if lax.axis_size("gx") % 2 == 0 else jnp.bool_(True)
    even_y = lax.axis_index("gy") % 2 == 0 if lax.axis_size("gy") % 2 == 0 else jnp.bool_(True)
    block = fields[0]
    stored = stored_rates[0]
    rows, columns = block.shape[1:]
    chain = min(levels, TICKS + 1)
    corrected = [link < levels - 1 and link < TICKS for link in range(chain)]
    sent = block.astype(jnp.bfloat16)

    def padded_y(pair, center):
        first, second = pair
        low, top = jnp.where(even_y, second, first), jnp.where(even_y, first, second)
        return jnp.concatenate([low[:, :, -LANES:], center, top[:, :, :LANES]], axis=2)

    own_y = neighbours("gy", even_y, sent, sent)
    centers = [sent] + [from_lower(sent, levels, link) for link in range(1, chain)]
    kept = jnp.concatenate(kept_terms(stored.astype(jnp.float32))[:2], axis=0).astype(jnp.bfloat16)
    kept_y = neighbours("gy", even_y, kept[:, :, :LANES], kept[:, :, -LANES:])
    both = jnp.concatenate(own_y, axis=0)
    forwarded = [from_lower(both, levels, link) for link in range(1, chain)]
    kept_y, forwarded = lax.optimization_barrier((kept_y, forwarded))

    padded = {}
    operands = []
    for link in range(chain):
        if link:
            link_y = (forwarded[link - 1][:FIELDS], forwarded[link - 1][FIELDS:])
            operands += [centers[link], *link_y]
        else:
            link_y = own_y
            operands += [block, *own_y]
        padded["state", link] = padded_y(link_y, centers[link])
        if corrected[link]:
            if link:
                link_kept = from_lower(kept, levels, link)
                link_y = tuple(from_lower(half, levels, link) for half in kept_y)
                operands += [from_lower(stored, levels, link), *link_y]
            else:
                link_kept, link_y = kept, kept_y
                operands += [stored, *link_y]
            link_padded = padded_y(link_y, link_kept)
            padded["kept", link, 0] = link_padded[:FIELDS]
            padded["kept", link, 1] = link_padded[FIELDS:]

    sources, taken = edge_layout(chain, corrected)
    width = columns + 2 * LANES

    def edge(from_top):
        grid = {}
        for kind, pieces in sources.items():
            for distance, count, tiles, row, first_tile in pieces:
                start = rows - distance - count if from_top else distance
                skip = (4 - tiles) // 2 * LANES
                grid[row, first_tile] = padded[kind][:, start : start + count, skip : width - skip]
        parts = []
        for row, first_tile in sorted(grid):
            if first_tile:
                continue
            part = grid[row, 0]
            if part.shape[2] < width:
                part = jnp.concatenate([part, grid.get((row, 2), part)], axis=2)
            parts.append(part)
        return jnp.concatenate(parts, axis=1)

    over_x = neighbours("gx", even_x, edge(False), edge(True))
    operands = [half.astype(jnp.float32) for half in over_x] + operands
    flags = jnp.stack([even_x.astype(jnp.int32), even_y.astype(jnp.int32), position])
    matrix = jnp.asarray(stencil_matrix(), jnp.bfloat16)
    high = rows + 2 * EDGE
    tall = high + 2 * EDGE
    vmem = pl.BlockSpec(memory_space=pltpu.VMEM)
    specs = [vmem] * (len(operands) + 1)
    specs[3] = pl.BlockSpec(memory_space=pl.ANY)
    result = pl.pallas_call(
        functools.partial(advance_kernel, chain, corrected, rows),
        out_shape=jax.ShapeDtypeStruct((FIELDS, rows, columns), jnp.float32),
        in_specs=[pl.BlockSpec(memory_space=pltpu.SMEM)] + specs,
        out_specs=vmem,
        scratch_shapes=[
            pltpu.VMEM((FIELDS, rows, columns), jnp.float32),
            pltpu.VMEM((chain, FIELDS, 6, high, LANES), jnp.float32),
            pltpu.VMEM((chain, TICKS, FIELDS, 4, high, LANES), jnp.float32),
            pltpu.VMEM((chain, TICKS, FIELDS, 4, high, LANES), jnp.float32),
            pltpu.VMEM((chain, FIELDS, 4, tall, LANES), jnp.float32),
            pltpu.VMEM((chain, FIELDS - 1, 4, tall, LANES), jnp.float32),
            pltpu.VMEM((chain * FIELDS * high, 6 * LANES), jnp.bfloat16),
            pltpu.VMEM((chain * FIELDS * high, 4 * LANES), jnp.bfloat16),
            pltpu.VMEM((chain * FIELDS * high, 6 * LANES), jnp.bfloat16),
            pltpu.VMEM((2, FIELDS, 4, -(-taken // 8) * 8, LANES), jnp.float32),
            pltpu.SemaphoreType.DMA(()),
        ],
        compiler_params=pltpu.CompilerParams(vmem_limit_bytes=48 * 1024 * 1024),
    )(flags, matrix, *operands)
    return result[None]


def solution(mesh):
    return jax.shard_map(
        per_device,
        mesh=mesh,
        in_specs=(P("sec", None, "gx", "gy"), P("sec", None, None, "gx", "gy")),
        out_specs=P("sec", None, "gx", "gy"),
        check_vma=False,
    )
```

time: 35.5 us -> 27.3 us (0.77)
  waiting for transfers between devices: 14.7 us -> 7.43 us
  local copies, waits for them, and re-layouts: 0.95 us -> 0.55 us
    ppermute x4 -> x3, starting transfers between devices: 5.69 us -> 2.16 us  [neighbours(): first = lax.ppermute(outward, axis, near)]
    ppermute x4 -> x3, waiting for transfers between devices: 8.81 us -> 5.39 us  [neighbours(): second = lax.ppermute(inward, axis, far)]
    ppermute x4 -> x3, starting transfers between devices: 3.64 us -> 6.99 us  [neighbours(): second = lax.ppermute(inward, axis, far)]
    ppermute x2, waiting for transfers between devices: 3.78 us -> 0.77 us  [from_lower(): return lax.ppermute(block, 'sec', route)]
    convert_element_type x7 -> x3, other arithmetic: 1.05 us -> 0.06 us  [the longest x1 0.04 us: per_device(): stored.astype(jnp.float32)]
    convert_element_type x1, other arithmetic: 0.01 us -> 0.97 us  [per_device(): sent = block.astype(jnp.bfloat16)]
    unnamed x9 -> x6, local copies, waits for them, and re-layouts: 0.94 us -> 0.02 us
    ppermute x4 -> x3, waiting for transfers between devices: 2.11 us -> 1.27 us  [neighbours(): first = lax.ppermute(outward, axis, near)]
  transfers between devices with their start and end apart: 10 -> 8, of which waited for: 7 -> 4; matrix products, arithmetic and copies ran while one was open for 1% -> 1% of each run, Pallas kernels for 0% -> 0%
where the time goes in v2:
time: 27.3 us; the launch traced here: 27.2 us
  starting transfers between devices  12.2 us (45%)
  waiting for transfers between devices  7.43 us (27%)
  Pallas kernels  5.34 us (20%)
  other arithmetic  1.38 us (5%)
  local copies, waits for them, and re-layouts  0.55 us (2%)
    ppermute x3, starting transfers between devices, neighbours(): second = lax.ppermute(inward, axis, far)  6.99 us
    ppermute x3, waiting for transfers between devices, neighbours(): second = lax.ppermute(inward, axis, far)  5.39 us
    pallas_call x1, Pallas kernels, per_device(): pl.pallas_call(functools.partial(advance_kernel, chain, corrected, rows),...  5.34 us
    ppermute x2, starting transfers between devices, from_lower(): return lax.ppermute(block, 'sec', route)  3.07 us
    ppermute x3, starting transfers between devices, neighbours(): first = lax.ppermute(outward, axis, near)  2.16 us
    ppermute x3, waiting for transfers between devices, neighbours(): first = lax.ppermute(outward, axis, near)  1.27 us
    convert_element_type x1, other arithmetic, per_device(): sent = block.astype(jnp.bfloat16)  0.97 us
    ppermute x2, waiting for transfers between devices, from_lower(): return lax.ppermute(block, 'sec', route)  0.77 us
  transfers between devices with their start and end apart: 8, of which 4 were waited for; matrix products, arithmetic and copies ran while one was open for 1% of the time, Pallas kernels for 0%

profile of v2, /device:TPU:0, one launch (start us, length us, event | category | flops | bytes accessed | tf_op | source)
XLA Modules:
  0.0 27.2 jit_solution(6366417448702237561)
XLA Ops:
  0.0 0.0 copy-start
  0.0 1.0 %bitcast_convert_fusion.1 = bf16[5,32,256]{2,1,0:T(8,128)(2,1)S(1)} fusion(f32[1,5,32,256]{3,2,1,0:T(8,128)} %param.3), kind=kLoop, calls=%fused_computation.39 | loop fusion | flops 40960 | bytes 245760 | tf_op jit(solution)/shard_map/convert_element_type | solution.py:280
  1.0 5.1 %collective-permute-start = (bf16[5,32,256]{2,1,0:T(8,128)(2,1)S(1)}, bf16[5,32,256]{2,1,0:T(8,128)(2,1)S(1)}, u32[]{:S(2)}, u32[]{:S(2)}) collective-permute-start(bf16[5,32,256]{2,1,0:T(8,128)(2,1)S(1)} %bitcast_convert_fusion.1), channel_id=1, source_target_pairs={{0,3},{1,2},{2,1},{3,0},{4,7},{5,6},{6,5},{7,4},{8,11},{9,10},{10,... | collective-permute-start | bytes 245768 | tf_op jit(solution)/shard_map/ppermute | solution.py:39
  6.1 0.0 collective-permute-start.1
  6.1 1.5 %collective-permute-start.5 = (bf16[5,32,256]{2,1,0:T(8,128)(2,1)S(1)}, bf16[5,32,256]{2,1,0:T(8,128)(2,1)S(1)}, u32[]{:S(2)}, u32[]{:S(2)}) collective-permute-start(bf16[5,32,256]{2,1,0:T(8,128)(2,1)S(1)} %bitcast_convert_fusion.1), channel_id=1, source_target_pairs={{0,16},{16,0},{1,17},{17,1},{2,18},{18,2},{3,19},{19,3},{4,20},{20... | collective-permute-start | bytes 245768 | tf_op jit(solution)/shard_map/ppermute | solution.py:49
  7.6 0.0 copy-done
  7.6 0.1 fusion.5
  7.7 2.1 %collective-permute-start.2 = (bf16[10,32,128]{2,1,0:T(8,128)(2,1)S(1)}, bf16[10,32,128]{2,1,0:T(8,128)(2,1)S(1)}, u32[]{:S(2)}, u32[]{:S(2)}) collective-permute-start(bf16[10,32,128]{2,1,0:T(8,128)(2,1)S(1)} %get-tuple-element.28), channel_id=1, source_target_pairs={{0,1},{1,0},{2,3},{3,2},{4,5},{5,4},{6,7},{7,6},{8,9},{9,8},{10,11... | collective-permute-start | bytes 245768 | tf_op jit(solution)/shard_map/ppermute | solution.py:40
  9.8 0.2 collective-permute-start.3
  10.2 0.0 collective-permute-done.refs_6_
  10.2 1.3 %collective-permute-done.1.refs_5_ = bf16[5,32,256]{2,1,0:T(8,128)(2,1)S(1)} collective-permute-done((bf16[5,32,256]{2,1,0:T(8,128)(2,1)S(1)}, bf16[5,32,256]{2,1,0:T(8,128)(2,1)S(1)}, u32[]{:S(2)}, u32[]{:S(2)}) %collective-permute-start.1) | collective-permute-done | bytes 81952 | tf_op jit(solution)/shard_map/ppermute | solution.py:40
  11.5 1.6 %collective-permute-start.4 = (bf16[10,32,256]{2,1,0:T(8,128)(2,1)S(1)}, bf16[10,32,256]{2,1,0:T(8,128)(2,1)S(1)}, u32[]{:S(2)}, u32[]{:S(2)}) collective-permute-start(bf16[10,32,256]{2,1,0:T(8,128)(2,1)S(1)} %pad_maximum_fusion), channel_id=1, source_target_pairs={{0,16},{16,0},{1,17},{17,1},{2,18},{18,2},{3,19},{19,3},{4,20},{20... | collective-permute-start | bytes 491528 | tf_op jit(solution)/shard_map/ppermute | solution.py:49
  13.0 0.0 collective-permute-done.5.refs_10_
  13.1 0.0 collective-permute-done.2.refs_8_
  13.2 2.9 %collective-permute-done.3.refs_9_ = bf16[10,32,128]{2,1,0:T(8,128)(2,1)S(1)} collective-permute-done((bf16[10,32,128]{2,1,0:T(8,128)(2,1)S(1)}, bf16[10,32,128]{2,1,0:T(8,128)(2,1)S(1)}, u32[]{:S(2)}, u32[]{:S(2)}) %collective-permute-start.3) | collective-permute-done | bytes 81952 | tf_op jit(solution)/shard_map/ppermute | solution.py:39
  16.1 0.8 %collective-permute-done.4 = bf16[10,32,256]{2,1,0:T(8,128)(2,1)S(1)} collective-permute-done((bf16[10,32,256]{2,1,0:T(8,128)(2,1)S(1)}, bf16[10,32,256]{2,1,0:T(8,128)(2,1)S(1)}, u32[]{:S(2)}, u32[]{:S(2)}) %collective-permute-start.4) | collective-permute-done | bytes 163872 | tf_op jit(solution)/shard_map/ppermute | solution.py:49
  16.9 0.0 copy-start.2
  17.0 0.2 concatenate.41
  17.2 0.2 concatenate.44
  17.5 0.1 collective-permute-start.6
  17.5 1.7 %collective-permute-start.7 = (bf16[5,14,512]{2,1,0:T(8,128)(2,1)S(1)}, bf16[5,14,512]{2,1,0:T(8,128)(2,1)S(1)}, u32[]{:S(2)}, u32[]{:S(2)}) collective-permute-start(bf16[5,14,512]{2,1,0:T(8,128)(2,1)S(1)} %get-tuple-element.15), channel_id=1, source_target_pairs={{0,12},{4,8},{8,4},{12,0},{1,13},{5,9},{9,5},{13,1},{2,14},{6,10},... | collective-permute-start | bytes 215048 | tf_op jit(solution)/shard_map/ppermute | solution.py:39
  19.2 0.1 pad_add_fusion.refs_0_
  19.3 0.0 collective-permute-done.6
  19.3 0.0 copy-start.1
  19.3 2.5 %collective-permute-done.7 = bf16[5,14,512]{2,1,0:T(8,128)(2,1)S(1)} collective-permute-done((bf16[5,14,512]{2,1,0:T(8,128)(2,1)S(1)}, bf16[5,14,512]{2,1,0:T(8,128)(2,1)S(1)}, u32[]{:S(2)}, u32[]{:S(2)}) %collective-permute-start.7) | collective-permute-done | bytes 71712 | tf_op jit(solution)/shard_map/ppermute | solution.py:39
  21.8 0.0 copy-done.2
  21.8 0.0 copy-done.1
  21.8 5.3 %shard_map.37 = f32[5,32,256]{2,1,0:T(8,128)} custom-call(s32[3]{0:T(128)S(1)} %pad_add_fusion.refs_0_, bf16[1280,256]{1,0:T(8,128)(2,1)S(1)} %copy-done.2, f32[5,14,512]{2,1,0:T(8,128)S(1)} %convert_element_type.17.refs_2_, f32[5,14,512]{2,1,0:T(8,128)S(1)} %convert_element_type.18.refs_3_, f32[5,32,256]{2,1,0:T(8,128)S(1)} %bitcast.13, ...), custom_call_target="tpu_custom_call" | custom-call | tf_op jit(solution)/shard_map/pallas_call | solution.py:346
  (19 shorter events, 0.4 us)
Async XLA Ops:
  0.0 7.6 %copy-start = (bf16[1,3,5,32,256]{4,3,2,1,0:T(8,128)(2,1)S(1)}, bf16[1,3,5,32,256]{4,3,2,1,0:T(8,128)(2,1)}, u32[]{:S(2)}) copy-start(bf16[1,3,5,32,256]{4,3,2,1,0:T(8,128)(2,1)} %param.4) | copy-start | bytes 737284
  1.0 9.2 %collective-permute-start = (bf16[5,32,256]{2,1,0:T(8,128)(2,1)S(1)}, bf16[5,32,256]{2,1,0:T(8,128)(2,1)S(1)}, u32[]{:S(2)}, u32[]{:S(2)}) collective-permute-start(bf16[5,32,256]{2,1,0:T(8,128)(2,1)S(1)} %bitcast_convert_fusion.1), channel_id=1, source_target_pairs={{0,3},{1,2},{2,1},{3,0},{4,7},{5,6},{6,5},{7,4},{8,11},{9,10},{10,... | collective-permute-start | bytes 245768 | tf_op jit(solution)/shard_map/ppermute | solution.py:39
  6.1 5.3 %collective-permute-start.1 = (bf16[5,32,256]{2,1,0:T(8,128)(2,1)S(1)}, bf16[5,32,256]{2,1,0:T(8,128)(2,1)S(1)}, u32[]{:S(2)}, u32[]{:S(2)}) collective-permute-start(bf16[5,32,256]{2,1,0:T(8,128)(2,1)S(1)} %bitcast_convert_fusion.1), channel_id=1, source_target_pairs={{0,1},{1,0},{2,3},{3,2},{4,5},{5,4},{6,7},{7,6},{8,9},{9,8},{10,11... | collective-permute-start | bytes 245768 | tf_op jit(solution)/shard_map/ppermute | solution.py:40
  6.1 7.0 %collective-permute-start.5 = (bf16[5,32,256]{2,1,0:T(8,128)(2,1)S(1)}, bf16[5,32,256]{2,1,0:T(8,128)(2,1)S(1)}, u32[]{:S(2)}, u32[]{:S(2)}) collective-permute-start(bf16[5,32,256]{2,1,0:T(8,128)(2,1)S(1)} %bitcast_convert_fusion.1), channel_id=1, source_target_pairs={{0,16},{16,0},{1,17},{17,1},{2,18},{18,2},{3,19},{19,3},{4,20},{20... | collective-permute-start | bytes 245768 | tf_op jit(solution)/shard_map/ppermute | solution.py:49
  7.7 5.4 %collective-permute-start.2 = (bf16[10,32,128]{2,1,0:T(8,128)(2,1)S(1)}, bf16[10,32,128]{2,1,0:T(8,128)(2,1)S(1)}, u32[]{:S(2)}, u32[]{:S(2)}) collective-permute-start(bf16[10,32,128]{2,1,0:T(8,128)(2,1)S(1)} %get-tuple-element.28), channel_id=1, source_target_pairs={{0,1},{1,0},{2,3},{3,2},{4,5},{5,4},{6,7},{7,6},{8,9},{9,8},{10,11... | collective-permute-start | bytes 245768 | tf_op jit(solution)/shard_map/ppermute | solution.py:40
  9.8 6.2 %collective-permute-start.3 = (bf16[10,32,128]{2,1,0:T(8,128)(2,1)S(1)}, bf16[10,32,128]{2,1,0:T(8,128)(2,1)S(1)}, u32[]{:S(2)}, u32[]{:S(2)}) collective-permute-start(bf16[10,32,128]{2,1,0:T(8,128)(2,1)S(1)} %get-tuple-element.27), channel_id=1, source_target_pairs={{0,3},{1,2},{2,1},{3,0},{4,7},{5,6},{6,5},{7,4},{8,11},{9,10},{10,... | collective-permute-start | bytes 245768 | tf_op jit(solution)/shard_map/ppermute | solution.py:39
  11.5 5.4 %collective-permute-start.4 = (bf16[10,32,256]{2,1,0:T(8,128)(2,1)S(1)}, bf16[10,32,256]{2,1,0:T(8,128)(2,1)S(1)}, u32[]{:S(2)}, u32[]{:S(2)}) collective-permute-start(bf16[10,32,256]{2,1,0:T(8,128)(2,1)S(1)} %pad_maximum_fusion), channel_id=1, source_target_pairs={{0,16},{16,0},{1,17},{17,1},{2,18},{18,2},{3,19},{19,3},{4,20},{20... | collective-permute-start | bytes 491528 | tf_op jit(solution)/shard_map/ppermute | solution.py:49
  16.9 4.9 %copy-start.2 = (bf16[1280,256]{1,0:T(8,128)(2,1)S(1)}, bf16[1280,256]{1,0:T(8,128)(2,1)}, u32[]{:S(2)}) copy-start(bf16[1280,256]{1,0:T(8,128)(2,1)} %constant.41.clone.refs_1_) | copy-start | bytes 1966084
  17.5 1.8 %collective-permute-start.6 = (bf16[5,14,512]{2,1,0:T(8,128)(2,1)S(1)}, bf16[5,14,512]{2,1,0:T(8,128)(2,1)S(1)}, u32[]{:S(2)}, u32[]{:S(2)}) collective-permute-start(bf16[5,14,512]{2,1,0:T(8,128)(2,1)S(1)} %get-tuple-element.16), channel_id=1, source_target_pairs={{0,4},{4,0},{8,12},{12,8},{1,5},{5,1},{9,13},{13,9},{2,6},{6,2},{1... | collective-permute-start | bytes 215048 | tf_op jit(solution)/shard_map/ppermute | solution.py:40
  17.5 4.2 %collective-permute-start.7 = (bf16[5,14,512]{2,1,0:T(8,128)(2,1)S(1)}, bf16[5,14,512]{2,1,0:T(8,128)(2,1)S(1)}, u32[]{:S(2)}, u32[]{:S(2)}) collective-permute-start(bf16[5,14,512]{2,1,0:T(8,128)(2,1)S(1)} %get-tuple-element.15), channel_id=1, source_target_pairs={{0,12},{4,8},{8,4},{12,0},{1,13},{5,9},{9,5},{13,1},{2,14},{6,10},... | collective-permute-start | bytes 215048 | tf_op jit(solution)/shard_map/ppermute | solution.py:39
  19.3 2.5 %copy-start.1 = (f32[1,5,32,256]{3,2,1,0:T(8,128)S(1)}, f32[1,5,32,256]{3,2,1,0:T(8,128)}, u32[]{:S(2)}) copy-start(f32[1,5,32,256]{3,2,1,0:T(8,128)} %param.3) | copy-start | bytes 491524

commit v3 on v2

--- a/solution.py
+++ b/solution.py
@@ -19,7 +19,9 @@
 QUAD_WEIGHTS = (1.0 / 24.0, -5.0 / 24.0, 19.0 / 24.0, 9.0 / 24.0)
 
 LANES = 128
-EDGE = 8
+FIRST = 12
+START = 8
+WINDOW = 2 * (FIRST - START)
 FIELDS = 5
 
 
@@ -51,10 +53,11 @@
 
 def stencil_matrix():
     per_tile = LANES // NZ
-    out = 2 * LANES
-    d_y = np.zeros((4 * LANES, out), np.float32)
-    d_z = np.zeros((out, out), np.float32)
-    sweep = np.zeros((4 * LANES, out), np.float32)
+    wide = 2 * LANES
+    half = LANES // 2
+    d_y = np.zeros((4 * LANES, wide), np.float32)
+    d_z = np.zeros((wide, wide), np.float32)
+    sweep = np.zeros((4 * LANES, wide), np.float32)
     for y in range(2 * per_tile):
         for z in range(NZ):
             column = y * NZ + z
@@ -69,7 +72,14 @@
             base = (y + per_tile) * NZ
             sweep[base + (z + 2) % NZ, column] += 0.25
             sweep[base + (z - 2) % NZ, column] += 0.25
-    return np.concatenate([d_y, d_z, sweep], axis=0)
+
+    def inner(matrix):
+        return matrix[LANES : 3 * LANES]
+
+    def outer(matrix):
+        return np.concatenate([matrix[3 * LANES : 3 * LANES + half], matrix[half:LANES]])
+
+    return np.concatenate([inner(d_y), d_z, inner(sweep), outer(d_y), outer(sweep)], axis=0)
 
 
 def advance_kernel(chain, corrected, rows, *refs):
@@ -85,9 +95,10 @@
         if corrected[link]:
             extra, refs = refs[:3], refs[3:]
         inputs.append((state, extra))
-    out, own, state_s, term_s, fresh_s, flow_x, slow, flow_y, flow_z, slow_yz, edges, arrival = refs
-    high = rows + 2 * EDGE
-    block = FIELDS * high
+    out, own, state_s, term_s, fresh_s, flow_x, slow, flow_y, flow_z, edges, arrival = refs
+    high = rows + WINDOW
+    above = START + high
+    window = pl.ds(START, high)
     load_own = pltpu.make_async_copy(inputs[0][0][0], own, arrival)
     load_own.start()
 
@@ -109,16 +120,16 @@
                 start = (4 - tiles) // 2 + tile
                 low = edges[0, index[-1], first_tile + tile, pl.ds(row, count), :]
                 top = edges[1, index[-1], first_tile + tile, pl.ds(row, count), :]
-                target(start)[pl.ds(EDGE - distance - count, count), :] = low
-                target(start)[pl.ds(EDGE + rows + distance, count), :] = top
-
-    for link in reversed(range(chain)):
+                target(start)[pl.ds(FIRST - distance - count, count), :] = low
+                target(start)[pl.ds(FIRST + rows + distance, count), :] = top
+
+    def assemble(link):
         (center, y_first, y_second), extra = inputs[link]
         if link == 0:
             load_own.wait()
             center = own
         for field in range(FIELDS):
-            rest = jnp.full((EDGE, LANES), (1.0, 0.0, 0.0, 0.0, 2.5)[field], jnp.float32)
+            rest = jnp.full((FIRST, LANES), (1.0, 0.0, 0.0, 0.0, 2.5)[field], jnp.float32)
             for tile in range(6):
                 if tile in (2, 3):
                     middle = center[field, :, lanes(tile - 2)].astype(jnp.float32)
@@ -126,32 +137,36 @@
                     one = y_first[field, :, lanes(tile % 2)].astype(jnp.float32)
                     two = y_second[field, :, lanes(tile % 2)].astype(jnp.float32)
                     middle = jnp.where(even_y, two, one) if tile < 2 else jnp.where(even_y, one, two)
-                state_s[link, field, tile, pl.ds(EDGE, rows), :] = middle
-                state_s[link, field, tile, pl.ds(0, EDGE), :] = rest
-                state_s[link, field, tile, pl.ds(EDGE + rows, EDGE), :] = rest
+                state_s[link, field, tile, pl.ds(FIRST, rows), :] = middle
+                state_s[link, field, tile, pl.ds(0, FIRST), :] = rest
+                state_s[link, field, tile, pl.ds(FIRST + rows, FIRST), :] = rest
             place(lambda tile: state_s.at[link, field, tile + 1], (field,), ("state", link))
+
+    def assemble_terms(link):
+        extra = inputs[link][1]
         if extra is not None:
             stored, y_first, y_second = extra
-            none = jnp.zeros((EDGE, LANES), jnp.float32)
+            none = jnp.zeros((FIRST, LANES), jnp.float32)
             for field in range(FIELDS):
                 for tile in (2, 3):
                     old = [stored[age, field, :, lanes(tile - 2)].astype(jnp.float32) for age in range(3)]
                     terms = kept_terms(old)
                     for tick in range(TICKS):
-                        term_s[link, tick, field, tile - 1, pl.ds(EDGE, rows), :] = terms[tick]
+                        term_s[link, tick, field, tile - 1, pl.ds(FIRST, rows), :] = terms[tick]
                 for tick in range(2):
                     plane = tick * FIELDS + field
                     one = y_first[plane].astype(jnp.float32)
                     two = y_second[plane].astype(jnp.float32)
-                    term_s[link, tick, field, 0, pl.ds(EDGE, rows), :] = jnp.where(even_y, two, one)
-                    term_s[link, tick, field, 3, pl.ds(EDGE, rows), :] = jnp.where(even_y, one, two)
+                    term_s[link, tick, field, 0, pl.ds(FIRST, rows), :] = jnp.where(even_y, two, one)
+                    term_s[link, tick, field, 3, pl.ds(FIRST, rows), :] = jnp.where(even_y, one, two)
                     for tile in range(4):
-                        term_s[link, tick, field, tile, pl.ds(0, EDGE), :] = none
-                        term_s[link, tick, field, tile, pl.ds(EDGE + rows, EDGE), :] = none
+                        term_s[link, tick, field, tile, pl.ds(0, FIRST), :] = none
+                        term_s[link, tick, field, tile, pl.ds(FIRST + rows, FIRST), :] = none
                     place(lambda tile: term_s.at[link, tick, field, tile], (field,), ("kept", link, tick))
 
-    def pointwise(link, tile):
-        density, mom_x, mom_y, mom_z, energy = [state_s[link, field, tile] for field in range(FIELDS)]
+    def pointwise(link, tile, start, count, only_x):
+        place = pl.ds(start, count)
+        density, mom_x, mom_y, mom_z, energy = [state_s[link, field, tile, place, :] for field in range(FIELDS)]
         inverse = 1.0 / density
         vel_x = mom_x * inverse
         vel_y = mom_y * inverse
@@ -173,69 +188,97 @@
             heat,
         )
         for field in range(FIELDS):
-            place = pl.ds(link * block + field * high, high)
-            flow_y[place, lanes(tile)] = along_y[field].astype(jnp.bfloat16)
             if 1 <= tile <= 4:
-                flow_z[place, lanes(tile - 1)] = along_z[field].astype(jnp.bfloat16)
-                flow_x[link, field, tile - 1, pl.ds(EDGE, high), :] = along_x[field]
+                flow_x[link, field, tile - 1, place, :] = along_x[field]
             if field:
-                slow_yz[place, lanes(tile)] = spread[field - 1].astype(jnp.bfloat16)
+                slow[link, field - 1, tile, place, :] = spread[field - 1]
+            if not only_x:
+                flow_y[link, tile, pl.ds(field * high, high), :] = along_y[field]
                 if 1 <= tile <= 4:
-                    slow[link, field - 1, tile - 1, pl.ds(EDGE, high), :] = spread[field - 1]
-
-    for link in range(chain):
-        slow_yz[pl.ds(link * block, high), :] = jnp.zeros((high, 6 * LANES), jnp.bfloat16)
+                    flow_z[link, tile - 1, pl.ds(field * high, high), :] = along_z[field]
 
     def along_x(link, field, tile):
-        def shifted(ref, index, step):
-            return ref[link, index, tile - 1, pl.ds(EDGE + step, high), :]
-
-        total = 0.5 * (shifted(flow_x, field, -1) - shifted(flow_x, field, 1))
+        def shifted(ref, *index, step):
+            return ref[(link, *index, pl.ds(START + step, high))]
+
+        total = 0.5 * (shifted(flow_x, field, tile - 1, step=-1) - shifted(flow_x, field, tile - 1, step=1))
         if field:
-            total = total + (
-                0.25 * (shifted(slow, field - 1, 2) + shifted(slow, field - 1, -2))
-                - 0.5 * shifted(slow, field - 1, 0)
-            )
+            around = shifted(slow, field - 1, tile, step=2) + shifted(slow, field - 1, tile, step=-2)
+            total = total + (0.25 * around - 0.5 * shifted(slow, field - 1, tile, step=0))
         return total
 
+    from_above = lax.broadcasted_iota(jnp.int32, (FIELDS * high, LANES), 1) < LANES // 2
+
+    def products(link, tick):
+        for tile in range(6) if tick == 0 else range(1, 5):
+            pointwise(link, tile, START, high, False)
+            if tick == 0 and 1 <= tile <= 4:
+                pointwise(link, tile, 0, START, True)
+                pointwise(link, tile, above, START, True)
+
+        def spreading(tile):
+            none = jnp.zeros((high, LANES), jnp.float32)
+            return jnp.concatenate([none] + [slow[link, field, tile, window, :] for field in range(FIELDS - 1)])
+
+        found = {}
+        for low, top in ((2, 3),) if tick == TICKS - 1 else ((1, 2), (3, 4)):
+            parts = [
+                flow_y[link, low],
+                flow_y[link, top],
+                flow_z[link, low - 1],
+                flow_z[link, top - 1],
+                spreading(low),
+                spreading(top),
+                jnp.where(from_above, flow_y[link, top + 1], flow_y[link, low - 1]),
+                jnp.where(from_above, spreading(top + 1), spreading(low - 1)),
+            ]
+            left = jnp.concatenate([part.astype(jnp.bfloat16) for part in parts], axis=1)
+            found[low, top] = jnp.dot(left, matrix[...], preferred_element_type=jnp.float32)
+        return found
+
+    def update(link, tick, found):
+        last = tick == TICKS - 1
+        for group, product in found.items():
+            for field in range(FIELDS):
+                for side, tile in enumerate(group):
+                    start = field * high
+                    rate = product[start : start + high, side * LANES : (side + 1) * LANES]
+                    rate = rate + along_x(link, field, tile)
+                    if link:
+                        fresh_s[link - 1, tick, field, tile - 1] = rate.astype(jnp.bfloat16).astype(jnp.float32)
+                    if link + tick >= TICKS:
+                        continue
+                    step = rate
+                    if corrected[link]:
+                        extra = term_s[link, tick, field, tile - 1, window, :] + QUAD_WEIGHTS[3] * fresh_s[
+                            link, tick, field, tile - 1
+                        ]
+                        for age in range(tick):
+                            weight = QUAD_WEIGHTS[3 - tick + age] - (1.0 if age == tick - 1 else 0.0)
+                            extra = extra + weight * fresh_s[link, age, field, tile - 1]
+                        step = rate + jnp.where(position > link, extra, 0.0)
+                    state = state_s[link, field, tile, window, :] + TIME_STEP * step
+                    state_s[link, field, tile, window, :] = state
+                    if last and link == 0:
+                        out[field, :, lanes(tile - 2)] = state_s[link, field, tile, pl.ds(FIRST, rows), :]
+
+    waiting = {}
+
+    def finish(link, tick):
+        if (link, tick) in waiting:
+            finish(link + 1, tick)
+            update(link, tick, waiting.pop((link, tick)))
+
     for tick in range(TICKS):
-        last = tick == TICKS - 1
-        active = min(chain, TICKS - tick + 1)
-        for link in reversed(range(active)):
-            for tile in range(6) if tick == 0 else range(1, 5):
-                pointwise(link, tile)
-        tall = pl.ds(0, active * block)
-        for group in ((2, 3),) if last else ((1, 2), (3, 4)):
-            around = pl.ds((group[0] - 1) * LANES, 4 * LANES)
-            inner = pl.ds((group[0] - 1) * LANES, 2 * LANES)
-            left = jnp.concatenate([flow_y[tall, around], flow_z[tall, inner], slow_yz[tall, around]], axis=1)
-            product = jnp.dot(left, matrix[...], preferred_element_type=jnp.float32)
-            for link in reversed(range(active)):
-                for field in range(FIELDS):
-                    for side, tile in enumerate(group):
-                        start = link * block + field * high
-                        rate = product[start : start + high, side * LANES : (side + 1) * LANES]
-                        rate = rate + along_x(link, field, tile)
-                        if link:
-                            fresh_s[link - 1, tick, field, tile - 1] = rate.astype(jnp.bfloat16).astype(
-                                jnp.float32
-                            )
-                        if link + tick >= TICKS:
-                            continue
-                        step = rate
-                        if corrected[link]:
-                            extra = term_s[link, tick, field, tile - 1] + QUAD_WEIGHTS[3] * fresh_s[
-                                link, tick, field, tile - 1
-                            ]
-                            for age in range(tick):
-                                weight = QUAD_WEIGHTS[3 - tick + age] - (1.0 if age == tick - 1 else 0.0)
-                                extra = extra + weight * fresh_s[link, age, field, tile - 1]
-                            step = rate + jnp.where(position > link, extra, 0.0)
-                        state = state_s[link, field, tile] + TIME_STEP * step
-                        if not last:
-                            state_s[link, field, tile] = state
-                        elif link == 0:
-                            out[field, :, lanes(tile - 2)] = state[EDGE : EDGE + rows]
+        for link in reversed(range(min(chain, TICKS - tick + 1))):
+            if tick == 0:
+                assemble(link)
+            finish(link, tick - 1)
+            waiting[link, tick] = products(link, tick)
+            if tick == 0:
+                assemble_terms(link)
+    for link, tick in sorted(waiting, reverse=True):
+        finish(link, tick)
 
 
 def edge_layout(chain, corrected):
@@ -288,15 +331,17 @@
     centers = [sent] + [from_lower(sent, levels, link) for link in range(1, chain)]
     kept = jnp.concatenate(kept_terms(stored.astype(jnp.float32))[:2], axis=0).astype(jnp.bfloat16)
     kept_y = neighbours("gy", even_y, kept[:, :, :LANES], kept[:, :, -LANES:])
-    both = jnp.concatenate(own_y, axis=0)
-    forwarded = [from_lower(both, levels, link) for link in range(1, chain)]
+    if chain > 1:
+        first, centers = lax.optimization_barrier((own_y[0], centers))
+        own_y = first, own_y[1]
+    forwarded = [tuple(from_lower(half, levels, link) for half in own_y) for link in range(1, chain)]
     kept_y, forwarded = lax.optimization_barrier((kept_y, forwarded))
 
     padded = {}
     operands = []
     for link in range(chain):
         if link:
-            link_y = (forwarded[link - 1][:FIELDS], forwarded[link - 1][FIELDS:])
+            link_y = forwarded[link - 1]
             operands += [centers[link], *link_y]
         else:
             link_y = own_y
@@ -338,8 +383,8 @@
     operands = [half.astype(jnp.float32) for half in over_x] + operands
     flags = jnp.stack([even_x.astype(jnp.int32), even_y.astype(jnp.int32), position])
     matrix = jnp.asarray(stencil_matrix(), jnp.bfloat16)
-    high = rows + 2 * EDGE
-    tall = high + 2 * EDGE
+    high = rows + WINDOW
+    tall = rows + 2 * FIRST
     vmem = pl.BlockSpec(memory_space=pltpu.VMEM)
     specs = [vmem] * (len(operands) + 1)
     specs[3] = pl.BlockSpec(memory_space=pl.ANY)
@@ -350,14 +395,13 @@
         out_specs=vmem,
         scratch_shapes=[
             pltpu.VMEM((FIELDS, rows, columns), jnp.float32),
-            pltpu.VMEM((chain, FIELDS, 6, high, LANES), jnp.float32),
-            pltpu.VMEM((chain, TICKS, FIELDS, 4, high, LANES), jnp.float32),
+            pltpu.VMEM((chain, FIELDS, 6, tall, LANES), jnp.float32),
+            pltpu.VMEM((chain, TICKS, FIELDS, 4, tall, LANES), jnp.float32),
             pltpu.VMEM((chain, TICKS, FIELDS, 4, high, LANES), jnp.float32),
             pltpu.VMEM((chain, FIELDS, 4, tall, LANES), jnp.float32),
-            pltpu.VMEM((chain, FIELDS - 1, 4, tall, LANES), jnp.float32),
-            pltpu.VMEM((chain * FIELDS * high, 6 * LANES), jnp.bfloat16),
-            pltpu.VMEM((chain * FIELDS * high, 4 * LANES), jnp.bfloat16),
-            pltpu.VMEM((chain * FIELDS * high, 6 * LANES), jnp.bfloat16),
+            pltpu.VMEM((chain, FIELDS - 1, 6, tall, LANES), jnp.float32),
+            pltpu.VMEM((chain, 6, FIELDS * high, LANES), jnp.float32),
+            pltpu.VMEM((chain, 4, FIELDS * high, LANES), jnp.float32),
             pltpu.VMEM((2, FIELDS, 4, -(-taken // 8) * 8, LANES), jnp.float32),
             pltpu.SemaphoreType.DMA(()),
         ],

time: 27.3 us -> 26.1 us (0.956)
  Pallas kernels: 5.34 us -> 4.47 us
  waiting for transfers between devices: 7.43 us -> 6.97 us
    ppermute x3, starting transfers between devices: 6.99 us -> 5.01 us  [neighbours(): second = lax.ppermute(inward, axis, far)]
    ppermute x3, starting transfers between devices: 2.16 us -> 3.9 us  [neighbours(): first = lax.ppermute(outward, axis, near)]
    ppermute x3, waiting for transfers between devices: 1.27 us -> 0.19 us  [neighbours(): first = lax.ppermute(outward, axis, near)]
    pallas_call x1, Pallas kernels: 5.34 us -> 4.47 us  [per_device(): pl.pallas_call(functools.partial(advance_kernel, chain, corrected, rows),...]
    ppermute x2 -> x3, waiting for transfers between devices: 0.77 us -> 1.28 us  [from_lower(): return lax.ppermute(block, 'sec', route)]
    ppermute x2 -> x3, starting transfers between devices: 3.07 us -> 3.53 us  [from_lower(): return lax.ppermute(block, 'sec', route)]
  transfers between devices with their start and end apart: 8 -> 9, of which waited for: 4 -> 5; matrix products, arithmetic and copies ran while one was open for 1% -> 1% of each run, Pallas kernels for 0% -> 0%
where the time goes in v3:
time: 26.1 us; the launch traced here: 26 us
  starting transfers between devices  12.4 us (48%)
  waiting for transfers between devices  6.97 us (27%)
  Pallas kernels  4.47 us (17%)
  other arithmetic  1.37 us (5%)
  local copies, waits for them, and re-layouts  0.52 us (2%)
    ppermute x3, waiting for transfers between devices, neighbours(): second = lax.ppermute(inward, axis, far)  5.5 us
    ppermute x3, starting transfers between devices, neighbours(): second = lax.ppermute(inward, axis, far)  5.01 us
    pallas_call x1, Pallas kernels, per_device(): pl.pallas_call(functools.partial(advance_kernel, chain, corrected, rows),...  4.47 us
    ppermute x3, starting transfers between devices, neighbours(): first = lax.ppermute(outward, axis, near)  3.9 us
    ppermute x3, starting transfers between devices, from_lower(): return lax.ppermute(block, 'sec', route)  3.53 us
    ppermute x3, waiting for transfers between devices, from_lower(): return lax.ppermute(block, 'sec', route)  1.28 us
    convert_element_type x1, other arithmetic, per_device(): sent = block.astype(jnp.bfloat16)  0.97 us
  transfers between devices with their start and end apart: 9, of which 5 were waited for; matrix products, arithmetic and copies ran while one was open for 1% of the time, Pallas kernels for 0%

profile of v3, /device:TPU:0, one launch (start us, length us, event | category | flops | bytes accessed | tf_op | source)
XLA Modules:
  0.0 26.0 jit_solution(1302482132787645156)
XLA Ops:
  0.0 0.0 copy-start
  0.0 1.0 %bitcast_convert_fusion.1 = bf16[5,32,256]{2,1,0:T(8,128)(2,1)S(1)} fusion(f32[1,5,32,256]{3,2,1,0:T(8,128)} %param.3), kind=kLoop, calls=%fused_computation.38 | loop fusion | flops 40960 | bytes 245760 | tf_op jit(solution)/shard_map/convert_element_type | solution.py:323
  1.0 3.1 %collective-permute-start.1 = (bf16[5,32,256]{2,1,0:T(8,128)(2,1)S(1)}, bf16[5,32,256]{2,1,0:T(8,128)(2,1)S(1)}, u32[]{:S(2)}, u32[]{:S(2)}) collective-permute-start(bf16[5,32,256]{2,1,0:T(8,128)(2,1)S(1)} %bitcast_convert_fusion.1), channel_id=1, source_target_pairs={{0,1},{1,0},{2,3},{3,2},{4,5},{5,4},{6,7},{7,6},{8,9},{9,8},{10,11... | collective-permute-start | bytes 245768 | tf_op jit(solution)/shard_map/ppermute | solution.py:42
  4.1 1.5 %collective-permute-start.2 = (bf16[5,32,256]{2,1,0:T(8,128)(2,1)S(1)}, bf16[5,32,256]{2,1,0:T(8,128)(2,1)S(1)}, u32[]{:S(2)}, u32[]{:S(2)}) collective-permute-start(bf16[5,32,256]{2,1,0:T(8,128)(2,1)S(1)} %bitcast_convert_fusion.1), channel_id=1, source_target_pairs={{0,16},{16,0},{1,17},{17,1},{2,18},{18,2},{3,19},{19,3},{4,20},{20... | collective-permute-start | bytes 245768 | tf_op jit(solution)/shard_map/ppermute | solution.py:51
  5.6 2.5 %collective-permute-start = (bf16[5,32,256]{2,1,0:T(8,128)(2,1)S(1)}, bf16[5,32,256]{2,1,0:T(8,128)(2,1)S(1)}, u32[]{:S(2)}, u32[]{:S(2)}) collective-permute-start(bf16[5,32,256]{2,1,0:T(8,128)(2,1)S(1)} %bitcast_convert_fusion.1), channel_id=1, source_target_pairs={{0,3},{1,2},{2,1},{3,0},{4,7},{5,6},{6,5},{7,4},{8,11},{9,10},{10,... | collective-permute-start | bytes 245768 | tf_op jit(solution)/shard_map/ppermute | solution.py:41
  8.0 0.0 copy-done
  8.1 0.1 fusion.5
  8.2 0.7 %collective-permute-start.3 = (bf16[10,32,128]{2,1,0:T(8,128)(2,1)S(1)}, bf16[10,32,128]{2,1,0:T(8,128)(2,1)S(1)}, u32[]{:S(2)}, u32[]{:S(2)}) collective-permute-start(bf16[10,32,128]{2,1,0:T(8,128)(2,1)S(1)} %get-tuple-element.34), channel_id=1, source_target_pairs={{0,1},{1,0},{2,3},{3,2},{4,5},{5,4},{6,7},{7,6},{8,9},{9,8},{10,11... | collective-permute-start | bytes 245768 | tf_op jit(solution)/shard_map/ppermute | solution.py:42
  8.9 0.9 %collective-permute-start.4 = (bf16[10,32,128]{2,1,0:T(8,128)(2,1)S(1)}, bf16[10,32,128]{2,1,0:T(8,128)(2,1)S(1)}, u32[]{:S(2)}, u32[]{:S(2)}) collective-permute-start(bf16[10,32,128]{2,1,0:T(8,128)(2,1)S(1)} %get-tuple-element.33), channel_id=1, source_target_pairs={{0,3},{1,2},{2,1},{3,0},{4,7},{5,6},{6,5},{7,4},{8,11},{9,10},{10,... | collective-permute-start | bytes 245768 | tf_op jit(solution)/shard_map/ppermute | solution.py:41
  9.9 0.0 collective-permute-done.1.refs_5_
  9.9 0.0 collective-permute-done.2.refs_10_
  9.9 0.6 %collective-permute-start.5 = (bf16[5,32,256]{2,1,0:T(8,128)(2,1)S(1)}, bf16[5,32,256]{2,1,0:T(8,128)(2,1)S(1)}, u32[]{:S(2)}, u32[]{:S(2)}) collective-permute-start(bf16[5,32,256]{2,1,0:T(8,128)(2,1)S(1)} %collective-permute-done.1.refs_5_), channel_id=1, source_target_pairs={{0,16},{16,0},{1,17},{17,1},{2,18},{18,2},{3,19},{19,3},{4,20},{20... | collective-permute-start | bytes 245768 | tf_op jit(solution)/shard_map/ppermute | solution.py:51
  10.5 1.4 %collective-permute-done.refs_6_ = bf16[5,32,256]{2,1,0:T(8,128)(2,1)S(1)} collective-permute-done((bf16[5,32,256]{2,1,0:T(8,128)(2,1)S(1)}, bf16[5,32,256]{2,1,0:T(8,128)(2,1)S(1)}, u32[]{:S(2)}, u32[]{:S(2)}) %collective-permute-start) | collective-permute-done | bytes 81952 | tf_op jit(solution)/shard_map/ppermute | solution.py:41
  12.0 1.4 %collective-permute-start.6 = (bf16[5,32,256]{2,1,0:T(8,128)(2,1)S(1)}, bf16[5,32,256]{2,1,0:T(8,128)(2,1)S(1)}, u32[]{:S(2)}, u32[]{:S(2)}) collective-permute-start(bf16[5,32,256]{2,1,0:T(8,128)(2,1)S(1)} %collective-permute-done.refs_6_), channel_id=1, source_target_pairs={{0,16},{16,0},{1,17},{17,1},{2,18},{18,2},{3,19},{19,3},{4,20},{20... | collective-permute-start | bytes 245768 | tf_op jit(solution)/shard_map/ppermute | solution.py:51
  13.5 0.2 collective-permute-done.3.refs_8_
  13.7 1.6 %collective-permute-done.4.refs_9_ = bf16[10,32,128]{2,1,0:T(8,128)(2,1)S(1)} collective-permute-done((bf16[10,32,128]{2,1,0:T(8,128)(2,1)S(1)}, bf16[10,32,128]{2,1,0:T(8,128)(2,1)S(1)}, u32[]{:S(2)}, u32[]{:S(2)}) %collective-permute-start.4) | collective-permute-done | bytes 81952 | tf_op jit(solution)/shard_map/ppermute | solution.py:41
  15.3 0.0 collective-permute-done.5.refs_11_
  15.3 1.3 %collective-permute-done.6.refs_12_ = bf16[5,32,256]{2,1,0:T(8,128)(2,1)S(1)} collective-permute-done((bf16[5,32,256]{2,1,0:T(8,128)(2,1)S(1)}, bf16[5,32,256]{2,1,0:T(8,128)(2,1)S(1)}, u32[]{:S(2)}, u32[]{:S(2)}) %collective-permute-start.6) | collective-permute-done | bytes 81952 | tf_op jit(solution)/shard_map/ppermute | solution.py:51
  16.7 0.2 concatenate.37
  16.9 0.0 copy-start.2
  16.9 0.2 concatenate.40
  17.2 0.1 collective-permute-start.7
  17.2 1.6 %collective-permute-start.8 = (bf16[5,14,512]{2,1,0:T(8,128)(2,1)S(1)}, bf16[5,14,512]{2,1,0:T(8,128)(2,1)S(1)}, u32[]{:S(2)}, u32[]{:S(2)}) collective-permute-start(bf16[5,14,512]{2,1,0:T(8,128)(2,1)S(1)} %get-tuple-element.23), channel_id=1, source_target_pairs={{0,12},{4,8},{8,4},{12,0},{1,13},{5,9},{9,5},{13,1},{2,14},{6,10},... | collective-permute-start | bytes 215048 | tf_op jit(solution)/shard_map/ppermute | solution.py:41
  18.9 0.1 pad_add_fusion.refs_0_
  18.9 0.0 collective-permute-done.7
  19.0 0.0 copy-start.1
  19.0 2.5 %collective-permute-done.8 = bf16[5,14,512]{2,1,0:T(8,128)(2,1)S(1)} collective-permute-done((bf16[5,14,512]{2,1,0:T(8,128)(2,1)S(1)}, bf16[5,14,512]{2,1,0:T(8,128)(2,1)S(1)}, u32[]{:S(2)}, u32[]{:S(2)}) %collective-permute-start.8) | collective-permute-done | bytes 71712 | tf_op jit(solution)/shard_map/ppermute | solution.py:41
  21.5 0.0 copy-done.2
  21.5 0.0 copy-done.1
  21.5 4.5 %shard_map.37 = f32[5,32,256]{2,1,0:T(8,128)} custom-call(s32[3]{0:T(128)S(1)} %pad_add_fusion.refs_0_, bf16[1024,256]{1,0:T(8,128)(2,1)S(1)} %copy-done.2, f32[5,14,512]{2,1,0:T(8,128)S(1)} %convert_element_type.17.refs_2_, f32[5,14,512]{2,1,0:T(8,128)S(1)} %convert_element_type.18.refs_3_, f32[5,32,256]{2,1,0:T(8,128)S(1)} %bitcast.13, ...), custom_call_target="tpu_custom_call" | custom-call | tf_op jit(solution)/shard_map/pallas_call | solution.py:391
  (17 shorter events, 0.3 us)
Async XLA Ops:
  0.0 8.0 %copy-start = (bf16[1,3,5,32,256]{4,3,2,1,0:T(8,128)(2,1)S(1)}, bf16[1,3,5,32,256]{4,3,2,1,0:T(8,128)(2,1)}, u32[]{:S(2)}) copy-start(bf16[1,3,5,32,256]{4,3,2,1,0:T(8,128)(2,1)} %param.4) | copy-start | bytes 737284
  1.0 8.9 %collective-permute-start.1 = (bf16[5,32,256]{2,1,0:T(8,128)(2,1)S(1)}, bf16[5,32,256]{2,1,0:T(8,128)(2,1)S(1)}, u32[]{:S(2)}, u32[]{:S(2)}) collective-permute-start(bf16[5,32,256]{2,1,0:T(8,128)(2,1)S(1)} %bitcast_convert_fusion.1), channel_id=1, source_target_pairs={{0,1},{1,0},{2,3},{3,2},{4,5},{5,4},{6,7},{7,6},{8,9},{9,8},{10,11... | collective-permute-start | bytes 245768 | tf_op jit(solution)/shard_map/ppermute | solution.py:42
  4.1 5.8 %collective-permute-start.2 = (bf16[5,32,256]{2,1,0:T(8,128)(2,1)S(1)}, bf16[5,32,256]{2,1,0:T(8,128)(2,1)S(1)}, u32[]{:S(2)}, u32[]{:S(2)}) collective-permute-start(bf16[5,32,256]{2,1,0:T(8,128)(2,1)S(1)} %bitcast_convert_fusion.1), channel_id=1, source_target_pairs={{0,16},{16,0},{1,17},{17,1},{2,18},{18,2},{3,19},{19,3},{4,20},{20... | collective-permute-start | bytes 245768 | tf_op jit(solution)/shard_map/ppermute | solution.py:51
  5.6 6.4 %collective-permute-start = (bf16[5,32,256]{2,1,0:T(8,128)(2,1)S(1)}, bf16[5,32,256]{2,1,0:T(8,128)(2,1)S(1)}, u32[]{:S(2)}, u32[]{:S(2)}) collective-permute-start(bf16[5,32,256]{2,1,0:T(8,128)(2,1)S(1)} %bitcast_convert_fusion.1), channel_id=1, source_target_pairs={{0,3},{1,2},{2,1},{3,0},{4,7},{5,6},{6,5},{7,4},{8,11},{9,10},{10,... | collective-permute-start | bytes 245768 | tf_op jit(solution)/shard_map/ppermute | solution.py:41
  8.2 5.5 %collective-permute-start.3 = (bf16[10,32,128]{2,1,0:T(8,128)(2,1)S(1)}, bf16[10,32,128]{2,1,0:T(8,128)(2,1)S(1)}, u32[]{:S(2)}, u32[]{:S(2)}) collective-permute-start(bf16[10,32,128]{2,1,0:T(8,128)(2,1)S(1)} %get-tuple-element.34), channel_id=1, source_target_pairs={{0,1},{1,0},{2,3},{3,2},{4,5},{5,4},{6,7},{7,6},{8,9},{9,8},{10,11... | collective-permute-start | bytes 245768 | tf_op jit(solution)/shard_map/ppermute | solution.py:42
  8.9 6.3 %collective-permute-start.4 = (bf16[10,32,128]{2,1,0:T(8,128)(2,1)S(1)}, bf16[10,32,128]{2,1,0:T(8,128)(2,1)S(1)}, u32[]{:S(2)}, u32[]{:S(2)}) collective-permute-start(bf16[10,32,128]{2,1,0:T(8,128)(2,1)S(1)} %get-tuple-element.33), channel_id=1, source_target_pairs={{0,3},{1,2},{2,1},{3,0},{4,7},{5,6},{6,5},{7,4},{8,11},{9,10},{10,... | collective-permute-start | bytes 245768 | tf_op jit(solution)/shard_map/ppermute | solution.py:41
  9.9 5.4 %collective-permute-start.5 = (bf16[5,32,256]{2,1,0:T(8,128)(2,1)S(1)}, bf16[5,32,256]{2,1,0:T(8,128)(2,1)S(1)}, u32[]{:S(2)}, u32[]{:S(2)}) collective-permute-start(bf16[5,32,256]{2,1,0:T(8,128)(2,1)S(1)} %collective-permute-done.1.refs_5_), channel_id=1, source_target_pairs={{0,16},{16,0},{1,17},{17,1},{2,18},{18,2},{3,19},{19,3},{4,20},{20... | collective-permute-start | bytes 245768 | tf_op jit(solution)/shard_map/ppermute | solution.py:51
  12.0 4.5 %collective-permute-start.6 = (bf16[5,32,256]{2,1,0:T(8,128)(2,1)S(1)}, bf16[5,32,256]{2,1,0:T(8,128)(2,1)S(1)}, u32[]{:S(2)}, u32[]{:S(2)}) collective-permute-start(bf16[5,32,256]{2,1,0:T(8,128)(2,1)S(1)} %collective-permute-done.refs_6_), channel_id=1, source_target_pairs={{0,16},{16,0},{1,17},{17,1},{2,18},{18,2},{3,19},{19,3},{4,20},{20... | collective-permute-start | bytes 245768 | tf_op jit(solution)/shard_map/ppermute | solution.py:51
  16.9 4.6 %copy-start.2 = (bf16[1024,256]{1,0:T(8,128)(2,1)S(1)}, bf16[1024,256]{1,0:T(8,128)(2,1)}, u32[]{:S(2)}) copy-start(bf16[1024,256]{1,0:T(8,128)(2,1)} %constant.41.clone.refs_1_) | copy-start | bytes 1572868
  17.2 1.8 %collective-permute-start.7 = (bf16[5,14,512]{2,1,0:T(8,128)(2,1)S(1)}, bf16[5,14,512]{2,1,0:T(8,128)(2,1)S(1)}, u32[]{:S(2)}, u32[]{:S(2)}) collective-permute-start(bf16[5,14,512]{2,1,0:T(8,128)(2,1)S(1)} %get-tuple-element.24), channel_id=1, source_target_pairs={{0,4},{4,0},{8,12},{12,8},{1,5},{5,1},{9,13},{13,9},{2,6},{6,2},{1... | collective-permute-start | bytes 215048 | tf_op jit(solution)/shard_map/ppermute | solution.py:42
  17.2 4.2 %collective-permute-start.8 = (bf16[5,14,512]{2,1,0:T(8,128)(2,1)S(1)}, bf16[5,14,512]{2,1,0:T(8,128)(2,1)S(1)}, u32[]{:S(2)}, u32[]{:S(2)}) collective-permute-start(bf16[5,14,512]{2,1,0:T(8,128)(2,1)S(1)} %get-tuple-element.23), channel_id=1, source_target_pairs={{0,12},{4,8},{8,4},{12,0},{1,13},{5,9},{9,5},{13,1},{2,14},{6,10},... | collective-permute-start | bytes 215048 | tf_op jit(solution)/shard_map/ppermute | solution.py:41
  19.0 2.5 %copy-start.1 = (f32[1,5,32,256]{3,2,1,0:T(8,128)S(1)}, f32[1,5,32,256]{3,2,1,0:T(8,128)}, u32[]{:S(2)}) copy-start(f32[1,5,32,256]{3,2,1,0:T(8,128)} %param.3) | copy-start | bytes 491524

commit v4 on v3

--- a/solution.py
+++ b/solution.py
@@ -95,12 +95,10 @@
         if corrected[link]:
             extra, refs = refs[:3], refs[3:]
         inputs.append((state, extra))
-    out, own, state_s, term_s, fresh_s, flow_x, slow, flow_y, flow_z, edges, arrival = refs
+    out, state_s, term_s, fresh_s, flow_x, slow, flow_y, flow_z, edges = refs
     high = rows + WINDOW
     above = START + high
     window = pl.ds(START, high)
-    load_own = pltpu.make_async_copy(inputs[0][0][0], own, arrival)
-    load_own.start()
 
     def lanes(tile):
         return pl.ds(tile * LANES, LANES)
@@ -125,9 +123,6 @@
 
     def assemble(link):
         (center, y_first, y_second), extra = inputs[link]
-        if link == 0:
-            load_own.wait()
-            center = own
         for field in range(FIELDS):
             rest = jnp.full((FIRST, LANES), (1.0, 0.0, 0.0, 0.0, 2.5)[field], jnp.float32)
             for tile in range(6):
@@ -236,7 +231,7 @@
             found[low, top] = jnp.dot(left, matrix[...], preferred_element_type=jnp.float32)
         return found
 
-    def update(link, tick, found):
+    def update(link, tick, found, lowest):
         last = tick == TICKS - 1
         for group, product in found.items():
             for field in range(FIELDS):
@@ -249,36 +244,43 @@
                     if link + tick >= TICKS:
                         continue
                     step = rate
-                    if corrected[link]:
+                    if corrected[link] and not lowest:
                         extra = term_s[link, tick, field, tile - 1, window, :] + QUAD_WEIGHTS[3] * fresh_s[
                             link, tick, field, tile - 1
                         ]
                         for age in range(tick):
                             weight = QUAD_WEIGHTS[3 - tick + age] - (1.0 if age == tick - 1 else 0.0)
                             extra = extra + weight * fresh_s[link, age, field, tile - 1]
-                        step = rate + jnp.where(position > link, extra, 0.0)
+                        step = rate + (jnp.where(position > link, extra, 0.0) if link else extra)
                     state = state_s[link, field, tile, window, :] + TIME_STEP * step
                     state_s[link, field, tile, window, :] = state
                     if last and link == 0:
                         out[field, :, lanes(tile - 2)] = state_s[link, field, tile, pl.ds(FIRST, rows), :]
 
-    waiting = {}
-
-    def finish(link, tick):
-        if (link, tick) in waiting:
-            finish(link + 1, tick)
-            update(link, tick, waiting.pop((link, tick)))
-
-    for tick in range(TICKS):
-        for link in reversed(range(min(chain, TICKS - tick + 1))):
-            if tick == 0:
-                assemble(link)
-            finish(link, tick - 1)
-            waiting[link, tick] = products(link, tick)
-            if tick == 0:
-                assemble_terms(link)
-    for link, tick in sorted(waiting, reverse=True):
-        finish(link, tick)
+    def advance(links):
+        waiting = {}
+
+        def finish(link, tick):
+            if (link, tick) in waiting:
+                finish(link + 1, tick)
+                update(link, tick, waiting.pop((link, tick)), links == 1)
+
+        for tick in range(TICKS):
+            for link in reversed(range(min(links, TICKS - tick + 1))):
+                if tick == 0:
+                    assemble(link)
+                finish(link, tick - 1)
+                waiting[link, tick] = products(link, tick)
+                if tick == 0 and links > 1:
+                    assemble_terms(link)
+        for link, tick in sorted(waiting, reverse=True):
+            finish(link, tick)
+
+    if chain == 1:
+        advance(1)
+    else:
+        pl.when(position == 0)(lambda: advance(1))
+        pl.when(position > 0)(lambda: advance(chain))
 
 
 def edge_layout(chain, corrected):
@@ -320,7 +322,9 @@
     rows, columns = block.shape[1:]
     chain = min(levels, TICKS + 1)
     corrected = [link < levels - 1 and link < TICKS for link in range(chain)]
+    whole = lax.reduce_precision(block, 8, 22)
     sent = block.astype(jnp.bfloat16)
+    whole, sent = lax.optimization_barrier((whole, sent))
 
     def padded_y(pair, center):
         first, second = pair
@@ -345,7 +349,7 @@
             operands += [centers[link], *link_y]
         else:
             link_y = own_y
-            operands += [block, *own_y]
+            operands += [whole, *own_y]
         padded["state", link] = padded_y(link_y, centers[link])
         if corrected[link]:
             if link:
@@ -387,14 +391,12 @@
     tall = rows + 2 * FIRST
     vmem = pl.BlockSpec(memory_space=pltpu.VMEM)
     specs = [vmem] * (len(operands) + 1)
-    specs[3] = pl.BlockSpec(memory_space=pl.ANY)
     result = pl.pallas_call(
         functools.partial(advance_kernel, chain, corrected, rows),
         out_shape=jax.ShapeDtypeStruct((FIELDS, rows, columns), jnp.float32),
         in_specs=[pl.BlockSpec(memory_space=pltpu.SMEM)] + specs,
         out_specs=vmem,
         scratch_shapes=[
-            pltpu.VMEM((FIELDS, rows, columns), jnp.float32),
             pltpu.VMEM((chain, FIELDS, 6, tall, LANES), jnp.float32),
             pltpu.VMEM((chain, TICKS, FIELDS, 4, tall, LANES), jnp.float32),
             pltpu.VMEM((chain, TICKS, FIELDS, 4, high, LANES), jnp.float32),
@@ -403,7 +405,6 @@
             pltpu.VMEM((chain, 6, FIELDS * high, LANES), jnp.float32),
             pltpu.VMEM((chain, 4, FIELDS * high, LANES), jnp.float32),
             pltpu.VMEM((2, FIELDS, 4, -(-taken // 8) * 8, LANES), jnp.float32),
-            pltpu.SemaphoreType.DMA(()),
         ],
         compiler_params=pltpu.CompilerParams(vmem_limit_bytes=48 * 1024 * 1024),
     )(flags, matrix, *operands)

time: 26.1 us -> 25.1 us (0.962)
  the two profiles are of different devices: /device:TPU:0 before, /device:TPU:3 now
where the time goes in v4:
time: 25.1 us; the launch traced here: 24.9 us
  starting transfers between devices  10.8 us (43%)
  waiting for transfers between devices  7.62 us (30%)
  Pallas kernels  4.35 us (17%)
  other arithmetic  1.48 us (6%)
  local copies, waits for them, and re-layouts  0.52 us (2%)
    ppermute x3, waiting for transfers between devices, neighbours(): second = lax.ppermute(inward, axis, far)  5.87 us
    ppermute x3, starting transfers between devices, neighbours(): first = lax.ppermute(outward, axis, near)  4.46 us
    pallas_call x1, Pallas kernels, per_device(): pl.pallas_call(functools.partial(advance_kernel, chain, corrected, rows),...  4.35 us
    ppermute x3, starting transfers between devices, neighbours(): second = lax.ppermute(inward, axis, far)  4.3 us
    ppermute x3, starting transfers between devices, from_lower(): return lax.ppermute(block, 'sec', route)  2.04 us
    ppermute x3, waiting for transfers between devices, from_lower(): return lax.ppermute(block, 'sec', route)  1.4 us
    convert_element_type x1, other arithmetic, per_device(): sent = block.astype(jnp.bfloat16)  1.07 us
  transfers between devices with their start and end apart: 9, of which 5 were waited for; matrix products, arithmetic and copies ran while one was open for 1% of the time, Pallas kernels for 0%

profile of v4, /device:TPU:3, one launch (start us, length us, event | category | flops | bytes accessed | tf_op | source)
XLA Modules:
  0.0 24.9 jit_solution(8648315857256644800)
XLA Ops:
  0.0 0.0 copy-start
  0.0 1.1 %convert_bitcast_fusion = (bf16[5,32,256]{2,1,0:T(8,128)(2,1)S(1)}, f32[5,32,256]{2,1,0:T(8,128)S(1)}) fusion(f32[1,5,32,256]{3,2,1,0:T(8,128)} %param.3), kind=kLoop, calls=%fused_computation.13 | loop fusion | flops 81920 | bytes 409600 | tf_op jit(solution)/shard_map/convert_element_type | solution.py:326
  1.1 1.4 %collective-permute-start.1 = (bf16[5,32,256]{2,1,0:T(8,128)(2,1)S(1)}, bf16[5,32,256]{2,1,0:T(8,128)(2,1)S(1)}, u32[]{:S(2)}, u32[]{:S(2)}) collective-permute-start(bf16[5,32,256]{2,1,0:T(8,128)(2,1)S(1)} %get-tuple-element.16), channel_id=1, source_target_pairs={{0,1},{1,0},{2,3},{3,2},{4,5},{5,4},{6,7},{7,6},{8,9},{9,8},{10,11... | collective-permute-start | bytes 245768 | tf_op jit(solution)/shard_map/ppermute | solution.py:42
  2.4 0.3 %collective-permute-start.2 = (bf16[5,32,256]{2,1,0:T(8,128)(2,1)S(1)}, bf16[5,32,256]{2,1,0:T(8,128)(2,1)S(1)}, u32[]{:S(2)}, u32[]{:S(2)}) collective-permute-start(bf16[5,32,256]{2,1,0:T(8,128)(2,1)S(1)} %get-tuple-element.16), channel_id=1, source_target_pairs={{0,16},{16,0},{1,17},{17,1},{2,18},{18,2},{3,19},{19,3},{4,20},{20... | collective-permute-start | bytes 245768 | tf_op jit(solution)/shard_map/ppermute | solution.py:51
  2.7 2.2 %collective-permute-start = (bf16[5,32,256]{2,1,0:T(8,128)(2,1)S(1)}, bf16[5,32,256]{2,1,0:T(8,128)(2,1)S(1)}, u32[]{:S(2)}, u32[]{:S(2)}) collective-permute-start(bf16[5,32,256]{2,1,0:T(8,128)(2,1)S(1)} %get-tuple-element.16), channel_id=1, source_target_pairs={{0,3},{1,2},{2,1},{3,0},{4,7},{5,6},{6,5},{7,4},{8,11},{9,10},{10,... | collective-permute-start | bytes 245768 | tf_op jit(solution)/shard_map/ppermute | solution.py:41
  4.9 0.0 copy-done
  4.9 0.1 fusion.5
  5.0 0.5 %collective-permute-start.3 = (bf16[10,32,128]{2,1,0:T(8,128)(2,1)S(1)}, bf16[10,32,128]{2,1,0:T(8,128)(2,1)S(1)}, u32[]{:S(2)}, u32[]{:S(2)}) collective-permute-start(bf16[10,32,128]{2,1,0:T(8,128)(2,1)S(1)} %get-tuple-element.38), channel_id=1, source_target_pairs={{0,1},{1,0},{2,3},{3,2},{4,5},{5,4},{6,7},{7,6},{8,9},{9,8},{10,11... | collective-permute-start | bytes 245768 | tf_op jit(solution)/shard_map/ppermute | solution.py:42
  5.5 0.9 %collective-permute-start.4 = (bf16[10,32,128]{2,1,0:T(8,128)(2,1)S(1)}, bf16[10,32,128]{2,1,0:T(8,128)(2,1)S(1)}, u32[]{:S(2)}, u32[]{:S(2)}) collective-permute-start(bf16[10,32,128]{2,1,0:T(8,128)(2,1)S(1)} %get-tuple-element.37), channel_id=1, source_target_pairs={{0,3},{1,2},{2,1},{3,0},{4,7},{5,6},{6,5},{7,4},{8,11},{9,10},{10,... | collective-permute-start | bytes 245768 | tf_op jit(solution)/shard_map/ppermute | solution.py:41
  6.5 0.0 collective-permute-done.1.refs_5_
  6.5 0.0 collective-permute-done.2.refs_10_
  6.5 1.3 %collective-permute-start.5 = (bf16[5,32,256]{2,1,0:T(8,128)(2,1)S(1)}, bf16[5,32,256]{2,1,0:T(8,128)(2,1)S(1)}, u32[]{:S(2)}, u32[]{:S(2)}) collective-permute-start(bf16[5,32,256]{2,1,0:T(8,128)(2,1)S(1)} %collective-permute-done.1.refs_5_), channel_id=1, source_target_pairs={{0,16},{16,0},{1,17},{17,1},{2,18},{18,2},{3,19},{19,3},{4,20},{20... | collective-permute-start | bytes 245768 | tf_op jit(solution)/shard_map/ppermute | solution.py:51
  7.8 0.8 %collective-permute-done.refs_6_ = bf16[5,32,256]{2,1,0:T(8,128)(2,1)S(1)} collective-permute-done((bf16[5,32,256]{2,1,0:T(8,128)(2,1)S(1)}, bf16[5,32,256]{2,1,0:T(8,128)(2,1)S(1)}, u32[]{:S(2)}, u32[]{:S(2)}) %collective-permute-start) | collective-permute-done | bytes 81952 | tf_op jit(solution)/shard_map/ppermute | solution.py:41
  8.7 0.5 %collective-permute-start.6 = (bf16[5,32,256]{2,1,0:T(8,128)(2,1)S(1)}, bf16[5,32,256]{2,1,0:T(8,128)(2,1)S(1)}, u32[]{:S(2)}, u32[]{:S(2)}) collective-permute-start(bf16[5,32,256]{2,1,0:T(8,128)(2,1)S(1)} %collective-permute-done.refs_6_), channel_id=1, source_target_pairs={{0,16},{16,0},{1,17},{17,1},{2,18},{18,2},{3,19},{19,3},{4,20},{20... | collective-permute-start | bytes 245768 | tf_op jit(solution)/shard_map/ppermute | solution.py:51
  9.2 0.3 %collective-permute-done.3.refs_8_ = bf16[10,32,128]{2,1,0:T(8,128)(2,1)S(1)} collective-permute-done((bf16[10,32,128]{2,1,0:T(8,128)(2,1)S(1)}, bf16[10,32,128]{2,1,0:T(8,128)(2,1)S(1)}, u32[]{:S(2)}, u32[]{:S(2)}) %collective-permute-start.3) | collective-permute-done | bytes 81952 | tf_op jit(solution)/shard_map/ppermute | solution.py:42
  9.6 2.2 %collective-permute-done.4.refs_9_ = bf16[10,32,128]{2,1,0:T(8,128)(2,1)S(1)} collective-permute-done((bf16[10,32,128]{2,1,0:T(8,128)(2,1)S(1)}, bf16[10,32,128]{2,1,0:T(8,128)(2,1)S(1)}, u32[]{:S(2)}, u32[]{:S(2)}) %collective-permute-start.4) | collective-permute-done | bytes 81952 | tf_op jit(solution)/shard_map/ppermute | solution.py:41
  11.8 0.0 collective-permute-done.5.refs_11_
  11.8 1.4 %collective-permute-done.6.refs_12_ = bf16[5,32,256]{2,1,0:T(8,128)(2,1)S(1)} collective-permute-done((bf16[5,32,256]{2,1,0:T(8,128)(2,1)S(1)}, bf16[5,32,256]{2,1,0:T(8,128)(2,1)S(1)}, u32[]{:S(2)}, u32[]{:S(2)}) %collective-permute-start.6) | collective-permute-done | bytes 81952 | tf_op jit(solution)/shard_map/ppermute | solution.py:51
  13.3 0.2 concatenate.37
  13.5 0.0 copy-start.1
  13.5 0.2 concatenate.40
  13.8 2.6 %collective-permute-start.7 = (bf16[5,14,512]{2,1,0:T(8,128)(2,1)S(1)}, bf16[5,14,512]{2,1,0:T(8,128)(2,1)S(1)}, u32[]{:S(2)}, u32[]{:S(2)}) collective-permute-start(bf16[5,14,512]{2,1,0:T(8,128)(2,1)S(1)} %get-tuple-element.28), channel_id=1, source_target_pairs={{0,4},{4,0},{8,12},{12,8},{1,5},{5,1},{9,13},{13,9},{2,6},{6,2},{1... | collective-permute-start | bytes 215048 | tf_op jit(solution)/shard_map/ppermute | solution.py:42
  16.4 1.2 %collective-permute-start.8 = (bf16[5,14,512]{2,1,0:T(8,128)(2,1)S(1)}, bf16[5,14,512]{2,1,0:T(8,128)(2,1)S(1)}, u32[]{:S(2)}, u32[]{:S(2)}) collective-permute-start(bf16[5,14,512]{2,1,0:T(8,128)(2,1)S(1)} %get-tuple-element.27), channel_id=1, source_target_pairs={{0,12},{4,8},{8,4},{12,0},{1,13},{5,9},{9,5},{13,1},{2,14},{6,10},... | collective-permute-start | bytes 215048 | tf_op jit(solution)/shard_map/ppermute | solution.py:41
  17.6 0.1 pad_add_fusion.refs_0_
  17.7 0.0 collective-permute-done.7
  17.7 2.8 %collective-permute-done.8 = bf16[5,14,512]{2,1,0:T(8,128)(2,1)S(1)} collective-permute-done((bf16[5,14,512]{2,1,0:T(8,128)(2,1)S(1)}, bf16[5,14,512]{2,1,0:T(8,128)(2,1)S(1)}, u32[]{:S(2)}, u32[]{:S(2)}) %collective-permute-start.8) | collective-permute-done | bytes 71712 | tf_op jit(solution)/shard_map/ppermute | solution.py:41
  20.6 0.0 copy-done.1
  20.6 4.4 %shard_map.37 = f32[5,32,256]{2,1,0:T(8,128)} custom-call(s32[3]{0:T(128)S(1)} %pad_add_fusion.refs_0_, bf16[1024,256]{1,0:T(8,128)(2,1)S(1)} %copy-done.1, f32[5,14,512]{2,1,0:T(8,128)S(1)} %convert_element_type.21.refs_2_, f32[5,14,512]{2,1,0:T(8,128)S(1)} %convert_element_type.22.refs_3_, f32[5,32,256]{2,1,0:T(8,128)S(1)} %get-tuple-element.22.refs_4_, ...), custom_call_target="tpu_custom_call" | custom-call | tf_op jit(solution)/shard_map/pallas_call | solution.py:394
  (17 shorter events, 0.3 us)
Async XLA Ops:
  0.0 4.9 %copy-start = (bf16[1,3,5,32,256]{4,3,2,1,0:T(8,128)(2,1)S(1)}, bf16[1,3,5,32,256]{4,3,2,1,0:T(8,128)(2,1)}, u32[]{:S(2)}) copy-start(bf16[1,3,5,32,256]{4,3,2,1,0:T(8,128)(2,1)} %param.4) | copy-start | bytes 737284
  1.1 5.4 %collective-permute-start.1 = (bf16[5,32,256]{2,1,0:T(8,128)(2,1)S(1)}, bf16[5,32,256]{2,1,0:T(8,128)(2,1)S(1)}, u32[]{:S(2)}, u32[]{:S(2)}) collective-permute-start(bf16[5,32,256]{2,1,0:T(8,128)(2,1)S(1)} %get-tuple-element.16), channel_id=1, source_target_pairs={{0,1},{1,0},{2,3},{3,2},{4,5},{5,4},{6,7},{7,6},{8,9},{9,8},{10,11... | collective-permute-start | bytes 245768 | tf_op jit(solution)/shard_map/ppermute | solution.py:42
  2.4 4.0 %collective-permute-start.2 = (bf16[5,32,256]{2,1,0:T(8,128)(2,1)S(1)}, bf16[5,32,256]{2,1,0:T(8,128)(2,1)S(1)}, u32[]{:S(2)}, u32[]{:S(2)}) collective-permute-start(bf16[5,32,256]{2,1,0:T(8,128)(2,1)S(1)} %get-tuple-element.16), channel_id=1, source_target_pairs={{0,16},{16,0},{1,17},{17,1},{2,18},{18,2},{3,19},{19,3},{4,20},{20... | collective-permute-start | bytes 245768 | tf_op jit(solution)/shard_map/ppermute | solution.py:51
  2.7 5.9 %collective-permute-start = (bf16[5,32,256]{2,1,0:T(8,128)(2,1)S(1)}, bf16[5,32,256]{2,1,0:T(8,128)(2,1)S(1)}, u32[]{:S(2)}, u32[]{:S(2)}) collective-permute-start(bf16[5,32,256]{2,1,0:T(8,128)(2,1)S(1)} %get-tuple-element.16), channel_id=1, source_target_pairs={{0,3},{1,2},{2,1},{3,0},{4,7},{5,6},{6,5},{7,4},{8,11},{9,10},{10,... | collective-permute-start | bytes 245768 | tf_op jit(solution)/shard_map/ppermute | solution.py:41
  5.0 4.5 %collective-permute-start.3 = (bf16[10,32,128]{2,1,0:T(8,128)(2,1)S(1)}, bf16[10,32,128]{2,1,0:T(8,128)(2,1)S(1)}, u32[]{:S(2)}, u32[]{:S(2)}) collective-permute-start(bf16[10,32,128]{2,1,0:T(8,128)(2,1)S(1)} %get-tuple-element.38), channel_id=1, source_target_pairs={{0,1},{1,0},{2,3},{3,2},{4,5},{5,4},{6,7},{7,6},{8,9},{9,8},{10,11... | collective-permute-start | bytes 245768 | tf_op jit(solution)/shard_map/ppermute | solution.py:42
  5.5 6.3 %collective-permute-start.4 = (bf16[10,32,128]{2,1,0:T(8,128)(2,1)S(1)}, bf16[10,32,128]{2,1,0:T(8,128)(2,1)S(1)}, u32[]{:S(2)}, u32[]{:S(2)}) collective-permute-start(bf16[10,32,128]{2,1,0:T(8,128)(2,1)S(1)} %get-tuple-element.37), channel_id=1, source_target_pairs={{0,3},{1,2},{2,1},{3,0},{4,7},{5,6},{6,5},{7,4},{8,11},{9,10},{10,... | collective-permute-start | bytes 245768 | tf_op jit(solution)/shard_map/ppermute | solution.py:41
  6.5 5.3 %collective-permute-start.5 = (bf16[5,32,256]{2,1,0:T(8,128)(2,1)S(1)}, bf16[5,32,256]{2,1,0:T(8,128)(2,1)S(1)}, u32[]{:S(2)}, u32[]{:S(2)}) collective-permute-start(bf16[5,32,256]{2,1,0:T(8,128)(2,1)S(1)} %collective-permute-done.1.refs_5_), channel_id=1, source_target_pairs={{0,16},{16,0},{1,17},{17,1},{2,18},{18,2},{3,19},{19,3},{4,20},{20... | collective-permute-start | bytes 245768 | tf_op jit(solution)/shard_map/ppermute | solution.py:51
  8.7 4.5 %collective-permute-start.6 = (bf16[5,32,256]{2,1,0:T(8,128)(2,1)S(1)}, bf16[5,32,256]{2,1,0:T(8,128)(2,1)S(1)}, u32[]{:S(2)}, u32[]{:S(2)}) collective-permute-start(bf16[5,32,256]{2,1,0:T(8,128)(2,1)S(1)} %collective-permute-done.refs_6_), channel_id=1, source_target_pairs={{0,16},{16,0},{1,17},{17,1},{2,18},{18,2},{3,19},{19,3},{4,20},{20... | collective-permute-start | bytes 245768 | tf_op jit(solution)/shard_map/ppermute | solution.py:51
  13.5 7.1 %copy-start.1 = (bf16[1024,256]{1,0:T(8,128)(2,1)S(1)}, bf16[1024,256]{1,0:T(8,128)(2,1)}, u32[]{:S(2)}) copy-start(bf16[1024,256]{1,0:T(8,128)(2,1)} %constant.41.clone.refs_1_) | copy-start | bytes 1572868
  13.8 3.9 %collective-permute-start.7 = (bf16[5,14,512]{2,1,0:T(8,128)(2,1)S(1)}, bf16[5,14,512]{2,1,0:T(8,128)(2,1)S(1)}, u32[]{:S(2)}, u32[]{:S(2)}) collective-permute-start(bf16[5,14,512]{2,1,0:T(8,128)(2,1)S(1)} %get-tuple-element.28), channel_id=1, source_target_pairs={{0,4},{4,0},{8,12},{12,8},{1,5},{5,1},{9,13},{13,9},{2,6},{6,2},{1... | collective-permute-start | bytes 215048 | tf_op jit(solution)/shard_map/ppermute | solution.py:42
  16.4 4.1 %collective-permute-start.8 = (bf16[5,14,512]{2,1,0:T(8,128)(2,1)S(1)}, bf16[5,14,512]{2,1,0:T(8,128)(2,1)S(1)}, u32[]{:S(2)}, u32[]{:S(2)}) collective-permute-start(bf16[5,14,512]{2,1,0:T(8,128)(2,1)S(1)} %get-tuple-element.27), channel_id=1, source_target_pairs={{0,12},{4,8},{8,4},{12,0},{1,13},{5,9},{9,5},{13,1},{2,14},{6,10},... | collective-permute-start | bytes 215048 | tf_op jit(solution)/shard_map/ppermute | solution.py:41

commit v5 on v4

--- a/solution.py
+++ b/solution.py
@@ -83,8 +83,8 @@
 
 
 def advance_kernel(chain, corrected, rows, *refs):
-    flags, matrix, x_first, x_second = refs[:4]
-    refs = list(refs[4:])
+    flags, matrix, *came = refs[:6]
+    refs = list(refs[6:])
     even_x = flags[0] == 1
     even_y = flags[1] == 1
     position = flags[2]
@@ -103,21 +103,25 @@
     def lanes(tile):
         return pl.ds(tile * LANES, LANES)
 
-    taken = x_first.shape[1]
-    for field in range(FIELDS):
-        for tile in range(4):
-            one = x_first[field, :, lanes(tile)]
-            two = x_second[field, :, lanes(tile)]
-            edges[0, field, tile, pl.ds(0, taken), :] = jnp.where(even_x, two, one)
-            edges[1, field, tile, pl.ds(0, taken), :] = jnp.where(even_x, one, two)
-    sources, _ = edge_layout(chain, corrected)
+    sources = {}
+    for turn, kinds in enumerate(edge_turns(chain, corrected)):
+        pieces, taken = edge_layout(kinds)
+        sources.update((kind, (turn, parts)) for kind, parts in pieces.items())
+        first, second = came[2 * turn : 2 * turn + 2]
+        for field in range(FIELDS):
+            for tile in range(4):
+                one = first[field, :, lanes(tile)]
+                two = second[field, :, lanes(tile)]
+                edges[turn, 0, field, tile, pl.ds(0, taken), :] = jnp.where(even_x, two, one)
+                edges[turn, 1, field, tile, pl.ds(0, taken), :] = jnp.where(even_x, one, two)
 
     def place(target, index, kind):
-        for distance, count, tiles, row, first_tile in sources[kind]:
+        turn, pieces = sources[kind]
+        for distance, count, tiles, row, first_tile in pieces:
             for tile in range(tiles):
                 start = (4 - tiles) // 2 + tile
-                low = edges[0, index[-1], first_tile + tile, pl.ds(row, count), :]
-                top = edges[1, index[-1], first_tile + tile, pl.ds(row, count), :]
+                low = edges[turn, 0, index[-1], first_tile + tile, pl.ds(row, count), :]
+                top = edges[turn, 1, index[-1], first_tile + tile, pl.ds(row, count), :]
                 target(start)[pl.ds(FIRST - distance - count, count), :] = low
                 target(start)[pl.ds(FIRST + rows + distance, count), :] = top
 
@@ -283,23 +287,33 @@
         pl.when(position > 0)(lambda: advance(chain))
 
 
-def edge_layout(chain, corrected):
+def edge_turns(chain, corrected):
+    state = ((0, 4, True), (4, 2, False))
+    terms = (((0, 2, True), (2, 2, False)), ((0, 2, False),))
+    early = [(("state", 0), state)]
+    late = []
+    for link in range(chain):
+        if link:
+            late.append((("state", link), state))
+        if corrected[link]:
+            late.append((("kept", link, 0), terms[0]))
+            (late if link else early).append((("kept", link, 1), terms[1]))
+    return early, late
+
+
+def edge_layout(kinds):
     sources = {}
-    wide = []
     narrow = []
-    for link in range(chain):
-        wide.append((("state", link), 0, 4))
-        narrow.append((("state", link), 4))
-        if corrected[link]:
-            wide.append((("kept", link, 0), 0, 2))
-            narrow.append((("kept", link, 0), 2))
-            narrow.append((("kept", link, 1), 0))
     row = 0
-    for kind, distance, count in wide:
-        sources.setdefault(kind, []).append((distance, count, 4, row, 0))
-        row += count
-    for place, (kind, distance) in enumerate(narrow):
-        sources.setdefault(kind, []).append((distance, 2, 2, row + 2 * (place // 2), 2 * (place % 2)))
+    for kind, pieces in kinds:
+        for distance, count, wide in pieces:
+            if wide:
+                sources.setdefault(kind, []).append((distance, count, 4, row, 0))
+                row += count
+            else:
+                narrow.append((kind, distance, count))
+    for place, (kind, distance, count) in enumerate(narrow):
+        sources.setdefault(kind, []).append((distance, count, 2, row + 2 * (place // 2), 2 * (place % 2)))
     return sources, row + 2 * ((len(narrow) + 1) // 2)
 
 
@@ -341,16 +355,42 @@
     forwarded = [tuple(from_lower(half, levels, link) for half in own_y) for link in range(1, chain)]
     kept_y, forwarded = lax.optimization_barrier((kept_y, forwarded))
 
-    padded = {}
-    operands = []
+    padded = {("state", 0): padded_y(own_y, sent)}
+    if corrected[0]:
+        padded["kept", 0, 1] = jnp.pad(kept[FIELDS:], ((0, 0), (0, 0), (LANES, LANES)))
+
+    width = columns + 2 * LANES
+
+    def over_x(kinds):
+        pieces, _ = edge_layout(kinds)
+
+        def edge(from_top):
+            grid = {}
+            for kind, parts in pieces.items():
+                for distance, count, tiles, row, first_tile in parts:
+                    start = rows - distance - count if from_top else distance
+                    skip = (4 - tiles) // 2 * LANES
+                    grid[row, first_tile] = padded[kind][:, start : start + count, skip : width - skip]
+            parts = []
+            for row, first_tile in sorted(grid):
+                if first_tile:
+                    continue
+                part = grid[row, 0]
+                if part.shape[2] < width:
+                    part = jnp.concatenate([part, grid.get((row, 2), part)], axis=2)
+                parts.append(part)
+            return jnp.concatenate(parts, axis=1)
+
+        return [half.astype(jnp.float32) for half in neighbours("gx", even_x, edge(False), edge(True))]
+
+    early, late = edge_turns(chain, corrected)
+    came = over_x(early)
+    kept_y, forwarded = lax.optimization_barrier((kept_y, forwarded))
+    operands = [whole, *own_y]
     for link in range(chain):
         if link:
-            link_y = forwarded[link - 1]
-            operands += [centers[link], *link_y]
-        else:
-            link_y = own_y
-            operands += [whole, *own_y]
-        padded["state", link] = padded_y(link_y, centers[link])
+            operands += [centers[link], *forwarded[link - 1]]
+            padded["state", link] = padded_y(forwarded[link - 1], centers[link])
         if corrected[link]:
             if link:
                 link_kept = from_lower(kept, levels, link)
@@ -361,35 +401,16 @@
                 operands += [stored, *link_y]
             link_padded = padded_y(link_y, link_kept)
             padded["kept", link, 0] = link_padded[:FIELDS]
-            padded["kept", link, 1] = link_padded[FIELDS:]
-
-    sources, taken = edge_layout(chain, corrected)
-    width = columns + 2 * LANES
-
-    def edge(from_top):
-        grid = {}
-        for kind, pieces in sources.items():
-            for distance, count, tiles, row, first_tile in pieces:
-                start = rows - distance - count if from_top else distance
-                skip = (4 - tiles) // 2 * LANES
-                grid[row, first_tile] = padded[kind][:, start : start + count, skip : width - skip]
-        parts = []
-        for row, first_tile in sorted(grid):
-            if first_tile:
-                continue
-            part = grid[row, 0]
-            if part.shape[2] < width:
-                part = jnp.concatenate([part, grid.get((row, 2), part)], axis=2)
-            parts.append(part)
-        return jnp.concatenate(parts, axis=1)
-
-    over_x = neighbours("gx", even_x, edge(False), edge(True))
-    operands = [half.astype(jnp.float32) for half in over_x] + operands
+            if link:
+                padded["kept", link, 1] = link_padded[FIELDS:]
+    came += over_x(late)
+    operands = came + operands
     flags = jnp.stack([even_x.astype(jnp.int32), even_y.astype(jnp.int32), position])
     matrix = jnp.asarray(stencil_matrix(), jnp.bfloat16)
     high = rows + WINDOW
     tall = rows + 2 * FIRST
     vmem = pl.BlockSpec(memory_space=pltpu.VMEM)
+    taken = max(edge_layout(kinds)[1] for kinds in (early, late))
     specs = [vmem] * (len(operands) + 1)
     result = pl.pallas_call(
         functools.partial(advance_kernel, chain, corrected, rows),
@@ -404,7 +425,7 @@
             pltpu.VMEM((chain, FIELDS - 1, 6, tall, LANES), jnp.float32),
             pltpu.VMEM((chain, 6, FIELDS * high, LANES), jnp.float32),
             pltpu.VMEM((chain, 4, FIELDS * high, LANES), jnp.float32),
-            pltpu.VMEM((2, FIELDS, 4, -(-taken // 8) * 8, LANES), jnp.float32),
+            pltpu.VMEM((2, 2, FIELDS, 4, -(-taken // 8) * 8, LANES), jnp.float32),
         ],
         compiler_params=pltpu.CompilerParams(vmem_limit_bytes=48 * 1024 * 1024),
     )(flags, matrix, *operands)

time: 25.1 us -> 24.1 us (0.960)
  waiting for transfers between devices: 7.62 us -> 2.92 us
  starting transfers between devices: 10.8 us -> 14.7 us
  local copies, waits for them, and re-layouts: 0.52 us -> 0.07 us
    ppermute x3 -> x4, waiting for transfers between devices: 5.87 us -> 2.9 us  [neighbours(): second = lax.ppermute(inward, axis, far)]
    ppermute x3 -> x4, starting transfers between devices: 4.46 us -> 7 us  [neighbours(): first = lax.ppermute(outward, axis, near)]
    ppermute x3 -> x4, starting transfers between devices: 4.3 us -> 5.7 us  [neighbours(): second = lax.ppermute(inward, axis, far)]
    ppermute x3, waiting for transfers between devices: 1.4 us -> 0.01 us  [from_lower(): return lax.ppermute(block, 'sec', route)]
    concatenate x2 -> x0, local copies, waits for them, and re-layouts: 0.46 us -> none  [edge(): return jnp.concatenate(parts, axis=1)]
    ppermute x3 -> x4, waiting for transfers between devices: 0.35 us -> 0.01 us  [neighbours(): first = lax.ppermute(outward, axis, near)]
  transfers between devices with their start and end apart: 9 -> 11, of which waited for: 5 -> 2; matrix products, arithmetic and copies ran while one was open for 1% -> 2% of each run, Pallas kernels for 0% -> 0%
where the time goes in v5:
time: 24.1 us; the launch traced here: 23.9 us
  starting transfers between devices  14.7 us (61%)
  Pallas kernels  4.47 us (19%)
  waiting for transfers between devices  2.92 us (12%)
  other arithmetic  1.52 us (6%)
    ppermute x4, starting transfers between devices, neighbours(): first = lax.ppermute(outward, axis, near)  7 us
    ppermute x4, starting transfers between devices, neighbours(): second = lax.ppermute(inward, axis, far)  5.7 us
    pallas_call x1, Pallas kernels, per_device(): pl.pallas_call(functools.partial(advance_kernel, chain, corrected, rows),...  4.47 us
    ppermute x4, waiting for transfers between devices, neighbours(): second = lax.ppermute(inward, axis, far)  2.9 us
    ppermute x3, starting transfers between devices, from_lower(): return lax.ppermute(block, 'sec', route)  2.04 us
    convert_element_type x1, other arithmetic, per_device(): sent = block.astype(jnp.bfloat16)  1.07 us
  transfers between devices with their start and end apart: 11, of which 2 were waited for; matrix products, arithmetic and copies ran while one was open for 2% of the time, Pallas kernels for 0%

profile of v5, /device:TPU:3, one launch (start us, length us, event | category | flops | bytes accessed | tf_op | source)
XLA Modules:
  0.0 23.9 jit_solution(11389820257645377761)
XLA Ops:
  0.0 0.0 copy-start
  0.0 1.1 %convert_bitcast_fusion = (bf16[5,32,256]{2,1,0:T(8,128)(2,1)S(1)}, f32[5,32,256]{2,1,0:T(8,128)S(1)}) fusion(f32[1,5,32,256]{3,2,1,0:T(8,128)} %param.3), kind=kLoop, calls=%fused_computation.24 | loop fusion | flops 81920 | bytes 409600 | tf_op jit(solution)/shard_map/convert_element_type | solution.py:340
  1.1 1.4 %collective-permute-start.1 = (bf16[5,32,256]{2,1,0:T(8,128)(2,1)S(1)}, bf16[5,32,256]{2,1,0:T(8,128)(2,1)S(1)}, u32[]{:S(2)}, u32[]{:S(2)}) collective-permute-start(bf16[5,32,256]{2,1,0:T(8,128)(2,1)S(1)} %get-tuple-element.13), channel_id=1, source_target_pairs={{0,1},{1,0},{2,3},{3,2},{4,5},{5,4},{6,7},{7,6},{8,9},{9,8},{10,11... | collective-permute-start | bytes 245768 | tf_op jit(solution)/shard_map/ppermute | solution.py:42
  2.4 0.3 %collective-permute-start.2 = (bf16[5,32,256]{2,1,0:T(8,128)(2,1)S(1)}, bf16[5,32,256]{2,1,0:T(8,128)(2,1)S(1)}, u32[]{:S(2)}, u32[]{:S(2)}) collective-permute-start(bf16[5,32,256]{2,1,0:T(8,128)(2,1)S(1)} %get-tuple-element.13), channel_id=1, source_target_pairs={{0,16},{16,0},{1,17},{17,1},{2,18},{18,2},{3,19},{19,3},{4,20},{20... | collective-permute-start | bytes 245768 | tf_op jit(solution)/shard_map/ppermute | solution.py:51
  2.7 2.2 %collective-permute-start = (bf16[5,32,256]{2,1,0:T(8,128)(2,1)S(1)}, bf16[5,32,256]{2,1,0:T(8,128)(2,1)S(1)}, u32[]{:S(2)}, u32[]{:S(2)}) collective-permute-start(bf16[5,32,256]{2,1,0:T(8,128)(2,1)S(1)} %get-tuple-element.13), channel_id=1, source_target_pairs={{0,3},{1,2},{2,1},{3,0},{4,7},{5,6},{6,5},{7,4},{8,11},{9,10},{10,... | collective-permute-start | bytes 245768 | tf_op jit(solution)/shard_map/ppermute | solution.py:41
  4.9 0.0 copy-done
  4.9 0.1 fusion.5
  5.0 0.5 %collective-permute-start.5 = (bf16[10,32,128]{2,1,0:T(8,128)(2,1)S(1)}, bf16[10,32,128]{2,1,0:T(8,128)(2,1)S(1)}, u32[]{:S(2)}, u32[]{:S(2)}) collective-permute-start(bf16[10,32,128]{2,1,0:T(8,128)(2,1)S(1)} %get-tuple-element.34), channel_id=1, source_target_pairs={{0,1},{1,0},{2,3},{3,2},{4,5},{5,4},{6,7},{7,6},{8,9},{9,8},{10,11... | collective-permute-start | bytes 245768 | tf_op jit(solution)/shard_map/ppermute | solution.py:42
  5.5 0.9 %collective-permute-start.6 = (bf16[10,32,128]{2,1,0:T(8,128)(2,1)S(1)}, bf16[10,32,128]{2,1,0:T(8,128)(2,1)S(1)}, u32[]{:S(2)}, u32[]{:S(2)}) collective-permute-start(bf16[10,32,128]{2,1,0:T(8,128)(2,1)S(1)} %get-tuple-element.33), channel_id=1, source_target_pairs={{0,3},{1,2},{2,1},{3,0},{4,7},{5,6},{6,5},{7,4},{8,11},{9,10},{10,... | collective-permute-start | bytes 245768 | tf_op jit(solution)/shard_map/ppermute | solution.py:41
  6.5 0.0 collective-permute-done.1.refs_7_
  6.5 0.0 collective-permute-done.2.refs_12_
  6.5 1.3 %collective-permute-start.7 = (bf16[5,32,256]{2,1,0:T(8,128)(2,1)S(1)}, bf16[5,32,256]{2,1,0:T(8,128)(2,1)S(1)}, u32[]{:S(2)}, u32[]{:S(2)}) collective-permute-start(bf16[5,32,256]{2,1,0:T(8,128)(2,1)S(1)} %collective-permute-done.1.refs_7_), channel_id=1, source_target_pairs={{0,16},{16,0},{1,17},{17,1},{2,18},{18,2},{3,19},{19,3},{4,20},{20... | collective-permute-start | bytes 245768 | tf_op jit(solution)/shard_map/ppermute | solution.py:51
  7.8 0.8 %collective-permute-done.refs_8_ = bf16[5,32,256]{2,1,0:T(8,128)(2,1)S(1)} collective-permute-done((bf16[5,32,256]{2,1,0:T(8,128)(2,1)S(1)}, bf16[5,32,256]{2,1,0:T(8,128)(2,1)S(1)}, u32[]{:S(2)}, u32[]{:S(2)}) %collective-permute-start) | collective-permute-done | bytes 81952 | tf_op jit(solution)/shard_map/ppermute | solution.py:41
  8.6 0.1 broadcast_select_fusion.6
  8.7 0.5 %collective-permute-start.8 = (bf16[5,32,256]{2,1,0:T(8,128)(2,1)S(1)}, bf16[5,32,256]{2,1,0:T(8,128)(2,1)S(1)}, u32[]{:S(2)}, u32[]{:S(2)}) collective-permute-start(bf16[5,32,256]{2,1,0:T(8,128)(2,1)S(1)} %collective-permute-done.refs_8_), channel_id=1, source_target_pairs={{0,16},{16,0},{1,17},{17,1},{2,18},{18,2},{3,19},{19,3},{4,20},{20... | collective-permute-start | bytes 245768 | tf_op jit(solution)/shard_map/ppermute | solution.py:51
  9.2 2.8 %collective-permute-start.3 = (bf16[5,6,512]{2,1,0:T(8,128)(2,1)S(1)}, bf16[5,6,512]{2,1,0:T(8,128)(2,1)S(1)}, u32[]{:S(2)}, u32[]{:S(2)}) collective-permute-start(bf16[5,6,512]{2,1,0:T(8,128)(2,1)S(1)} %broadcast_select_fusion.7), channel_id=1, source_target_pairs={{0,4},{4,0},{8,12},{12,8},{1,5},{5,1},{9,13},{13,9},{2,6},{6,2},{1... | collective-permute-start | bytes 92168 | tf_op jit(solution)/shard_map/ppermute | solution.py:42
  12.1 0.0 collective-permute-done.5.refs_10_
  12.1 1.4 %collective-permute-start.4 = (bf16[5,6,512]{2,1,0:T(8,128)(2,1)S(1)}, bf16[5,6,512]{2,1,0:T(8,128)(2,1)S(1)}, u32[]{:S(2)}, u32[]{:S(2)}) collective-permute-start(bf16[5,6,512]{2,1,0:T(8,128)(2,1)S(1)} %get-tuple-element.24), channel_id=1, source_target_pairs={{0,12},{4,8},{8,4},{12,0},{1,13},{5,9},{9,5},{13,1},{2,14},{6,10},... | collective-permute-start | bytes 92168 | tf_op jit(solution)/shard_map/ppermute | solution.py:41
  13.5 0.0 collective-permute-done.6.refs_11_
  13.5 0.0 collective-permute-done.7.refs_13_
  13.5 0.0 collective-permute-done.8.refs_14_
  13.5 0.0 copy-start.1
  13.5 0.1 broadcast_select_fusion.4
  13.6 2.3 %collective-permute-start.9 = (bf16[5,8,512]{2,1,0:T(8,128)(2,1)S(1)}, bf16[5,8,512]{2,1,0:T(8,128)(2,1)S(1)}, u32[]{:S(2)}, u32[]{:S(2)}) collective-permute-start(bf16[5,8,512]{2,1,0:T(8,128)(2,1)S(1)} %broadcast_select_fusion.5), channel_id=1, source_target_pairs={{0,4},{4,0},{8,12},{12,8},{1,5},{5,1},{9,13},{13,9},{2,6},{6,2},{1... | collective-permute-start | bytes 122888 | tf_op jit(solution)/shard_map/ppermute | solution.py:42
  16.0 1.2 %collective-permute-start.10 = (bf16[5,8,512]{2,1,0:T(8,128)(2,1)S(1)}, bf16[5,8,512]{2,1,0:T(8,128)(2,1)S(1)}, u32[]{:S(2)}, u32[]{:S(2)}) collective-permute-start(bf16[5,8,512]{2,1,0:T(8,128)(2,1)S(1)} %get-tuple-element.21), channel_id=1, source_target_pairs={{0,12},{4,8},{8,4},{12,0},{1,13},{5,9},{9,5},{13,1},{2,14},{6,10},... | collective-permute-start | bytes 122888 | tf_op jit(solution)/shard_map/ppermute | solution.py:41
  17.2 0.1 pad_add_fusion.refs_0_
  17.3 0.0 collective-permute-done.3
  17.3 0.0 collective-permute-done.4
  17.3 0.0 collective-permute-done.9
  17.3 2.1 %collective-permute-done.10 = bf16[5,8,512]{2,1,0:T(8,128)(2,1)S(1)} collective-permute-done((bf16[5,8,512]{2,1,0:T(8,128)(2,1)S(1)}, bf16[5,8,512]{2,1,0:T(8,128)(2,1)S(1)}, u32[]{:S(2)}, u32[]{:S(2)}) %collective-permute-start.10) | collective-permute-done | bytes 40992 | tf_op jit(solution)/shard_map/ppermute | solution.py:41
  19.4 0.0 copy-done.1
  19.4 4.5 %shard_map.37 = f32[5,32,256]{2,1,0:T(8,128)} custom-call(s32[3]{0:T(128)S(1)} %pad_add_fusion.refs_0_, bf16[1024,256]{1,0:T(8,128)(2,1)S(1)} %copy-done.1, f32[5,6,512]{2,1,0:T(8,128)S(1)} %convert_element_type.29.refs_2_, f32[5,6,512]{2,1,0:T(8,128)S(1)} %convert_element_type.30.refs_3_, f32[5,8,512]{2,1,0:T(8,128)S(1)} %convert_element_type.31.refs_4_, ...), custom_call_target="tpu_custom_call" | custom-call | tf_op jit(solution)/shard_map/pallas_call | solution.py:415
  (15 shorter events, 0.2 us)
Async XLA Ops:
  0.0 4.9 %copy-start = (bf16[1,3,5,32,256]{4,3,2,1,0:T(8,128)(2,1)S(1)}, bf16[1,3,5,32,256]{4,3,2,1,0:T(8,128)(2,1)}, u32[]{:S(2)}) copy-start(bf16[1,3,5,32,256]{4,3,2,1,0:T(8,128)(2,1)} %param.4) | copy-start | bytes 737284
  1.1 5.4 %collective-permute-start.1 = (bf16[5,32,256]{2,1,0:T(8,128)(2,1)S(1)}, bf16[5,32,256]{2,1,0:T(8,128)(2,1)S(1)}, u32[]{:S(2)}, u32[]{:S(2)}) collective-permute-start(bf16[5,32,256]{2,1,0:T(8,128)(2,1)S(1)} %get-tuple-element.13), channel_id=1, source_target_pairs={{0,1},{1,0},{2,3},{3,2},{4,5},{5,4},{6,7},{7,6},{8,9},{9,8},{10,11... | collective-permute-start | bytes 245768 | tf_op jit(solution)/shard_map/ppermute | solution.py:42
  2.4 4.1 %collective-permute-start.2 = (bf16[5,32,256]{2,1,0:T(8,128)(2,1)S(1)}, bf16[5,32,256]{2,1,0:T(8,128)(2,1)S(1)}, u32[]{:S(2)}, u32[]{:S(2)}) collective-permute-start(bf16[5,32,256]{2,1,0:T(8,128)(2,1)S(1)} %get-tuple-element.13), channel_id=1, source_target_pairs={{0,16},{16,0},{1,17},{17,1},{2,18},{18,2},{3,19},{19,3},{4,20},{20... | collective-permute-start | bytes 245768 | tf_op jit(solution)/shard_map/ppermute | solution.py:51
  2.7 5.9 %collective-permute-start = (bf16[5,32,256]{2,1,0:T(8,128)(2,1)S(1)}, bf16[5,32,256]{2,1,0:T(8,128)(2,1)S(1)}, u32[]{:S(2)}, u32[]{:S(2)}) collective-permute-start(bf16[5,32,256]{2,1,0:T(8,128)(2,1)S(1)} %get-tuple-element.13), channel_id=1, source_target_pairs={{0,3},{1,2},{2,1},{3,0},{4,7},{5,6},{6,5},{7,4},{8,11},{9,10},{10,... | collective-permute-start | bytes 245768 | tf_op jit(solution)/shard_map/ppermute | solution.py:41
  5.0 7.0 %collective-permute-start.5 = (bf16[10,32,128]{2,1,0:T(8,128)(2,1)S(1)}, bf16[10,32,128]{2,1,0:T(8,128)(2,1)S(1)}, u32[]{:S(2)}, u32[]{:S(2)}) collective-permute-start(bf16[10,32,128]{2,1,0:T(8,128)(2,1)S(1)} %get-tuple-element.34), channel_id=1, source_target_pairs={{0,1},{1,0},{2,3},{3,2},{4,5},{5,4},{6,7},{7,6},{8,9},{9,8},{10,11... | collective-permute-start | bytes 245768 | tf_op jit(solution)/shard_map/ppermute | solution.py:42
  5.5 8.0 %collective-permute-start.6 = (bf16[10,32,128]{2,1,0:T(8,128)(2,1)S(1)}, bf16[10,32,128]{2,1,0:T(8,128)(2,1)S(1)}, u32[]{:S(2)}, u32[]{:S(2)}) collective-permute-start(bf16[10,32,128]{2,1,0:T(8,128)(2,1)S(1)} %get-tuple-element.33), channel_id=1, source_target_pairs={{0,3},{1,2},{2,1},{3,0},{4,7},{5,6},{6,5},{7,4},{8,11},{9,10},{10,... | collective-permute-start | bytes 245768 | tf_op jit(solution)/shard_map/ppermute | solution.py:41
  6.5 7.0 %collective-permute-start.7 = (bf16[5,32,256]{2,1,0:T(8,128)(2,1)S(1)}, bf16[5,32,256]{2,1,0:T(8,128)(2,1)S(1)}, u32[]{:S(2)}, u32[]{:S(2)}) collective-permute-start(bf16[5,32,256]{2,1,0:T(8,128)(2,1)S(1)} %collective-permute-done.1.refs_7_), channel_id=1, source_target_pairs={{0,16},{16,0},{1,17},{17,1},{2,18},{18,2},{3,19},{19,3},{4,20},{20... | collective-permute-start | bytes 245768 | tf_op jit(solution)/shard_map/ppermute | solution.py:51
  8.7 4.8 %collective-permute-start.8 = (bf16[5,32,256]{2,1,0:T(8,128)(2,1)S(1)}, bf16[5,32,256]{2,1,0:T(8,128)(2,1)S(1)}, u32[]{:S(2)}, u32[]{:S(2)}) collective-permute-start(bf16[5,32,256]{2,1,0:T(8,128)(2,1)S(1)} %collective-permute-done.refs_8_), channel_id=1, source_target_pairs={{0,16},{16,0},{1,17},{17,1},{2,18},{18,2},{3,19},{19,3},{4,20},{20... | collective-permute-start | bytes 245768 | tf_op jit(solution)/shard_map/ppermute | solution.py:51
  9.2 8.0 %collective-permute-start.3 = (bf16[5,6,512]{2,1,0:T(8,128)(2,1)S(1)}, bf16[5,6,512]{2,1,0:T(8,128)(2,1)S(1)}, u32[]{:S(2)}, u32[]{:S(2)}) collective-permute-start(bf16[5,6,512]{2,1,0:T(8,128)(2,1)S(1)} %broadcast_select_fusion.7), channel_id=1, source_target_pairs={{0,4},{4,0},{8,12},{12,8},{1,5},{5,1},{9,13},{13,9},{2,6},{6,2},{1... | collective-permute-start | bytes 92168 | tf_op jit(solution)/shard_map/ppermute | solution.py:42
  12.1 5.2 %collective-permute-start.4 = (bf16[5,6,512]{2,1,0:T(8,128)(2,1)S(1)}, bf16[5,6,512]{2,1,0:T(8,128)(2,1)S(1)}, u32[]{:S(2)}, u32[]{:S(2)}) collective-permute-start(bf16[5,6,512]{2,1,0:T(8,128)(2,1)S(1)} %get-tuple-element.24), channel_id=1, source_target_pairs={{0,12},{4,8},{8,4},{12,0},{1,13},{5,9},{9,5},{13,1},{2,14},{6,10},... | collective-permute-start | bytes 92168 | tf_op jit(solution)/shard_map/ppermute | solution.py:41
  13.5 5.9 %copy-start.1 = (bf16[1024,256]{1,0:T(8,128)(2,1)S(1)}, bf16[1024,256]{1,0:T(8,128)(2,1)}, u32[]{:S(2)}) copy-start(bf16[1024,256]{1,0:T(8,128)(2,1)} %constant.41.clone.refs_1_) | copy-start | bytes 1572868
  13.6 3.7 %collective-permute-start.9 = (bf16[5,8,512]{2,1,0:T(8,128)(2,1)S(1)}, bf16[5,8,512]{2,1,0:T(8,128)(2,1)S(1)}, u32[]{:S(2)}, u32[]{:S(2)}) collective-permute-start(bf16[5,8,512]{2,1,0:T(8,128)(2,1)S(1)} %broadcast_select_fusion.5), channel_id=1, source_target_pairs={{0,4},{4,0},{8,12},{12,8},{1,5},{5,1},{9,13},{13,9},{2,6},{6,2},{1... | collective-permute-start | bytes 122888 | tf_op jit(solution)/shard_map/ppermute | solution.py:42
  16.0 3.4 %collective-permute-start.10 = (bf16[5,8,512]{2,1,0:T(8,128)(2,1)S(1)}, bf16[5,8,512]{2,1,0:T(8,128)(2,1)S(1)}, u32[]{:S(2)}, u32[]{:S(2)}) collective-permute-start(bf16[5,8,512]{2,1,0:T(8,128)(2,1)S(1)} %get-tuple-element.21), channel_id=1, source_target_pairs={{0,12},{4,8},{8,4},{12,0},{1,13},{5,9},{9,5},{13,1},{2,14},{6,10},... | collective-permute-start | bytes 122888 | tf_op jit(solution)/shard_map/ppermute | solution.py:41

commit v6 on v5

v6 whole, which is shorter than its diff:
```python
import functools

import jax
import jax.numpy as jnp
import numpy as np
from jax import lax
from jax.experimental import pallas as pl
from jax.experimental.pallas import tpu as pltpu
from jax.sharding import PartitionSpec as P

NZ = 32
TICKS = 3


TIME_STEP = 0.04
DYNAMIC_FRICTION = 0.4
CONDUCTIVITY = 0.5
GAMMA_LESS = 0.4
QUAD_WEIGHTS = (1.0 / 24.0, -5.0 / 24.0, 19.0 / 24.0, 9.0 / 24.0)

LANES = 128
FIRST = 12
START = 8
WINDOW = 2 * (FIRST - START)
FIELDS = 5


def neighbours(axis, even, low_edge, high_edge):
    count = lax.axis_size(axis)
    if count % 2:
        from_next = lax.ppermute(low_edge, axis, [(i, (i - 1) % count) for i in range(count)])
        from_last = lax.ppermute(high_edge, axis, [(i, (i + 1) % count) for i in range(count)])
        return from_next, from_last
    if low_edge is high_edge:
        outward = inward = low_edge
    else:
        outward = jnp.where(even, high_edge, low_edge)
        inward = jnp.where(even, low_edge, high_edge)
    far = [(i, (i + 1) % count if i % 2 else (i - 1) % count) for i in range(count)]
    near = [(i, i + 1 if i % 2 == 0 else i - 1) for i in range(count)]
    second = lax.ppermute(inward, axis, far)
    first = lax.ppermute(outward, axis, near)
    return first, second


def from_lower(block, levels, distance):
    count = lax.axis_size("sec")
    route = []
    for start in range(0, count, levels):
        route += [(start + i, start + (i + distance) % levels) for i in range(levels)]
    return lax.ppermute(block, "sec", route)


def stencil_matrix():
    per_tile = LANES // NZ
    wide = 2 * LANES
    half = LANES // 2
    d_y = np.zeros((4 * LANES, wide), np.float32)
    d_z = np.zeros((wide, wide), np.float32)
    sweep = np.zeros((4 * LANES, wide), np.float32)
    for y in range(2 * per_tile):
        for z in range(NZ):
            column = y * NZ + z
            here = (y + per_tile) * NZ + z
            d_y[here + NZ, column] -= 0.5
            d_y[here - NZ, column] += 0.5
            d_z[y * NZ + (z + 1) % NZ, column] -= 0.5
            d_z[y * NZ + (z - 1) % NZ, column] += 0.5
            sweep[here, column] -= 1.0
            sweep[here + 2 * NZ, column] += 0.25
            sweep[here - 2 * NZ, column] += 0.25
            base = (y + per_tile) * NZ
            sweep[base + (z + 2) % NZ, column] += 0.25
            sweep[base + (z - 2) % NZ, column] += 0.25

    def inner(matrix):
        return matrix[LANES : 3 * LANES]

    def outer(matrix):
        return np.concatenate([matrix[3 * LANES : 3 * LANES + half], matrix[half:LANES]])

    return np.concatenate([inner(d_y), d_z, inner(sweep), outer(d_y), outer(sweep)], axis=0)


def lanes(tile):
    return pl.ds(tile * LANES, LANES)


def scratch_of_level(rows):
    high, tall = rows + WINDOW, rows + 2 * FIRST
    return [
        pltpu.VMEM((FIELDS, 6, tall, LANES), jnp.float32),
        pltpu.VMEM((FIELDS, 4, tall, LANES), jnp.float32),
        pltpu.VMEM((FIELDS - 1, 6, tall, LANES), jnp.float32),
        pltpu.VMEM((6, FIELDS * high, LANES), jnp.float32),
        pltpu.VMEM((4, FIELDS * high, LANES), jnp.float32),
    ]


def unpack_edges(edges, first, second, even_x):
    count = first.shape[1]
    for field in range(FIELDS):
        for tile in range(4):
            one = first[field, :, lanes(tile)]
            two = second[field, :, lanes(tile)]
            edges[0, field, tile, pl.ds(0, count), :] = jnp.where(even_x, two, one)
            edges[1, field, tile, pl.ds(0, count), :] = jnp.where(even_x, one, two)


def place_edges(target, edges, pieces, field, rows):
    for distance, count, tiles, row, first_tile in pieces:
        for tile in range(tiles):
            start = (4 - tiles) // 2 + tile
            came = field, first_tile + tile, pl.ds(row, count)
            target(start)[pl.ds(FIRST - distance - count, count), :] = edges[(0, *came)]
            target(start)[pl.ds(FIRST + rows + distance, count), :] = edges[(1, *came)]


class Level:
    def __init__(self, rows, even_x, even_y, matrix, scratch):
        self.rows, self.even_x, self.even_y, self.matrix = rows, even_x, even_y, matrix
        self.state, self.flow_x, self.slow, self.flow_y, self.flow_z = scratch
        self.high = rows + WINDOW
        self.window = pl.ds(START, self.high)

    def ordered(self, even, first, second):
        return jnp.where(even, second, first), jnp.where(even, first, second)

    def assemble(self, center, y_first, y_second, edges, pieces):
        rows = self.rows
        for field in range(FIELDS):
            rest = jnp.full((FIRST, LANES), (1.0, 0.0, 0.0, 0.0, 2.5)[field], jnp.float32)
            for tile in range(6):
                target = self.state.at[field, tile]
                if tile in (2, 3):
                    middle = center[field, :, lanes(tile - 2)].astype(jnp.float32)
                else:
                    one = y_first[field, :, lanes(tile % 2)].astype(jnp.float32)
                    two = y_second[field, :, lanes(tile % 2)].astype(jnp.float32)
                    middle = self.ordered(self.even_y, one, two)[tile // 4]
                target[pl.ds(FIRST, rows), :] = middle
                target[pl.ds(0, FIRST), :] = rest
                target[pl.ds(FIRST + rows, FIRST), :] = rest
            place_edges(lambda tile: self.state.at[field, tile + 1], edges, pieces, field, rows)

    def assemble_terms(self, terms, stored, y_first, y_second, edges, pieces):
        rows = self.rows
        none = jnp.zeros((FIRST, LANES), jnp.float32)
        for field in range(FIELDS):
            for tile in (1, 2):
                old = [stored[age, field, :, lanes(tile - 1)].astype(jnp.float32) for age in range(3)]
                for tick, term in enumerate(kept_terms(old)):
                    terms[tick, field, tile, pl.ds(FIRST, rows), :] = term
            for tick in range(2):
                one = y_first[tick * FIELDS + field].astype(jnp.float32)
                two = y_second[tick * FIELDS + field].astype(jnp.float32)
                low, top = self.ordered(self.even_y, one, two)
                terms[tick, field, 0, pl.ds(FIRST, rows), :] = low
                terms[tick, field, 3, pl.ds(FIRST, rows), :] = top
                for tile in range(4):
                    terms[tick, field, tile, pl.ds(0, FIRST), :] = none
                    terms[tick, field, tile, pl.ds(FIRST + rows, FIRST), :] = none
                place_edges(lambda tile: terms.at[tick, field, tile], edges[tick], pieces[tick], field, rows)

    def pointwise(self, tile, start, count, only_x):
        place = pl.ds(start, count)
        density, mom_x, mom_y, mom_z, energy = [self.state[field, tile, place, :] for field in range(FIELDS)]
        inverse = 1.0 / density
        vel_x = mom_x * inverse
        vel_y = mom_y * inverse
        vel_z = mom_z * inverse
        kinetic = 0.5 * (vel_x * vel_x + vel_y * vel_y + vel_z * vel_z)
        pressure = GAMMA_LESS * (energy - density * kinetic)
        enthalpy = energy + pressure
        heat = DYNAMIC_FRICTION * kinetic + CONDUCTIVITY * (pressure * inverse)
        xy = mom_x * vel_y
        xz = mom_x * vel_z
        yz = mom_y * vel_z
        along_x = (mom_x, mom_x * vel_x + pressure, xy, xz, enthalpy * vel_x)
        along_y = (mom_y, xy, mom_y * vel_y + pressure, yz, enthalpy * vel_y)
        along_z = (mom_z, xz, yz, mom_z * vel_z + pressure, enthalpy * vel_z)
        spread = (
            DYNAMIC_FRICTION * vel_x,
            DYNAMIC_FRICTION * vel_y,
            DYNAMIC_FRICTION * vel_z,
            heat,
        )
        for field in range(FIELDS):
            if 1 <= tile <= 4:
                self.flow_x[field, tile - 1, place, :] = along_x[field]
            if field:
                self.slow[field - 1, tile, place, :] = spread[field - 1]
            if not only_x:
                self.flow_y[tile, pl.ds(field * self.high, self.high), :] = along_y[field]
                if 1 <= tile <= 4:
                    self.flow_z[tile - 1, pl.ds(field * self.high, self.high), :] = along_z[field]

    def spreading(self, tile):
        none = jnp.zeros((self.high, LANES), jnp.float32)
        return jnp.concatenate([none] + [self.slow[kind, tile, self.window, :] for kind in range(FIELDS - 1)])

    def products(self, tick):
        for tile in range(6) if tick == 0 else range(1, 5):
            self.pointwise(tile, START, self.high, False)
            if tick == 0 and 1 <= tile <= 4:
                self.pointwise(tile, 0, START, True)
                self.pointwise(tile, START + self.high, START, True)
        from_above = lax.broadcasted_iota(jnp.int32, (FIELDS * self.high, LANES), 1) < LANES // 2
        flow_y, flow_z, spreading = self.flow_y, self.flow_z, self.spreading
        found = {}
        for low, top in ((2, 3),) if tick == TICKS - 1 else ((1, 2), (3, 4)):
            parts = [
                flow_y[low],
                flow_y[top],
                flow_z[low - 1],
                flow_z[top - 1],
                spreading(low),
                spreading(top),
                jnp.where(from_above, flow_y[top + 1], flow_y[low - 1]),
                jnp.where(from_above, spreading(top + 1), spreading(low - 1)),
            ]
            left = jnp.concatenate([part.astype(jnp.bfloat16) for part in parts], axis=1)
            found[low, top] = jnp.dot(left, self.matrix[...], preferred_element_type=jnp.float32)
        return found

    def along_x(self, field, tile):
        def shifted(ref, *index, step):
            return ref[(*index, pl.ds(START + step, self.high))]

        total = 0.5 * (shifted(self.flow_x, field, tile - 1, step=-1) - shifted(self.flow_x, field, tile - 1, step=1))
        if field:
            kind = field - 1
            around = shifted(self.slow, kind, tile, step=2) + shifted(self.slow, kind, tile, step=-2)
            total = total + (0.25 * around - 0.5 * shifted(self.slow, kind, tile, step=0))
        return total

    def rates(self, found):
        for group, product in found.items():
            for field in range(FIELDS):
                for side, tile in enumerate(group):
                    start = field * self.high
                    part = product[start : start + self.high, side * LANES : (side + 1) * LANES]
                    yield field, tile, part + self.along_x(field, tile)


def edge_turns(chain, corrected):
    state = ((0, 4, True), (4, 2, False))
    terms = (((0, 2, True), (2, 2, False)), ((0, 2, False),))
    early = [(("state", 0), state)]
    late = []
    for link in range(chain):
        if link:
            late.append((("state", link), state))
        if corrected[link]:
            late.append((("kept", link, 0), terms[0]))
            (late if link else early).append((("kept", link, 1), terms[1]))
    return early, late


def edge_layout(kinds):
    sources = {}
    narrow = []
    row = 0
    for kind, pieces in kinds:
        for distance, count, wide in pieces:
            if wide:
                sources.setdefault(kind, []).append((distance, count, 4, row, 0))
                row += count
            else:
                narrow.append((kind, distance, count))
    for place, (kind, distance, count) in enumerate(narrow):
        sources.setdefault(kind, []).append((distance, count, 2, row + 2 * (place // 2), 2 * (place % 2)))
    return sources, row + 2 * ((len(narrow) + 1) // 2)


def first_kernel(chain, corrected, rows, *refs):
    flags, matrix, x_first, x_second, center, y_first, y_second, out, edges, *scratch = refs
    even_x = flags[0] == 1
    pieces, _ = edge_layout(edge_turns(chain, corrected)[0])
    unpack_edges(edges, x_first, x_second, even_x)
    level = Level(rows, even_x, flags[1] == 1, matrix, scratch)
    level.assemble(center, y_first, y_second, edges, pieces["state", 0])
    for field, tile, rate in level.rates(level.products(0)):
        out[field, tile - 1] = level.state[field, tile, level.window, :] + TIME_STEP * rate


def advance_kernel(chain, corrected, rows, *refs):
    flags, matrix, begun, *refs = refs
    came, refs = refs[:4], refs[4:]
    inputs = []
    for link in range(chain):
        state, refs = (refs[:3], refs[3:]) if link else (None, refs)
        stored, refs = (refs[:3], refs[3:]) if corrected[link] else (None, refs)
        inputs.append((state, stored))
    out, fresh, terms, edges, *refs = refs
    even_x = flags[0] == 1
    position = flags[2]
    levels = [
        Level(rows, even_x, flags[1] == 1, matrix, refs[5 * link : 5 * link + 5]) for link in range(chain)
    ]
    window = levels[0].window
    layout = {}
    for turn, kinds in enumerate(edge_turns(chain, corrected)):
        pieces, _ = edge_layout(kinds)
        layout.update((kind, (edges.at[turn], parts)) for kind, parts in pieces.items())

    def correction(link, tick, field, tile):
        total = terms[link, tick, field, tile - 1, window, :] + QUAD_WEIGHTS[3] * fresh[link, tick, field, tile - 1]
        for age in range(tick):
            weight = QUAD_WEIGHTS[3 - tick + age] - (1.0 if age == tick - 1 else 0.0)
            total = total + weight * fresh[link, age, field, tile - 1]
        return jnp.where(position > link, total, 0.0) if link else total

    def advance(links):
        def begin(link):
            state, stored = inputs[link]
            if state is not None:
                levels[link].assemble(*state, *layout["state", link])

        def begin_terms(link):
            if corrected[link]:
                places = [layout["kept", link, tick] for tick in range(2)]
                levels[link].assemble_terms(terms.at[link], *inputs[link][1], *zip(*places))

        def update(link, tick, found):
            level = levels[link]
            fix = corrected[link] and links > 1
            if link == 0 and tick == 0:
                for field in range(FIELDS):
                    for tile in range(1, 5):
                        state = begun[field, tile - 1]
                        if fix:
                            state = state + TIME_STEP * correction(0, 0, field, tile)
                        level.state[field, tile, window, :] = state
                return
            for field, tile, rate in level.rates(found):
                if link:
                    fresh[link - 1, tick, field, tile - 1] = rate.astype(jnp.bfloat16).astype(jnp.float32)
                if link + tick >= TICKS:
                    continue
                step = rate + correction(link, tick, field, tile) if fix else rate
                level.state[field, tile, window, :] = level.state[field, tile, window, :] + TIME_STEP * step
                if tick == TICKS - 1:
                    out[field, :, lanes(tile - 2)] = level.state[field, tile, pl.ds(FIRST, rows), :]

        waiting = {}

        def finish(link, tick):
            if (link, tick) in waiting:
                finish(link + 1, tick)
                update(link, tick, waiting.pop((link, tick)))

        if links > 1:
            for turn in range(2):
                unpack_edges(edges.at[turn], *came[2 * turn : 2 * turn + 2], even_x)
        for tick in range(TICKS):
            for link in reversed(range(min(links, TICKS - tick + 1))):
                if tick == 0:
                    begin(link)
                finish(link, tick - 1)
                waiting[link, tick] = levels[link].products(tick) if link or tick else None
                if tick == 0 and links > 1:
                    begin_terms(link)
        for link, tick in sorted(waiting, reverse=True):
            finish(link, tick)

    if chain == 1:
        advance(1)
    else:
        pl.when(position == 0)(lambda: advance(1))
        pl.when(position > 0)(lambda: advance(chain))


def kept_terms(old):
    first, second, third, _ = QUAD_WEIGHTS
    return (
        first * old[0] + second * old[1] + (third - 1.0) * old[2],
        first * old[1] + second * old[2],
        first * old[2],
    )


def per_device(fields, stored_rates):
    levels = min(4, lax.axis_size("sec"))
    position = lax.axis_index("sec") % levels
    even_x = lax.axis_index("gx") % 2 == 0 if lax.axis_size("gx") % 2 == 0 else jnp.bool_(True)
    even_y = lax.axis_index("gy") % 2 == 0 if lax.axis_size("gy") % 2 == 0 else jnp.bool_(True)
    block = fields[0]
    stored = stored_rates[0]
    rows, columns = block.shape[1:]
    chain = min(levels, TICKS + 1)
    corrected = [link < levels - 1 and link < TICKS for link in range(chain)]
    whole = lax.reduce_precision(block, 8, 22)
    sent = block.astype(jnp.bfloat16)
    whole, sent = lax.optimization_barrier((whole, sent))

    def padded_y(pair, center):
        first, second = pair
        low, top = jnp.where(even_y, second, first), jnp.where(even_y, first, second)
        return jnp.concatenate([low[:, :, -LANES:], center, top[:, :, :LANES]], axis=2)

    own_y = neighbours("gy", even_y, sent, sent)
    centers = [sent] + [from_lower(sent, levels, link) for link in range(1, chain)]
    kept = jnp.concatenate(kept_terms(stored.astype(jnp.float32))[:2], axis=0).astype(jnp.bfloat16)
    kept_y = neighbours("gy", even_y, kept[:, :, :LANES], kept[:, :, -LANES:])
    if chain > 1:
        first, centers = lax.optimization_barrier((own_y[0], centers))
        own_y = first, own_y[1]
    forwarded = [tuple(from_lower(half, levels, link) for half in own_y) for link in range(1, chain)]
    kept_y, forwarded = lax.optimization_barrier((kept_y, forwarded))

    padded = {("state", 0): padded_y(own_y, sent)}
    if corrected[0]:
        padded["kept", 0, 1] = jnp.pad(kept[FIELDS:], ((0, 0), (0, 0), (LANES, LANES)))

    width = columns + 2 * LANES

    def over_x(kinds):
        pieces, _ = edge_layout(kinds)

        def edge(from_top):
            grid = {}
            for kind, parts in pieces.items():
                for distance, count, tiles, row, first_tile in parts:
                    start = rows - distance - count if from_top else distance
                    skip = (4 - tiles) // 2 * LANES
                    grid[row, first_tile] = padded[kind][:, start : start + count, skip : width - skip]
            parts = []
            for row, first_tile in sorted(grid):
                if first_tile:
                    continue
                part = grid[row, 0]
                if part.shape[2] < width:
                    part = jnp.concatenate([part, grid.get((row, 2), part)], axis=2)
                parts.append(part)
            return jnp.concatenate(parts, axis=1)

        return [half.astype(jnp.float32) for half in neighbours("gx", even_x, edge(False), edge(True))]

    early, late = edge_turns(chain, corrected)
    came = over_x(early)
    kept_y, forwarded = lax.optimization_barrier((kept_y, forwarded))
    operands = []
    for link in range(chain):
        if link:
            operands += [centers[link], *forwarded[link - 1]]
            padded["state", link] = padded_y(forwarded[link - 1], centers[link])
        if corrected[link]:
            if link:
                link_kept = from_lower(kept, levels, link)
                link_y = tuple(from_lower(half, levels, link) for half in kept_y)
                operands += [from_lower(stored, levels, link), *link_y]
            else:
                link_kept, link_y = kept, kept_y
                operands += [stored, *link_y]
            link_padded = padded_y(link_y, link_kept)
            padded["kept", link, 0] = link_padded[:FIELDS]
            if link:
                padded["kept", link, 1] = link_padded[FIELDS:]
    came += over_x(late)
    flags = jnp.stack([even_x.astype(jnp.int32), even_y.astype(jnp.int32), position])
    matrix = jnp.asarray(stencil_matrix(), jnp.bfloat16)
    high, tall = rows + WINDOW, rows + 2 * FIRST
    smem = pl.BlockSpec(memory_space=pltpu.SMEM)
    vmem = pl.BlockSpec(memory_space=pltpu.VMEM)
    params = pltpu.CompilerParams(vmem_limit_bytes=48 * 1024 * 1024)
    taken = max(edge_layout(kinds)[1] for kinds in (early, late))
    edges = 2, FIELDS, 4, -(-taken // 8) * 8, LANES
    begun = pl.pallas_call(
        functools.partial(first_kernel, chain, corrected, rows),
        out_shape=jax.ShapeDtypeStruct((FIELDS, 4, high, LANES), jnp.float32),
        in_specs=[smem] + [vmem] * 6,
        out_specs=vmem,
        scratch_shapes=[pltpu.VMEM(edges, jnp.float32), *scratch_of_level(rows)],
        compiler_params=params,
        name="own_first_tick",
    )(flags, matrix, *came[:2], whole, *own_y)
    operands = [begun, *came, *operands]
    result = pl.pallas_call(
        functools.partial(advance_kernel, chain, corrected, rows),
        out_shape=jax.ShapeDtypeStruct((FIELDS, rows, columns), jnp.float32),
        in_specs=[smem] + [vmem] * (len(operands) + 1),
        out_specs=vmem,
        scratch_shapes=[
            pltpu.VMEM((chain, TICKS, FIELDS, 4, high, LANES), jnp.float32),
            pltpu.VMEM((chain, TICKS, FIELDS, 4, tall, LANES), jnp.float32),
            pltpu.VMEM((2, *edges), jnp.float32),
            *(scratch_of_level(rows) * chain),
        ],
        compiler_params=params,
        name="advance",
    )(flags, matrix, *operands)
    return result[None]


def solution(mesh):
    return jax.shard_map(
        per_device,
        mesh=mesh,
        in_specs=(P("sec", None, "gx", "gy"), P("sec", None, None, "gx", "gy")),
        out_specs=P("sec", None, "gx", "gy"),
        check_vma=False,
    )
```

time: 24.1 us -> 23.3 us (0.967)
  waiting for transfers between devices: 2.92 us -> 1.72 us
  Pallas kernels: 4.47 us -> 4.9 us
    ppermute x4, waiting for transfers between devices: 2.9 us -> 1.7 us  [neighbours(): second = lax.ppermute(inward, axis, far)]
    pallas_call x0 -> x1, Pallas kernels: none -> 1.18 us  [per_device(): pl.pallas_call(functools.partial(first_kernel, chain, corrected, rows), o...]
    pallas_call x1, Pallas kernels: 4.47 us -> 3.71 us  [per_device(): pl.pallas_call(functools.partial(advance_kernel, chain, corrected, rows),...]
  transfers between devices with their start and end apart: 11 -> 11, of which waited for: 2 -> 2; matrix products, arithmetic and copies ran while one was open for 2% -> 2% of each run, Pallas kernels for 0% -> 5%
where the time goes in v6:
time: 23.3 us; the launch traced here: 23.1 us
  starting transfers between devices  14.7 us (63%)
  Pallas kernels  4.9 us (21%)
  waiting for transfers between devices  1.72 us (7%)
  other arithmetic  1.52 us (7%)
    ppermute x4, starting transfers between devices, neighbours(): first = lax.ppermute(outward, axis, near)  7 us
    ppermute x4, starting transfers between devices, neighbours(): second = lax.ppermute(inward, axis, far)  5.7 us
    pallas_call x1, Pallas kernels, per_device(): pl.pallas_call(functools.partial(advance_kernel, chain, corrected, rows),...  3.71 us
    ppermute x3, starting transfers between devices, from_lower(): return lax.ppermute(block, 'sec', route)  2.04 us
    ppermute x4, waiting for transfers between devices, neighbours(): second = lax.ppermute(inward, axis, far)  1.7 us
    pallas_call x1, Pallas kernels, per_device(): pl.pallas_call(functools.partial(first_kernel, chain, corrected, rows), o...  1.18 us
    convert_element_type x1, other arithmetic, per_device(): sent = block.astype(jnp.bfloat16)  1.07 us
  transfers between devices with their start and end apart: 11, of which 2 were waited for; matrix products, arithmetic and copies ran while one was open for 2% of the time, Pallas kernels for 5%

profile of v6, /device:TPU:3, one launch (start us, length us, event | category | flops | bytes accessed | tf_op | source)
XLA Modules:
  0.0 23.1 jit_solution(17259643929115000768)
XLA Ops:
  0.0 0.0 copy-start.1
  0.0 1.1 %convert_bitcast_fusion = (bf16[5,32,256]{2,1,0:T(8,128)(2,1)S(1)}, f32[5,32,256]{2,1,0:T(8,128)S(1)}) fusion(f32[1,5,32,256]{3,2,1,0:T(8,128)} %param.3), kind=kLoop, calls=%fused_computation.24 | loop fusion | flops 81920 | bytes 409600 | tf_op jit(solution)/shard_map/convert_element_type | solution.py:394
  1.1 1.4 %collective-permute-start.1 = (bf16[5,32,256]{2,1,0:T(8,128)(2,1)S(1)}, bf16[5,32,256]{2,1,0:T(8,128)(2,1)S(1)}, u32[]{:S(2)}, u32[]{:S(2)}) collective-permute-start(bf16[5,32,256]{2,1,0:T(8,128)(2,1)S(1)} %get-tuple-element.13), channel_id=1, source_target_pairs={{0,1},{1,0},{2,3},{3,2},{4,5},{5,4},{6,7},{7,6},{8,9},{9,8},{10,11... | collective-permute-start | bytes 245768 | tf_op jit(solution)/shard_map/ppermute | solution.py:42
  2.4 0.3 %collective-permute-start.2 = (bf16[5,32,256]{2,1,0:T(8,128)(2,1)S(1)}, bf16[5,32,256]{2,1,0:T(8,128)(2,1)S(1)}, u32[]{:S(2)}, u32[]{:S(2)}) collective-permute-start(bf16[5,32,256]{2,1,0:T(8,128)(2,1)S(1)} %get-tuple-element.13), channel_id=1, source_target_pairs={{0,16},{16,0},{1,17},{17,1},{2,18},{18,2},{3,19},{19,3},{4,20},{20... | collective-permute-start | bytes 245768 | tf_op jit(solution)/shard_map/ppermute | solution.py:51
  2.7 2.2 %collective-permute-start = (bf16[5,32,256]{2,1,0:T(8,128)(2,1)S(1)}, bf16[5,32,256]{2,1,0:T(8,128)(2,1)S(1)}, u32[]{:S(2)}, u32[]{:S(2)}) collective-permute-start(bf16[5,32,256]{2,1,0:T(8,128)(2,1)S(1)} %get-tuple-element.13), channel_id=1, source_target_pairs={{0,3},{1,2},{2,1},{3,0},{4,7},{5,6},{6,5},{7,4},{8,11},{9,10},{10,... | collective-permute-start | bytes 245768 | tf_op jit(solution)/shard_map/ppermute | solution.py:41
  4.9 0.0 copy-done.1
  4.9 0.1 fusion.5
  5.0 0.5 %collective-permute-start.5 = (bf16[10,32,128]{2,1,0:T(8,128)(2,1)S(1)}, bf16[10,32,128]{2,1,0:T(8,128)(2,1)S(1)}, u32[]{:S(2)}, u32[]{:S(2)}) collective-permute-start(bf16[10,32,128]{2,1,0:T(8,128)(2,1)S(1)} %get-tuple-element.34), channel_id=1, source_target_pairs={{0,1},{1,0},{2,3},{3,2},{4,5},{5,4},{6,7},{7,6},{8,9},{9,8},{10,11... | collective-permute-start | bytes 245768 | tf_op jit(solution)/shard_map/ppermute | solution.py:42
  5.5 0.9 %collective-permute-start.6 = (bf16[10,32,128]{2,1,0:T(8,128)(2,1)S(1)}, bf16[10,32,128]{2,1,0:T(8,128)(2,1)S(1)}, u32[]{:S(2)}, u32[]{:S(2)}) collective-permute-start(bf16[10,32,128]{2,1,0:T(8,128)(2,1)S(1)} %get-tuple-element.33), channel_id=1, source_target_pairs={{0,3},{1,2},{2,1},{3,0},{4,7},{5,6},{6,5},{7,4},{8,11},{9,10},{10,... | collective-permute-start | bytes 245768 | tf_op jit(solution)/shard_map/ppermute | solution.py:41
  6.5 0.0 collective-permute-done.1.refs_5_
  6.5 0.0 collective-permute-done.2.refs_10_
  6.5 1.3 %collective-permute-start.7 = (bf16[5,32,256]{2,1,0:T(8,128)(2,1)S(1)}, bf16[5,32,256]{2,1,0:T(8,128)(2,1)S(1)}, u32[]{:S(2)}, u32[]{:S(2)}) collective-permute-start(bf16[5,32,256]{2,1,0:T(8,128)(2,1)S(1)} %collective-permute-done.1.refs_5_), channel_id=1, source_target_pairs={{0,16},{16,0},{1,17},{17,1},{2,18},{18,2},{3,19},{19,3},{4,20},{20... | collective-permute-start | bytes 245768 | tf_op jit(solution)/shard_map/ppermute | solution.py:51
  7.8 0.8 %collective-permute-done.refs_6_ = bf16[5,32,256]{2,1,0:T(8,128)(2,1)S(1)} collective-permute-done((bf16[5,32,256]{2,1,0:T(8,128)(2,1)S(1)}, bf16[5,32,256]{2,1,0:T(8,128)(2,1)S(1)}, u32[]{:S(2)}, u32[]{:S(2)}) %collective-permute-start) | collective-permute-done | bytes 81952 | tf_op jit(solution)/shard_map/ppermute | solution.py:41
  8.6 0.1 broadcast_select_fusion.6
  8.7 0.5 %collective-permute-start.8 = (bf16[5,32,256]{2,1,0:T(8,128)(2,1)S(1)}, bf16[5,32,256]{2,1,0:T(8,128)(2,1)S(1)}, u32[]{:S(2)}, u32[]{:S(2)}) collective-permute-start(bf16[5,32,256]{2,1,0:T(8,128)(2,1)S(1)} %collective-permute-done.refs_6_), channel_id=1, source_target_pairs={{0,16},{16,0},{1,17},{17,1},{2,18},{18,2},{3,19},{19,3},{4,20},{20... | collective-permute-start | bytes 245768 | tf_op jit(solution)/shard_map/ppermute | solution.py:51
  9.2 2.8 %collective-permute-start.3 = (bf16[5,6,512]{2,1,0:T(8,128)(2,1)S(1)}, bf16[5,6,512]{2,1,0:T(8,128)(2,1)S(1)}, u32[]{:S(2)}, u32[]{:S(2)}) collective-permute-start(bf16[5,6,512]{2,1,0:T(8,128)(2,1)S(1)} %broadcast_select_fusion.7), channel_id=1, source_target_pairs={{0,4},{4,0},{8,12},{12,8},{1,5},{5,1},{9,13},{13,9},{2,6},{6,2},{1... | collective-permute-start | bytes 92168 | tf_op jit(solution)/shard_map/ppermute | solution.py:42
  12.1 0.0 collective-permute-done.5.refs_8_
  12.1 1.4 %collective-permute-start.4 = (bf16[5,6,512]{2,1,0:T(8,128)(2,1)S(1)}, bf16[5,6,512]{2,1,0:T(8,128)(2,1)S(1)}, u32[]{:S(2)}, u32[]{:S(2)}) collective-permute-start(bf16[5,6,512]{2,1,0:T(8,128)(2,1)S(1)} %get-tuple-element.24), channel_id=1, source_target_pairs={{0,12},{4,8},{8,4},{12,0},{1,13},{5,9},{9,5},{13,1},{2,14},{6,10},... | collective-permute-start | bytes 92168 | tf_op jit(solution)/shard_map/ppermute | solution.py:41
  13.5 0.0 collective-permute-done.6.refs_9_
  13.5 0.0 collective-permute-done.7.refs_11_
  13.5 0.0 collective-permute-done.8.refs_12_
  13.5 0.0 copy-start
  13.5 0.1 broadcast_select_fusion.4
  13.6 2.3 %collective-permute-start.9 = (bf16[5,8,512]{2,1,0:T(8,128)(2,1)S(1)}, bf16[5,8,512]{2,1,0:T(8,128)(2,1)S(1)}, u32[]{:S(2)}, u32[]{:S(2)}) collective-permute-start(bf16[5,8,512]{2,1,0:T(8,128)(2,1)S(1)} %broadcast_select_fusion.5), channel_id=1, source_target_pairs={{0,4},{4,0},{8,12},{12,8},{1,5},{5,1},{9,13},{13,9},{2,6},{6,2},{1... | collective-permute-start | bytes 122888 | tf_op jit(solution)/shard_map/ppermute | solution.py:42
  16.0 1.2 %collective-permute-start.10 = (bf16[5,8,512]{2,1,0:T(8,128)(2,1)S(1)}, bf16[5,8,512]{2,1,0:T(8,128)(2,1)S(1)}, u32[]{:S(2)}, u32[]{:S(2)}) collective-permute-start(bf16[5,8,512]{2,1,0:T(8,128)(2,1)S(1)} %get-tuple-element.21), channel_id=1, source_target_pairs={{0,12},{4,8},{8,4},{12,0},{1,13},{5,9},{9,5},{13,1},{2,14},{6,10},... | collective-permute-start | bytes 122888 | tf_op jit(solution)/shard_map/ppermute | solution.py:41
  17.2 0.1 pad_add_fusion.refs_0_
  17.3 0.0 collective-permute-done.3
  17.3 0.0 collective-permute-done.4
  17.3 0.0 copy-done
  17.3 1.2 %own_first_tick.1.refs_2_ = f32[5,4,40,128]{3,2,1,0:T(8,128)S(1)} custom-call(s32[3]{0:T(128)S(1)} %pad_add_fusion.refs_0_, bf16[1024,256]{1,0:T(8,128)(2,1)S(1)} %copy-done, f32[5,6,512]{2,1,0:T(8,128)S(1)} %convert_element_type.29.refs_2_.refs_3_, f32[5,6,512]{2,1,0:T(8,128)S(1)} %convert_element_type.30.refs_3_.refs_4_, ...), custom_call_target="tpu_custom_call" | custom-call | tf_op jit(solution)/shard_map/own_first_tick/pallas_call | solution.py:469
  18.5 0.0 collective-permute-done.9
  18.5 0.9 %collective-permute-done.10 = bf16[5,8,512]{2,1,0:T(8,128)(2,1)S(1)} collective-permute-done((bf16[5,8,512]{2,1,0:T(8,128)(2,1)S(1)}, bf16[5,8,512]{2,1,0:T(8,128)(2,1)S(1)}, u32[]{:S(2)}, u32[]{:S(2)}) %collective-permute-start.10) | collective-permute-done | bytes 40992 | tf_op jit(solution)/shard_map/ppermute | solution.py:41
  19.4 3.7 %advance.1 = f32[5,32,256]{2,1,0:T(8,128)} custom-call(s32[3]{0:T(128)S(1)} %pad_add_fusion.refs_0_, bf16[1024,256]{1,0:T(8,128)(2,1)S(1)} %copy-done, f32[5,4,40,128]{3,2,1,0:T(8,128)S(1)} %own_first_tick.1.refs_2_, f32[5,6,512]{2,1,0:T(8,128)S(1)} %convert_element_type.29.refs_2_.refs_3_, f32[5,6,512]{2,1,0:T(8,128)S(1)} %convert_element_type.30.refs_3_.refs_4_, ...), custom_call_target="tpu_custom_call" | custom-call | tf_op jit(solution)/shard_map/advance/pallas_call | solution.py:479
  (15 shorter events, 0.2 us)
Async XLA Ops:
  0.0 4.9 %copy-start.1 = (bf16[1,3,5,32,256]{4,3,2,1,0:T(8,128)(2,1)S(1)}, bf16[1,3,5,32,256]{4,3,2,1,0:T(8,128)(2,1)}, u32[]{:S(2)}) copy-start(bf16[1,3,5,32,256]{4,3,2,1,0:T(8,128)(2,1)} %param.4) | copy-start | bytes 737284
  1.1 5.4 %collective-permute-start.1 = (bf16[5,32,256]{2,1,0:T(8,128)(2,1)S(1)}, bf16[5,32,256]{2,1,0:T(8,128)(2,1)S(1)}, u32[]{:S(2)}, u32[]{:S(2)}) collective-permute-start(bf16[5,32,256]{2,1,0:T(8,128)(2,1)S(1)} %get-tuple-element.13), channel_id=1, source_target_pairs={{0,1},{1,0},{2,3},{3,2},{4,5},{5,4},{6,7},{7,6},{8,9},{9,8},{10,11... | collective-permute-start | bytes 245768 | tf_op jit(solution)/shard_map/ppermute | solution.py:42
  2.4 4.1 %collective-permute-start.2 = (bf16[5,32,256]{2,1,0:T(8,128)(2,1)S(1)}, bf16[5,32,256]{2,1,0:T(8,128)(2,1)S(1)}, u32[]{:S(2)}, u32[]{:S(2)}) collective-permute-start(bf16[5,32,256]{2,1,0:T(8,128)(2,1)S(1)} %get-tuple-element.13), channel_id=1, source_target_pairs={{0,16},{16,0},{1,17},{17,1},{2,18},{18,2},{3,19},{19,3},{4,20},{20... | collective-permute-start | bytes 245768 | tf_op jit(solution)/shard_map/ppermute | solution.py:51
  2.7 5.9 %collective-permute-start = (bf16[5,32,256]{2,1,0:T(8,128)(2,1)S(1)}, bf16[5,32,256]{2,1,0:T(8,128)(2,1)S(1)}, u32[]{:S(2)}, u32[]{:S(2)}) collective-permute-start(bf16[5,32,256]{2,1,0:T(8,128)(2,1)S(1)} %get-tuple-element.13), channel_id=1, source_target_pairs={{0,3},{1,2},{2,1},{3,0},{4,7},{5,6},{6,5},{7,4},{8,11},{9,10},{10,... | collective-permute-start | bytes 245768 | tf_op jit(solution)/shard_map/ppermute | solution.py:41
  5.0 7.0 %collective-permute-start.5 = (bf16[10,32,128]{2,1,0:T(8,128)(2,1)S(1)}, bf16[10,32,128]{2,1,0:T(8,128)(2,1)S(1)}, u32[]{:S(2)}, u32[]{:S(2)}) collective-permute-start(bf16[10,32,128]{2,1,0:T(8,128)(2,1)S(1)} %get-tuple-element.34), channel_id=1, source_target_pairs={{0,1},{1,0},{2,3},{3,2},{4,5},{5,4},{6,7},{7,6},{8,9},{9,8},{10,11... | collective-permute-start | bytes 245768 | tf_op jit(solution)/shard_map/ppermute | solution.py:42
  5.5 8.0 %collective-permute-start.6 = (bf16[10,32,128]{2,1,0:T(8,128)(2,1)S(1)}, bf16[10,32,128]{2,1,0:T(8,128)(2,1)S(1)}, u32[]{:S(2)}, u32[]{:S(2)}) collective-permute-start(bf16[10,32,128]{2,1,0:T(8,128)(2,1)S(1)} %get-tuple-element.33), channel_id=1, source_target_pairs={{0,3},{1,2},{2,1},{3,0},{4,7},{5,6},{6,5},{7,4},{8,11},{9,10},{10,... | collective-permute-start | bytes 245768 | tf_op jit(solution)/shard_map/ppermute | solution.py:41
  6.5 7.0 %collective-permute-start.7 = (bf16[5,32,256]{2,1,0:T(8,128)(2,1)S(1)}, bf16[5,32,256]{2,1,0:T(8,128)(2,1)S(1)}, u32[]{:S(2)}, u32[]{:S(2)}) collective-permute-start(bf16[5,32,256]{2,1,0:T(8,128)(2,1)S(1)} %collective-permute-done.1.refs_5_), channel_id=1, source_target_pairs={{0,16},{16,0},{1,17},{17,1},{2,18},{18,2},{3,19},{19,3},{4,20},{20... | collective-permute-start | bytes 245768 | tf_op jit(solution)/shard_map/ppermute | solution.py:51
  8.7 4.8 %collective-permute-start.8 = (bf16[5,32,256]{2,1,0:T(8,128)(2,1)S(1)}, bf16[5,32,256]{2,1,0:T(8,128)(2,1)S(1)}, u32[]{:S(2)}, u32[]{:S(2)}) collective-permute-start(bf16[5,32,256]{2,1,0:T(8,128)(2,1)S(1)} %collective-permute-done.refs_6_), channel_id=1, source_target_pairs={{0,16},{16,0},{1,17},{17,1},{2,18},{18,2},{3,19},{19,3},{4,20},{20... | collective-permute-start | bytes 245768 | tf_op jit(solution)/shard_map/ppermute | solution.py:51
  9.2 8.0 %collective-permute-start.3 = (bf16[5,6,512]{2,1,0:T(8,128)(2,1)S(1)}, bf16[5,6,512]{2,1,0:T(8,128)(2,1)S(1)}, u32[]{:S(2)}, u32[]{:S(2)}) collective-permute-start(bf16[5,6,512]{2,1,0:T(8,128)(2,1)S(1)} %broadcast_select_fusion.7), channel_id=1, source_target_pairs={{0,4},{4,0},{8,12},{12,8},{1,5},{5,1},{9,13},{13,9},{2,6},{6,2},{1... | collective-permute-start | bytes 92168 | tf_op jit(solution)/shard_map/ppermute | solution.py:42
  12.1 5.2 %collective-permute-start.4 = (bf16[5,6,512]{2,1,0:T(8,128)(2,1)S(1)}, bf16[5,6,512]{2,1,0:T(8,128)(2,1)S(1)}, u32[]{:S(2)}, u32[]{:S(2)}) collective-permute-start(bf16[5,6,512]{2,1,0:T(8,128)(2,1)S(1)} %get-tuple-element.24), channel_id=1, source_target_pairs={{0,12},{4,8},{8,4},{12,0},{1,13},{5,9},{9,5},{13,1},{2,14},{6,10},... | collective-permute-start | bytes 92168 | tf_op jit(solution)/shard_map/ppermute | solution.py:41
  13.5 3.8 %copy-start = (bf16[1024,256]{1,0:T(8,128)(2,1)S(1)}, bf16[1024,256]{1,0:T(8,128)(2,1)}, u32[]{:S(2)}) copy-start(bf16[1024,256]{1,0:T(8,128)(2,1)} %constant.41.clone.refs_1_) | copy-start | bytes 1572868
  13.6 4.9 %collective-permute-start.9 = (bf16[5,8,512]{2,1,0:T(8,128)(2,1)S(1)}, bf16[5,8,512]{2,1,0:T(8,128)(2,1)S(1)}, u32[]{:S(2)}, u32[]{:S(2)}) collective-permute-start(bf16[5,8,512]{2,1,0:T(8,128)(2,1)S(1)} %broadcast_select_fusion.5), channel_id=1, source_target_pairs={{0,4},{4,0},{8,12},{12,8},{1,5},{5,1},{9,13},{13,9},{2,6},{6,2},{1... | collective-permute-start | bytes 122888 | tf_op jit(solution)/shard_map/ppermute | solution.py:42
  16.0 3.4 %collective-permute-start.10 = (bf16[5,8,512]{2,1,0:T(8,128)(2,1)S(1)}, bf16[5,8,512]{2,1,0:T(8,128)(2,1)S(1)}, u32[]{:S(2)}, u32[]{:S(2)}) collective-permute-start(bf16[5,8,512]{2,1,0:T(8,128)(2,1)S(1)} %get-tuple-element.21), channel_id=1, source_target_pairs={{0,12},{4,8},{8,4},{12,0},{1,13},{5,9},{9,5},{13,1},{2,14},{6,10},... | collective-permute-start | bytes 122888 | tf_op jit(solution)/shard_map/ppermute | solution.py:41

commit v7 on v6

--- a/solution.py
+++ b/solution.py
@@ -195,28 +195,34 @@
                 if 1 <= tile <= 4:
                     self.flow_z[tile - 1, pl.ds(field * self.high, self.high), :] = along_z[field]
 
-    def spreading(self, tile):
-        none = jnp.zeros((self.high, LANES), jnp.float32)
-        return jnp.concatenate([none] + [self.slow[kind, tile, self.window, :] for kind in range(FIELDS - 1)])
-
     def products(self, tick):
-        for tile in range(6) if tick == 0 else range(1, 5):
+        known = range(6) if tick == 0 else range(1, 5)
+        for tile in known:
             self.pointwise(tile, START, self.high, False)
             if tick == 0 and 1 <= tile <= 4:
                 self.pointwise(tile, 0, START, True)
                 self.pointwise(tile, START + self.high, START, True)
         from_above = lax.broadcasted_iota(jnp.int32, (FIELDS * self.high, LANES), 1) < LANES // 2
-        flow_y, flow_z, spreading = self.flow_y, self.flow_z, self.spreading
+        flow_z = self.flow_z
+
+        def flow_y(tile):
+            return self.flow_y[tile] if tile in known else jnp.zeros((FIELDS * self.high, LANES), jnp.float32)
+
+        def spreading(tile):
+            none = jnp.zeros((self.high, LANES), jnp.float32)
+            kinds = [self.slow[kind, tile, self.window, :] if tile in known else none for kind in range(FIELDS - 1)]
+            return jnp.concatenate([none, *kinds])
+
         found = {}
         for low, top in ((2, 3),) if tick == TICKS - 1 else ((1, 2), (3, 4)):
             parts = [
-                flow_y[low],
-                flow_y[top],
+                flow_y(low),
+                flow_y(top),
                 flow_z[low - 1],
                 flow_z[top - 1],
                 spreading(low),
                 spreading(top),
-                jnp.where(from_above, flow_y[top + 1], flow_y[low - 1]),
+                jnp.where(from_above, flow_y(top + 1), flow_y(low - 1)),
                 jnp.where(from_above, spreading(top + 1), spreading(low - 1)),
             ]
             left = jnp.concatenate([part.astype(jnp.bfloat16) for part in parts], axis=1)

time: 23.3 us -> 23.2 us (level)
  no operation moved by 1% of the time
where the time goes in v7:
time: 23.2 us; the launch traced here: 23 us
  starting transfers between devices  14.7 us (63%)
  Pallas kernels  4.8 us (21%)
  waiting for transfers between devices  1.72 us (7%)
  other arithmetic  1.52 us (7%)
    ppermute x4, starting transfers between devices, neighbours(): first = lax.ppermute(outward, axis, near)  7 us
    ppermute x4, starting transfers between devices, neighbours(): second = lax.ppermute(inward, axis, far)  5.7 us
    pallas_call x1, Pallas kernels, per_device(): pl.pallas_call(functools.partial(advance_kernel, chain, corrected, rows),...  3.61 us
    ppermute x3, starting transfers between devices, from_lower(): return lax.ppermute(block, 'sec', route)  2.04 us
    ppermute x4, waiting for transfers between devices, neighbours(): second = lax.ppermute(inward, axis, far)  1.7 us
    pallas_call x1, Pallas kernels, per_device(): pl.pallas_call(functools.partial(first_kernel, chain, corrected, rows), o...  1.18 us
    convert_element_type x1, other arithmetic, per_device(): sent = block.astype(jnp.bfloat16)  1.07 us
  transfers between devices with their start and end apart: 11, of which 2 were waited for; matrix products, arithmetic and copies ran while one was open for 2% of the time, Pallas kernels for 5%

profile of v7, /device:TPU:3, one launch (start us, length us, event | category | flops | bytes accessed | tf_op | source)
XLA Modules:
  0.0 23.0 jit_solution(7936459341664551091)
XLA Ops:
  0.0 0.0 copy-start.1
  0.0 1.1 %convert_bitcast_fusion = (bf16[5,32,256]{2,1,0:T(8,128)(2,1)S(1)}, f32[5,32,256]{2,1,0:T(8,128)S(1)}) fusion(f32[1,5,32,256]{3,2,1,0:T(8,128)} %param.3), kind=kLoop, calls=%fused_computation.24 | loop fusion | flops 81920 | bytes 409600 | tf_op jit(solution)/shard_map/convert_element_type | solution.py:400
  1.1 1.4 %collective-permute-start.1 = (bf16[5,32,256]{2,1,0:T(8,128)(2,1)S(1)}, bf16[5,32,256]{2,1,0:T(8,128)(2,1)S(1)}, u32[]{:S(2)}, u32[]{:S(2)}) collective-permute-start(bf16[5,32,256]{2,1,0:T(8,128)(2,1)S(1)} %get-tuple-element.13), channel_id=1, source_target_pairs={{0,1},{1,0},{2,3},{3,2},{4,5},{5,4},{6,7},{7,6},{8,9},{9,8},{10,11... | collective-permute-start | bytes 245768 | tf_op jit(solution)/shard_map/ppermute | solution.py:42
  2.4 0.3 %collective-permute-start.2 = (bf16[5,32,256]{2,1,0:T(8,128)(2,1)S(1)}, bf16[5,32,256]{2,1,0:T(8,128)(2,1)S(1)}, u32[]{:S(2)}, u32[]{:S(2)}) collective-permute-start(bf16[5,32,256]{2,1,0:T(8,128)(2,1)S(1)} %get-tuple-element.13), channel_id=1, source_target_pairs={{0,16},{16,0},{1,17},{17,1},{2,18},{18,2},{3,19},{19,3},{4,20},{20... | collective-permute-start | bytes 245768 | tf_op jit(solution)/shard_map/ppermute | solution.py:51
  2.7 2.2 %collective-permute-start = (bf16[5,32,256]{2,1,0:T(8,128)(2,1)S(1)}, bf16[5,32,256]{2,1,0:T(8,128)(2,1)S(1)}, u32[]{:S(2)}, u32[]{:S(2)}) collective-permute-start(bf16[5,32,256]{2,1,0:T(8,128)(2,1)S(1)} %get-tuple-element.13), channel_id=1, source_target_pairs={{0,3},{1,2},{2,1},{3,0},{4,7},{5,6},{6,5},{7,4},{8,11},{9,10},{10,... | collective-permute-start | bytes 245768 | tf_op jit(solution)/shard_map/ppermute | solution.py:41
  4.9 0.0 copy-done.1
  4.9 0.1 fusion.5
  5.0 0.5 %collective-permute-start.5 = (bf16[10,32,128]{2,1,0:T(8,128)(2,1)S(1)}, bf16[10,32,128]{2,1,0:T(8,128)(2,1)S(1)}, u32[]{:S(2)}, u32[]{:S(2)}) collective-permute-start(bf16[10,32,128]{2,1,0:T(8,128)(2,1)S(1)} %get-tuple-element.34), channel_id=1, source_target_pairs={{0,1},{1,0},{2,3},{3,2},{4,5},{5,4},{6,7},{7,6},{8,9},{9,8},{10,11... | collective-permute-start | bytes 245768 | tf_op jit(solution)/shard_map/ppermute | solution.py:42
  5.5 0.9 %collective-permute-start.6 = (bf16[10,32,128]{2,1,0:T(8,128)(2,1)S(1)}, bf16[10,32,128]{2,1,0:T(8,128)(2,1)S(1)}, u32[]{:S(2)}, u32[]{:S(2)}) collective-permute-start(bf16[10,32,128]{2,1,0:T(8,128)(2,1)S(1)} %get-tuple-element.33), channel_id=1, source_target_pairs={{0,3},{1,2},{2,1},{3,0},{4,7},{5,6},{6,5},{7,4},{8,11},{9,10},{10,... | collective-permute-start | bytes 245768 | tf_op jit(solution)/shard_map/ppermute | solution.py:41
  6.5 0.0 collective-permute-done.1.refs_5_
  6.5 0.0 collective-permute-done.2.refs_10_
  6.5 1.3 %collective-permute-start.7 = (bf16[5,32,256]{2,1,0:T(8,128)(2,1)S(1)}, bf16[5,32,256]{2,1,0:T(8,128)(2,1)S(1)}, u32[]{:S(2)}, u32[]{:S(2)}) collective-permute-start(bf16[5,32,256]{2,1,0:T(8,128)(2,1)S(1)} %collective-permute-done.1.refs_5_), channel_id=1, source_target_pairs={{0,16},{16,0},{1,17},{17,1},{2,18},{18,2},{3,19},{19,3},{4,20},{20... | collective-permute-start | bytes 245768 | tf_op jit(solution)/shard_map/ppermute | solution.py:51
  7.8 0.8 %collective-permute-done.refs_6_ = bf16[5,32,256]{2,1,0:T(8,128)(2,1)S(1)} collective-permute-done((bf16[5,32,256]{2,1,0:T(8,128)(2,1)S(1)}, bf16[5,32,256]{2,1,0:T(8,128)(2,1)S(1)}, u32[]{:S(2)}, u32[]{:S(2)}) %collective-permute-start) | collective-permute-done | bytes 81952 | tf_op jit(solution)/shard_map/ppermute | solution.py:41
  8.6 0.1 broadcast_select_fusion.6
  8.7 0.5 %collective-permute-start.8 = (bf16[5,32,256]{2,1,0:T(8,128)(2,1)S(1)}, bf16[5,32,256]{2,1,0:T(8,128)(2,1)S(1)}, u32[]{:S(2)}, u32[]{:S(2)}) collective-permute-start(bf16[5,32,256]{2,1,0:T(8,128)(2,1)S(1)} %collective-permute-done.refs_6_), channel_id=1, source_target_pairs={{0,16},{16,0},{1,17},{17,1},{2,18},{18,2},{3,19},{19,3},{4,20},{20... | collective-permute-start | bytes 245768 | tf_op jit(solution)/shard_map/ppermute | solution.py:51
  9.2 2.8 %collective-permute-start.3 = (bf16[5,6,512]{2,1,0:T(8,128)(2,1)S(1)}, bf16[5,6,512]{2,1,0:T(8,128)(2,1)S(1)}, u32[]{:S(2)}, u32[]{:S(2)}) collective-permute-start(bf16[5,6,512]{2,1,0:T(8,128)(2,1)S(1)} %broadcast_select_fusion.7), channel_id=1, source_target_pairs={{0,4},{4,0},{8,12},{12,8},{1,5},{5,1},{9,13},{13,9},{2,6},{6,2},{1... | collective-permute-start | bytes 92168 | tf_op jit(solution)/shard_map/ppermute | solution.py:42
  12.1 0.0 collective-permute-done.5.refs_8_
  12.1 1.4 %collective-permute-start.4 = (bf16[5,6,512]{2,1,0:T(8,128)(2,1)S(1)}, bf16[5,6,512]{2,1,0:T(8,128)(2,1)S(1)}, u32[]{:S(2)}, u32[]{:S(2)}) collective-permute-start(bf16[5,6,512]{2,1,0:T(8,128)(2,1)S(1)} %get-tuple-element.24), channel_id=1, source_target_pairs={{0,12},{4,8},{8,4},{12,0},{1,13},{5,9},{9,5},{13,1},{2,14},{6,10},... | collective-permute-start | bytes 92168 | tf_op jit(solution)/shard_map/ppermute | solution.py:41
  13.5 0.0 collective-permute-done.6.refs_9_
  13.5 0.0 collective-permute-done.7.refs_11_
  13.5 0.0 collective-permute-done.8.refs_12_
  13.5 0.0 copy-start
  13.5 0.1 broadcast_select_fusion.4
  13.6 2.3 %collective-permute-start.9 = (bf16[5,8,512]{2,1,0:T(8,128)(2,1)S(1)}, bf16[5,8,512]{2,1,0:T(8,128)(2,1)S(1)}, u32[]{:S(2)}, u32[]{:S(2)}) collective-permute-start(bf16[5,8,512]{2,1,0:T(8,128)(2,1)S(1)} %broadcast_select_fusion.5), channel_id=1, source_target_pairs={{0,4},{4,0},{8,12},{12,8},{1,5},{5,1},{9,13},{13,9},{2,6},{6,2},{1... | collective-permute-start | bytes 122888 | tf_op jit(solution)/shard_map/ppermute | solution.py:42
  16.0 1.2 %collective-permute-start.10 = (bf16[5,8,512]{2,1,0:T(8,128)(2,1)S(1)}, bf16[5,8,512]{2,1,0:T(8,128)(2,1)S(1)}, u32[]{:S(2)}, u32[]{:S(2)}) collective-permute-start(bf16[5,8,512]{2,1,0:T(8,128)(2,1)S(1)} %get-tuple-element.21), channel_id=1, source_target_pairs={{0,12},{4,8},{8,4},{12,0},{1,13},{5,9},{9,5},{13,1},{2,14},{6,10},... | collective-permute-start | bytes 122888 | tf_op jit(solution)/shard_map/ppermute | solution.py:41
  17.2 0.1 pad_add_fusion.refs_0_
  17.3 0.0 collective-permute-done.3
  17.3 0.0 collective-permute-done.4
  17.3 0.0 copy-done
  17.3 1.2 %own_first_tick.1.refs_2_ = f32[5,4,40,128]{3,2,1,0:T(8,128)S(1)} custom-call(s32[3]{0:T(128)S(1)} %pad_add_fusion.refs_0_, bf16[1024,256]{1,0:T(8,128)(2,1)S(1)} %copy-done, f32[5,6,512]{2,1,0:T(8,128)S(1)} %convert_element_type.29.refs_2_.refs_3_, f32[5,6,512]{2,1,0:T(8,128)S(1)} %convert_element_type.30.refs_3_.refs_4_, ...), custom_call_target="tpu_custom_call" | custom-call | tf_op jit(solution)/shard_map/own_first_tick/pallas_call | solution.py:475
  18.5 0.0 collective-permute-done.9
  18.5 0.9 %collective-permute-done.10 = bf16[5,8,512]{2,1,0:T(8,128)(2,1)S(1)} collective-permute-done((bf16[5,8,512]{2,1,0:T(8,128)(2,1)S(1)}, bf16[5,8,512]{2,1,0:T(8,128)(2,1)S(1)}, u32[]{:S(2)}, u32[]{:S(2)}) %collective-permute-start.10) | collective-permute-done | bytes 40992 | tf_op jit(solution)/shard_map/ppermute | solution.py:41
  19.4 3.6 %advance.1 = f32[5,32,256]{2,1,0:T(8,128)} custom-call(s32[3]{0:T(128)S(1)} %pad_add_fusion.refs_0_, bf16[1024,256]{1,0:T(8,128)(2,1)S(1)} %copy-done, f32[5,4,40,128]{3,2,1,0:T(8,128)S(1)} %own_first_tick.1.refs_2_, f32[5,6,512]{2,1,0:T(8,128)S(1)} %convert_element_type.29.refs_2_.refs_3_, f32[5,6,512]{2,1,0:T(8,128)S(1)} %convert_element_type.30.refs_3_.refs_4_, ...), custom_call_target="tpu_custom_call" | custom-call | tf_op jit(solution)/shard_map/advance/pallas_call | solution.py:485
  (15 shorter events, 0.2 us)
Async XLA Ops:
  0.0 4.9 %copy-start.1 = (bf16[1,3,5,32,256]{4,3,2,1,0:T(8,128)(2,1)S(1)}, bf16[1,3,5,32,256]{4,3,2,1,0:T(8,128)(2,1)}, u32[]{:S(2)}) copy-start(bf16[1,3,5,32,256]{4,3,2,1,0:T(8,128)(2,1)} %param.4) | copy-start | bytes 737284
  1.1 5.4 %collective-permute-start.1 = (bf16[5,32,256]{2,1,0:T(8,128)(2,1)S(1)}, bf16[5,32,256]{2,1,0:T(8,128)(2,1)S(1)}, u32[]{:S(2)}, u32[]{:S(2)}) collective-permute-start(bf16[5,32,256]{2,1,0:T(8,128)(2,1)S(1)} %get-tuple-element.13), channel_id=1, source_target_pairs={{0,1},{1,0},{2,3},{3,2},{4,5},{5,4},{6,7},{7,6},{8,9},{9,8},{10,11... | collective-permute-start | bytes 245768 | tf_op jit(solution)/shard_map/ppermute | solution.py:42
  2.4 4.1 %collective-permute-start.2 = (bf16[5,32,256]{2,1,0:T(8,128)(2,1)S(1)}, bf16[5,32,256]{2,1,0:T(8,128)(2,1)S(1)}, u32[]{:S(2)}, u32[]{:S(2)}) collective-permute-start(bf16[5,32,256]{2,1,0:T(8,128)(2,1)S(1)} %get-tuple-element.13), channel_id=1, source_target_pairs={{0,16},{16,0},{1,17},{17,1},{2,18},{18,2},{3,19},{19,3},{4,20},{20... | collective-permute-start | bytes 245768 | tf_op jit(solution)/shard_map/ppermute | solution.py:51
  2.7 5.9 %collective-permute-start = (bf16[5,32,256]{2,1,0:T(8,128)(2,1)S(1)}, bf16[5,32,256]{2,1,0:T(8,128)(2,1)S(1)}, u32[]{:S(2)}, u32[]{:S(2)}) collective-permute-start(bf16[5,32,256]{2,1,0:T(8,128)(2,1)S(1)} %get-tuple-element.13), channel_id=1, source_target_pairs={{0,3},{1,2},{2,1},{3,0},{4,7},{5,6},{6,5},{7,4},{8,11},{9,10},{10,... | collective-permute-start | bytes 245768 | tf_op jit(solution)/shard_map/ppermute | solution.py:41
  5.0 7.0 %collective-permute-start.5 = (bf16[10,32,128]{2,1,0:T(8,128)(2,1)S(1)}, bf16[10,32,128]{2,1,0:T(8,128)(2,1)S(1)}, u32[]{:S(2)}, u32[]{:S(2)}) collective-permute-start(bf16[10,32,128]{2,1,0:T(8,128)(2,1)S(1)} %get-tuple-element.34), channel_id=1, source_target_pairs={{0,1},{1,0},{2,3},{3,2},{4,5},{5,4},{6,7},{7,6},{8,9},{9,8},{10,11... | collective-permute-start | bytes 245768 | tf_op jit(solution)/shard_map/ppermute | solution.py:42
  5.5 8.0 %collective-permute-start.6 = (bf16[10,32,128]{2,1,0:T(8,128)(2,1)S(1)}, bf16[10,32,128]{2,1,0:T(8,128)(2,1)S(1)}, u32[]{:S(2)}, u32[]{:S(2)}) collective-permute-start(bf16[10,32,128]{2,1,0:T(8,128)(2,1)S(1)} %get-tuple-element.33), channel_id=1, source_target_pairs={{0,3},{1,2},{2,1},{3,0},{4,7},{5,6},{6,5},{7,4},{8,11},{9,10},{10,... | collective-permute-start | bytes 245768 | tf_op jit(solution)/shard_map/ppermute | solution.py:41
  6.5 7.0 %collective-permute-start.7 = (bf16[5,32,256]{2,1,0:T(8,128)(2,1)S(1)}, bf16[5,32,256]{2,1,0:T(8,128)(2,1)S(1)}, u32[]{:S(2)}, u32[]{:S(2)}) collective-permute-start(bf16[5,32,256]{2,1,0:T(8,128)(2,1)S(1)} %collective-permute-done.1.refs_5_), channel_id=1, source_target_pairs={{0,16},{16,0},{1,17},{17,1},{2,18},{18,2},{3,19},{19,3},{4,20},{20... | collective-permute-start | bytes 245768 | tf_op jit(solution)/shard_map/ppermute | solution.py:51
  8.7 4.8 %collective-permute-start.8 = (bf16[5,32,256]{2,1,0:T(8,128)(2,1)S(1)}, bf16[5,32,256]{2,1,0:T(8,128)(2,1)S(1)}, u32[]{:S(2)}, u32[]{:S(2)}) collective-permute-start(bf16[5,32,256]{2,1,0:T(8,128)(2,1)S(1)} %collective-permute-done.refs_6_), channel_id=1, source_target_pairs={{0,16},{16,0},{1,17},{17,1},{2,18},{18,2},{3,19},{19,3},{4,20},{20... | collective-permute-start | bytes 245768 | tf_op jit(solution)/shard_map/ppermute | solution.py:51
  9.2 8.0 %collective-permute-start.3 = (bf16[5,6,512]{2,1,0:T(8,128)(2,1)S(1)}, bf16[5,6,512]{2,1,0:T(8,128)(2,1)S(1)}, u32[]{:S(2)}, u32[]{:S(2)}) collective-permute-start(bf16[5,6,512]{2,1,0:T(8,128)(2,1)S(1)} %broadcast_select_fusion.7), channel_id=1, source_target_pairs={{0,4},{4,0},{8,12},{12,8},{1,5},{5,1},{9,13},{13,9},{2,6},{6,2},{1... | collective-permute-start | bytes 92168 | tf_op jit(solution)/shard_map/ppermute | solution.py:42
  12.1 5.2 %collective-permute-start.4 = (bf16[5,6,512]{2,1,0:T(8,128)(2,1)S(1)}, bf16[5,6,512]{2,1,0:T(8,128)(2,1)S(1)}, u32[]{:S(2)}, u32[]{:S(2)}) collective-permute-start(bf16[5,6,512]{2,1,0:T(8,128)(2,1)S(1)} %get-tuple-element.24), channel_id=1, source_target_pairs={{0,12},{4,8},{8,4},{12,0},{1,13},{5,9},{9,5},{13,1},{2,14},{6,10},... | collective-permute-start | bytes 92168 | tf_op jit(solution)/shard_map/ppermute | solution.py:41
  13.5 3.8 %copy-start = (bf16[1024,256]{1,0:T(8,128)(2,1)S(1)}, bf16[1024,256]{1,0:T(8,128)(2,1)}, u32[]{:S(2)}) copy-start(bf16[1024,256]{1,0:T(8,128)(2,1)} %constant.41.clone.refs_1_) | copy-start | bytes 1572868
  13.6 4.9 %collective-permute-start.9 = (bf16[5,8,512]{2,1,0:T(8,128)(2,1)S(1)}, bf16[5,8,512]{2,1,0:T(8,128)(2,1)S(1)}, u32[]{:S(2)}, u32[]{:S(2)}) collective-permute-start(bf16[5,8,512]{2,1,0:T(8,128)(2,1)S(1)} %broadcast_select_fusion.5), channel_id=1, source_target_pairs={{0,4},{4,0},{8,12},{12,8},{1,5},{5,1},{9,13},{13,9},{2,6},{6,2},{1... | collective-permute-start | bytes 122888 | tf_op jit(solution)/shard_map/ppermute | solution.py:42
  16.0 3.4 %collective-permute-start.10 = (bf16[5,8,512]{2,1,0:T(8,128)(2,1)S(1)}, bf16[5,8,512]{2,1,0:T(8,128)(2,1)S(1)}, u32[]{:S(2)}, u32[]{:S(2)}) collective-permute-start(bf16[5,8,512]{2,1,0:T(8,128)(2,1)S(1)} %get-tuple-element.21), channel_id=1, source_target_pairs={{0,12},{4,8},{8,4},{12,0},{1,13},{5,9},{9,5},{13,1},{2,14},{6,10},... | collective-permute-start | bytes 122888 | tf_op jit(solution)/shard_map/ppermute | solution.py:41

commit v8 on v7

--- a/solution.py
+++ b/solution.py
@@ -62,16 +62,16 @@
         for z in range(NZ):
             column = y * NZ + z
             here = (y + per_tile) * NZ + z
-            d_y[here + NZ, column] -= 0.5
-            d_y[here - NZ, column] += 0.5
-            d_z[y * NZ + (z + 1) % NZ, column] -= 0.5
-            d_z[y * NZ + (z - 1) % NZ, column] += 0.5
-            sweep[here, column] -= 1.0
-            sweep[here + 2 * NZ, column] += 0.25
-            sweep[here - 2 * NZ, column] += 0.25
+            d_y[here + NZ, column] -= 1.0
+            d_y[here - NZ, column] += 1.0
+            d_z[y * NZ + (z + 1) % NZ, column] -= 1.0
+            d_z[y * NZ + (z - 1) % NZ, column] += 1.0
+            sweep[here, column] -= 6.0
+            sweep[here + 2 * NZ, column] += 1.0
+            sweep[here - 2 * NZ, column] += 1.0
             base = (y + per_tile) * NZ
-            sweep[base + (z + 2) % NZ, column] += 0.25
-            sweep[base + (z - 2) % NZ, column] += 0.25
+            sweep[base + (z + 2) % NZ, column] += 1.0
+            sweep[base + (z - 2) % NZ, column] += 1.0
 
     def inner(matrix):
         return matrix[LANES : 3 * LANES]
@@ -162,59 +162,72 @@
                     terms[tick, field, tile, pl.ds(FIRST + rows, FIRST), :] = none
                 place_edges(lambda tile: terms.at[tick, field, tile], edges[tick], pieces[tick], field, rows)
 
-    def pointwise(self, tile, start, count, only_x):
-        place = pl.ds(start, count)
-        density, mom_x, mom_y, mom_z, energy = [self.state[field, tile, place, :] for field in range(FIELDS)]
+    def pointwise(self, state, tile, place, along=True, across=True):
+        density, mom_x, mom_y, mom_z, energy = state
         inverse = 1.0 / density
         vel_x = mom_x * inverse
         vel_y = mom_y * inverse
         vel_z = mom_z * inverse
-        kinetic = 0.5 * (vel_x * vel_x + vel_y * vel_y + vel_z * vel_z)
-        pressure = GAMMA_LESS * (energy - density * kinetic)
+        xx, yy, zz = mom_x * vel_x, mom_y * vel_y, mom_z * vel_z
+        moving = xx + yy + zz
+        pressure = GAMMA_LESS * energy - (0.5 * GAMMA_LESS) * moving
         enthalpy = energy + pressure
-        heat = DYNAMIC_FRICTION * kinetic + CONDUCTIVITY * (pressure * inverse)
+        heat = ((0.25 * DYNAMIC_FRICTION) * moving + (0.5 * CONDUCTIVITY) * pressure) * inverse
         xy = mom_x * vel_y
         xz = mom_x * vel_z
         yz = mom_y * vel_z
-        along_x = (mom_x, mom_x * vel_x + pressure, xy, xz, enthalpy * vel_x)
-        along_y = (mom_y, xy, mom_y * vel_y + pressure, yz, enthalpy * vel_y)
-        along_z = (mom_z, xz, yz, mom_z * vel_z + pressure, enthalpy * vel_z)
-        spread = (
-            DYNAMIC_FRICTION * vel_x,
-            DYNAMIC_FRICTION * vel_y,
-            DYNAMIC_FRICTION * vel_z,
-            heat,
-        )
+        along_x = (mom_x, xx + pressure, xy, xz, enthalpy * vel_x)
+        along_y = (mom_y, xy, yy + pressure, yz, enthalpy * vel_y)
+        along_z = (mom_z, xz, yz, zz + pressure, enthalpy * vel_z)
+        friction = 0.5 * DYNAMIC_FRICTION
+        spread = (friction * vel_x, friction * vel_y, friction * vel_z, heat)
         for field in range(FIELDS):
-            if 1 <= tile <= 4:
+            if along:
                 self.flow_x[field, tile - 1, place, :] = along_x[field]
             if field:
                 self.slow[field - 1, tile, place, :] = spread[field - 1]
-            if not only_x:
-                self.flow_y[tile, pl.ds(field * self.high, self.high), :] = along_y[field]
-                if 1 <= tile <= 4:
-                    self.flow_z[tile - 1, pl.ds(field * self.high, self.high), :] = along_z[field]
+            if across:
+                rows = pl.ds(field * self.high, self.high)
+                self.flow_y[tile, rows, :] = along_y[field]
+                if along:
+                    self.flow_z[tile - 1, rows, :] = along_z[field]
 
     def products(self, tick):
-        known = range(6) if tick == 0 else range(1, 5)
-        for tile in known:
-            self.pointwise(tile, START, self.high, False)
-            if tick == 0 and 1 <= tile <= 4:
-                self.pointwise(tile, 0, START, True)
-                self.pointwise(tile, START + self.high, START, True)
+        last = tick == TICKS - 1
+        inner = (2, 3) if last else (1, 2, 3, 4)
+        for tile in inner:
+            parts = [(START, True)] + ([(0, False), (START + self.high, False)] if tick == 0 else [])
+            for start, across in parts:
+                place = pl.ds(start, self.high if across else START)
+                state = [self.state[field, tile, place, :] for field in range(FIELDS)]
+                self.pointwise(state, tile, place, across=across)
+        outer = {0: (0, 5), TICKS - 1: (1, 4)}.get(tick)
+        if outer:
+            above = lax.broadcasted_iota(jnp.int32, (self.high, LANES), 1) < LANES // 2
+            pairs = [[self.state[field, tile, self.window, :] for tile in outer] for field in range(FIELDS)]
+            state = [jnp.where(above, top, low) for low, top in pairs]
+            self.pointwise(state, 0, self.window, along=False)
+        none = jnp.zeros((self.high, LANES), jnp.float32)
+
+        def flow_y(tile):
+            if tile in inner:
+                return self.flow_y[tile]
+            return self.flow_y[0] if outer else jnp.concatenate([none] * FIELDS)
+
+        def spreading(tile):
+            tile = tile if tile in inner else 0
+            kinds = range(FIELDS - 1)
+            known = tile or outer
+            return jnp.concatenate([none] + [self.slow[kind, tile, self.window, :] if known else none for kind in kinds])
+
         from_above = lax.broadcasted_iota(jnp.int32, (FIELDS * self.high, LANES), 1) < LANES // 2
         flow_z = self.flow_z
-
-        def flow_y(tile):
-            return self.flow_y[tile] if tile in known else jnp.zeros((FIELDS * self.high, LANES), jnp.float32)
-
-        def spreading(tile):
-            none = jnp.zeros((self.high, LANES), jnp.float32)
-            kinds = [self.slow[kind, tile, self.window, :] if tile in known else none for kind in range(FIELDS - 1)]
-            return jnp.concatenate([none, *kinds])
-
         found = {}
-        for low, top in ((2, 3),) if tick == TICKS - 1 else ((1, 2), (3, 4)):
+        for low, top in ((2, 3),) if last else ((1, 2), (3, 4)):
+            if last:
+                around = [flow_y(0), spreading(0)]
+            else:
+                around = [jnp.where(from_above, part(top + 1), part(low - 1)) for part in (flow_y, spreading)]
             parts = [
                 flow_y(low),
                 flow_y(top),
@@ -222,8 +235,7 @@
                 flow_z[top - 1],
                 spreading(low),
                 spreading(top),
-                jnp.where(from_above, flow_y(top + 1), flow_y(low - 1)),
-                jnp.where(from_above, spreading(top + 1), spreading(low - 1)),
+                *around,
             ]
             left = jnp.concatenate([part.astype(jnp.bfloat16) for part in parts], axis=1)
             found[low, top] = jnp.dot(left, self.matrix[...], preferred_element_type=jnp.float32)
@@ -233,11 +245,10 @@
         def shifted(ref, *index, step):
             return ref[(*index, pl.ds(START + step, self.high))]
 
-        total = 0.5 * (shifted(self.flow_x, field, tile - 1, step=-1) - shifted(self.flow_x, field, tile - 1, step=1))
+        total = shifted(self.flow_x, field, tile - 1, step=-1) - shifted(self.flow_x, field, tile - 1, step=1)
         if field:
             kind = field - 1
-            around = shifted(self.slow, kind, tile, step=2) + shifted(self.slow, kind, tile, step=-2)
-            total = total + (0.25 * around - 0.5 * shifted(self.slow, kind, tile, step=0))
+            total = total + (shifted(self.slow, kind, tile, step=2) + shifted(self.slow, kind, tile, step=-2))
         return total
 
     def rates(self, found):
@@ -287,7 +298,7 @@
     level = Level(rows, even_x, flags[1] == 1, matrix, scratch)
     level.assemble(center, y_first, y_second, edges, pieces["state", 0])
     for field, tile, rate in level.rates(level.products(0)):
-        out[field, tile - 1] = level.state[field, tile, level.window, :] + TIME_STEP * rate
+        out[field, tile - 1] = level.state[field, tile, level.window, :] + (0.5 * TIME_STEP) * rate
 
 
 def advance_kernel(chain, corrected, rows, *refs):
@@ -341,11 +352,13 @@
                 return
             for field, tile, rate in level.rates(found):
                 if link:
-                    fresh[link - 1, tick, field, tile - 1] = rate.astype(jnp.bfloat16).astype(jnp.float32)
+                    fresh[link - 1, tick, field, tile - 1] = (0.5 * rate).astype(jnp.bfloat16).astype(jnp.float32)
                 if link + tick >= TICKS:
                     continue
-                step = rate + correction(link, tick, field, tile) if fix else rate
-                level.state[field, tile, window, :] = level.state[field, tile, window, :] + TIME_STEP * step
+                state = level.state[field, tile, window, :] + (0.5 * TIME_STEP) * rate
+                if fix:
+                    state = state + TIME_STEP * correction(link, tick, field, tile)
+                level.state[field, tile, window, :] = state
                 if tick == TICKS - 1:
                     out[field, :, lanes(tile - 2)] = level.state[field, tile, pl.ds(FIRST, rows), :]
 

time: 23.2 us -> 23 us (level)
  Pallas kernels: 4.8 us -> 4.56 us
where the time goes in v8:
time: 23 us; the launch traced here: 22.9 us
  starting transfers between devices  14.7 us (64%)
  Pallas kernels  4.56 us (20%)
  waiting for transfers between devices  1.79 us (8%)
  other arithmetic  1.52 us (7%)
    ppermute x4, starting transfers between devices, neighbours(): first = lax.ppermute(outward, axis, near)  7 us
    ppermute x4, starting transfers between devices, neighbours(): second = lax.ppermute(inward, axis, far)  5.7 us
    pallas_call x1, Pallas kernels, per_device(): pl.pallas_call(functools.partial(advance_kernel, chain, corrected, rows),...  3.45 us
    ppermute x3, starting transfers between devices, from_lower(): return lax.ppermute(block, 'sec', route)  2.04 us
    ppermute x4, waiting for transfers between devices, neighbours(): second = lax.ppermute(inward, axis, far)  1.77 us
    pallas_call x1, Pallas kernels, per_device(): pl.pallas_call(functools.partial(first_kernel, chain, corrected, rows), o...  1.12 us
    convert_element_type x1, other arithmetic, per_device(): sent = block.astype(jnp.bfloat16)  1.07 us
  transfers between devices with their start and end apart: 11, of which 2 were waited for; matrix products, arithmetic and copies ran while one was open for 2% of the time, Pallas kernels for 5%

profile of v8, /device:TPU:3, one launch (start us, length us, event | category | flops | bytes accessed | tf_op | source)
XLA Modules:
  0.0 22.9 jit_solution(11190275151288311277)
XLA Ops:
  0.0 0.0 copy-start.1
  0.0 1.1 %convert_bitcast_fusion = (bf16[5,32,256]{2,1,0:T(8,128)(2,1)S(1)}, f32[5,32,256]{2,1,0:T(8,128)S(1)}) fusion(f32[1,5,32,256]{3,2,1,0:T(8,128)} %param.3), kind=kLoop, calls=%fused_computation.24 | loop fusion | flops 81920 | bytes 409600 | tf_op jit(solution)/shard_map/convert_element_type | solution.py:413
  1.1 1.4 %collective-permute-start.1 = (bf16[5,32,256]{2,1,0:T(8,128)(2,1)S(1)}, bf16[5,32,256]{2,1,0:T(8,128)(2,1)S(1)}, u32[]{:S(2)}, u32[]{:S(2)}) collective-permute-start(bf16[5,32,256]{2,1,0:T(8,128)(2,1)S(1)} %get-tuple-element.13), channel_id=1, source_target_pairs={{0,1},{1,0},{2,3},{3,2},{4,5},{5,4},{6,7},{7,6},{8,9},{9,8},{10,11... | collective-permute-start | bytes 245768 | tf_op jit(solution)/shard_map/ppermute | solution.py:42
  2.4 0.3 %collective-permute-start.2 = (bf16[5,32,256]{2,1,0:T(8,128)(2,1)S(1)}, bf16[5,32,256]{2,1,0:T(8,128)(2,1)S(1)}, u32[]{:S(2)}, u32[]{:S(2)}) collective-permute-start(bf16[5,32,256]{2,1,0:T(8,128)(2,1)S(1)} %get-tuple-element.13), channel_id=1, source_target_pairs={{0,16},{16,0},{1,17},{17,1},{2,18},{18,2},{3,19},{19,3},{4,20},{20... | collective-permute-start | bytes 245768 | tf_op jit(solution)/shard_map/ppermute | solution.py:51
  2.7 2.2 %collective-permute-start = (bf16[5,32,256]{2,1,0:T(8,128)(2,1)S(1)}, bf16[5,32,256]{2,1,0:T(8,128)(2,1)S(1)}, u32[]{:S(2)}, u32[]{:S(2)}) collective-permute-start(bf16[5,32,256]{2,1,0:T(8,128)(2,1)S(1)} %get-tuple-element.13), channel_id=1, source_target_pairs={{0,3},{1,2},{2,1},{3,0},{4,7},{5,6},{6,5},{7,4},{8,11},{9,10},{10,... | collective-permute-start | bytes 245768 | tf_op jit(solution)/shard_map/ppermute | solution.py:41
  4.9 0.0 copy-done.1
  4.9 0.1 fusion.5
  5.0 0.5 %collective-permute-start.5 = (bf16[10,32,128]{2,1,0:T(8,128)(2,1)S(1)}, bf16[10,32,128]{2,1,0:T(8,128)(2,1)S(1)}, u32[]{:S(2)}, u32[]{:S(2)}) collective-permute-start(bf16[10,32,128]{2,1,0:T(8,128)(2,1)S(1)} %get-tuple-element.34), channel_id=1, source_target_pairs={{0,1},{1,0},{2,3},{3,2},{4,5},{5,4},{6,7},{7,6},{8,9},{9,8},{10,11... | collective-permute-start | bytes 245768 | tf_op jit(solution)/shard_map/ppermute | solution.py:42
  5.5 0.9 %collective-permute-start.6 = (bf16[10,32,128]{2,1,0:T(8,128)(2,1)S(1)}, bf16[10,32,128]{2,1,0:T(8,128)(2,1)S(1)}, u32[]{:S(2)}, u32[]{:S(2)}) collective-permute-start(bf16[10,32,128]{2,1,0:T(8,128)(2,1)S(1)} %get-tuple-element.33), channel_id=1, source_target_pairs={{0,3},{1,2},{2,1},{3,0},{4,7},{5,6},{6,5},{7,4},{8,11},{9,10},{10,... | collective-permute-start | bytes 245768 | tf_op jit(solution)/shard_map/ppermute | solution.py:41
  6.5 0.0 collective-permute-done.1.refs_5_
  6.5 0.0 collective-permute-done.2.refs_10_
  6.5 1.3 %collective-permute-start.7 = (bf16[5,32,256]{2,1,0:T(8,128)(2,1)S(1)}, bf16[5,32,256]{2,1,0:T(8,128)(2,1)S(1)}, u32[]{:S(2)}, u32[]{:S(2)}) collective-permute-start(bf16[5,32,256]{2,1,0:T(8,128)(2,1)S(1)} %collective-permute-done.1.refs_5_), channel_id=1, source_target_pairs={{0,16},{16,0},{1,17},{17,1},{2,18},{18,2},{3,19},{19,3},{4,20},{20... | collective-permute-start | bytes 245768 | tf_op jit(solution)/shard_map/ppermute | solution.py:51
  7.8 0.8 %collective-permute-done.refs_6_ = bf16[5,32,256]{2,1,0:T(8,128)(2,1)S(1)} collective-permute-done((bf16[5,32,256]{2,1,0:T(8,128)(2,1)S(1)}, bf16[5,32,256]{2,1,0:T(8,128)(2,1)S(1)}, u32[]{:S(2)}, u32[]{:S(2)}) %collective-permute-start) | collective-permute-done | bytes 81952 | tf_op jit(solution)/shard_map/ppermute | solution.py:41
  8.6 0.1 broadcast_select_fusion.6
  8.7 0.5 %collective-permute-start.8 = (bf16[5,32,256]{2,1,0:T(8,128)(2,1)S(1)}, bf16[5,32,256]{2,1,0:T(8,128)(2,1)S(1)}, u32[]{:S(2)}, u32[]{:S(2)}) collective-permute-start(bf16[5,32,256]{2,1,0:T(8,128)(2,1)S(1)} %collective-permute-done.refs_6_), channel_id=1, source_target_pairs={{0,16},{16,0},{1,17},{17,1},{2,18},{18,2},{3,19},{19,3},{4,20},{20... | collective-permute-start | bytes 245768 | tf_op jit(solution)/shard_map/ppermute | solution.py:51
  9.2 2.8 %collective-permute-start.3 = (bf16[5,6,512]{2,1,0:T(8,128)(2,1)S(1)}, bf16[5,6,512]{2,1,0:T(8,128)(2,1)S(1)}, u32[]{:S(2)}, u32[]{:S(2)}) collective-permute-start(bf16[5,6,512]{2,1,0:T(8,128)(2,1)S(1)} %broadcast_select_fusion.7), channel_id=1, source_target_pairs={{0,4},{4,0},{8,12},{12,8},{1,5},{5,1},{9,13},{13,9},{2,6},{6,2},{1... | collective-permute-start | bytes 92168 | tf_op jit(solution)/shard_map/ppermute | solution.py:42
  12.1 0.0 collective-permute-done.5.refs_8_
  12.1 1.4 %collective-permute-start.4 = (bf16[5,6,512]{2,1,0:T(8,128)(2,1)S(1)}, bf16[5,6,512]{2,1,0:T(8,128)(2,1)S(1)}, u32[]{:S(2)}, u32[]{:S(2)}) collective-permute-start(bf16[5,6,512]{2,1,0:T(8,128)(2,1)S(1)} %get-tuple-element.24), channel_id=1, source_target_pairs={{0,12},{4,8},{8,4},{12,0},{1,13},{5,9},{9,5},{13,1},{2,14},{6,10},... | collective-permute-start | bytes 92168 | tf_op jit(solution)/shard_map/ppermute | solution.py:41
  13.5 0.0 collective-permute-done.6.refs_9_
  13.5 0.0 collective-permute-done.7.refs_11_
  13.5 0.0 collective-permute-done.8.refs_12_
  13.5 0.0 copy-start
  13.5 0.1 broadcast_select_fusion.4
  13.6 2.3 %collective-permute-start.9 = (bf16[5,8,512]{2,1,0:T(8,128)(2,1)S(1)}, bf16[5,8,512]{2,1,0:T(8,128)(2,1)S(1)}, u32[]{:S(2)}, u32[]{:S(2)}) collective-permute-start(bf16[5,8,512]{2,1,0:T(8,128)(2,1)S(1)} %broadcast_select_fusion.5), channel_id=1, source_target_pairs={{0,4},{4,0},{8,12},{12,8},{1,5},{5,1},{9,13},{13,9},{2,6},{6,2},{1... | collective-permute-start | bytes 122888 | tf_op jit(solution)/shard_map/ppermute | solution.py:42
  16.0 1.2 %collective-permute-start.10 = (bf16[5,8,512]{2,1,0:T(8,128)(2,1)S(1)}, bf16[5,8,512]{2,1,0:T(8,128)(2,1)S(1)}, u32[]{:S(2)}, u32[]{:S(2)}) collective-permute-start(bf16[5,8,512]{2,1,0:T(8,128)(2,1)S(1)} %get-tuple-element.21), channel_id=1, source_target_pairs={{0,12},{4,8},{8,4},{12,0},{1,13},{5,9},{9,5},{13,1},{2,14},{6,10},... | collective-permute-start | bytes 122888 | tf_op jit(solution)/shard_map/ppermute | solution.py:41
  17.2 0.1 pad_add_fusion.refs_0_
  17.3 0.0 collective-permute-done.3
  17.3 0.0 collective-permute-done.4
  17.3 0.0 copy-done
  17.3 1.1 %own_first_tick.1.refs_2_ = f32[5,4,40,128]{3,2,1,0:T(8,128)S(1)} custom-call(s32[3]{0:T(128)S(1)} %pad_add_fusion.refs_0_, bf16[1024,256]{1,0:T(8,128)(2,1)S(1)} %copy-done, f32[5,6,512]{2,1,0:T(8,128)S(1)} %convert_element_type.29.refs_2_.refs_3_, f32[5,6,512]{2,1,0:T(8,128)S(1)} %convert_element_type.30.refs_3_.refs_4_, ...), custom_call_target="tpu_custom_call" | custom-call | tf_op jit(solution)/shard_map/own_first_tick/pallas_call | solution.py:488
  18.4 0.0 collective-permute-done.9
  18.5 1.0 %collective-permute-done.10 = bf16[5,8,512]{2,1,0:T(8,128)(2,1)S(1)} collective-permute-done((bf16[5,8,512]{2,1,0:T(8,128)(2,1)S(1)}, bf16[5,8,512]{2,1,0:T(8,128)(2,1)S(1)}, u32[]{:S(2)}, u32[]{:S(2)}) %collective-permute-start.10) | collective-permute-done | bytes 40992 | tf_op jit(solution)/shard_map/ppermute | solution.py:41
  19.4 3.4 %advance.1 = f32[5,32,256]{2,1,0:T(8,128)} custom-call(s32[3]{0:T(128)S(1)} %pad_add_fusion.refs_0_, bf16[1024,256]{1,0:T(8,128)(2,1)S(1)} %copy-done, f32[5,4,40,128]{3,2,1,0:T(8,128)S(1)} %own_first_tick.1.refs_2_, f32[5,6,512]{2,1,0:T(8,128)S(1)} %convert_element_type.29.refs_2_.refs_3_, f32[5,6,512]{2,1,0:T(8,128)S(1)} %convert_element_type.30.refs_3_.refs_4_, ...), custom_call_target="tpu_custom_call" | custom-call | tf_op jit(solution)/shard_map/advance/pallas_call | solution.py:498
  (15 shorter events, 0.2 us)
Async XLA Ops:
  0.0 4.9 %copy-start.1 = (bf16[1,3,5,32,256]{4,3,2,1,0:T(8,128)(2,1)S(1)}, bf16[1,3,5,32,256]{4,3,2,1,0:T(8,128)(2,1)}, u32[]{:S(2)}) copy-start(bf16[1,3,5,32,256]{4,3,2,1,0:T(8,128)(2,1)} %param.4) | copy-start | bytes 737284
  1.1 5.4 %collective-permute-start.1 = (bf16[5,32,256]{2,1,0:T(8,128)(2,1)S(1)}, bf16[5,32,256]{2,1,0:T(8,128)(2,1)S(1)}, u32[]{:S(2)}, u32[]{:S(2)}) collective-permute-start(bf16[5,32,256]{2,1,0:T(8,128)(2,1)S(1)} %get-tuple-element.13), channel_id=1, source_target_pairs={{0,1},{1,0},{2,3},{3,2},{4,5},{5,4},{6,7},{7,6},{8,9},{9,8},{10,11... | collective-permute-start | bytes 245768 | tf_op jit(solution)/shard_map/ppermute | solution.py:42
  2.4 4.1 %collective-permute-start.2 = (bf16[5,32,256]{2,1,0:T(8,128)(2,1)S(1)}, bf16[5,32,256]{2,1,0:T(8,128)(2,1)S(1)}, u32[]{:S(2)}, u32[]{:S(2)}) collective-permute-start(bf16[5,32,256]{2,1,0:T(8,128)(2,1)S(1)} %get-tuple-element.13), channel_id=1, source_target_pairs={{0,16},{16,0},{1,17},{17,1},{2,18},{18,2},{3,19},{19,3},{4,20},{20... | collective-permute-start | bytes 245768 | tf_op jit(solution)/shard_map/ppermute | solution.py:51
  2.7 5.9 %collective-permute-start = (bf16[5,32,256]{2,1,0:T(8,128)(2,1)S(1)}, bf16[5,32,256]{2,1,0:T(8,128)(2,1)S(1)}, u32[]{:S(2)}, u32[]{:S(2)}) collective-permute-start(bf16[5,32,256]{2,1,0:T(8,128)(2,1)S(1)} %get-tuple-element.13), channel_id=1, source_target_pairs={{0,3},{1,2},{2,1},{3,0},{4,7},{5,6},{6,5},{7,4},{8,11},{9,10},{10,... | collective-permute-start | bytes 245768 | tf_op jit(solution)/shard_map/ppermute | solution.py:41
  5.0 7.0 %collective-permute-start.5 = (bf16[10,32,128]{2,1,0:T(8,128)(2,1)S(1)}, bf16[10,32,128]{2,1,0:T(8,128)(2,1)S(1)}, u32[]{:S(2)}, u32[]{:S(2)}) collective-permute-start(bf16[10,32,128]{2,1,0:T(8,128)(2,1)S(1)} %get-tuple-element.34), channel_id=1, source_target_pairs={{0,1},{1,0},{2,3},{3,2},{4,5},{5,4},{6,7},{7,6},{8,9},{9,8},{10,11... | collective-permute-start | bytes 245768 | tf_op jit(solution)/shard_map/ppermute | solution.py:42
  5.5 8.0 %collective-permute-start.6 = (bf16[10,32,128]{2,1,0:T(8,128)(2,1)S(1)}, bf16[10,32,128]{2,1,0:T(8,128)(2,1)S(1)}, u32[]{:S(2)}, u32[]{:S(2)}) collective-permute-start(bf16[10,32,128]{2,1,0:T(8,128)(2,1)S(1)} %get-tuple-element.33), channel_id=1, source_target_pairs={{0,3},{1,2},{2,1},{3,0},{4,7},{5,6},{6,5},{7,4},{8,11},{9,10},{10,... | collective-permute-start | bytes 245768 | tf_op jit(solution)/shard_map/ppermute | solution.py:41
  6.5 7.0 %collective-permute-start.7 = (bf16[5,32,256]{2,1,0:T(8,128)(2,1)S(1)}, bf16[5,32,256]{2,1,0:T(8,128)(2,1)S(1)}, u32[]{:S(2)}, u32[]{:S(2)}) collective-permute-start(bf16[5,32,256]{2,1,0:T(8,128)(2,1)S(1)} %collective-permute-done.1.refs_5_), channel_id=1, source_target_pairs={{0,16},{16,0},{1,17},{17,1},{2,18},{18,2},{3,19},{19,3},{4,20},{20... | collective-permute-start | bytes 245768 | tf_op jit(solution)/shard_map/ppermute | solution.py:51
  8.7 4.8 %collective-permute-start.8 = (bf16[5,32,256]{2,1,0:T(8,128)(2,1)S(1)}, bf16[5,32,256]{2,1,0:T(8,128)(2,1)S(1)}, u32[]{:S(2)}, u32[]{:S(2)}) collective-permute-start(bf16[5,32,256]{2,1,0:T(8,128)(2,1)S(1)} %collective-permute-done.refs_6_), channel_id=1, source_target_pairs={{0,16},{16,0},{1,17},{17,1},{2,18},{18,2},{3,19},{19,3},{4,20},{20... | collective-permute-start | bytes 245768 | tf_op jit(solution)/shard_map/ppermute | solution.py:51
  9.2 8.0 %collective-permute-start.3 = (bf16[5,6,512]{2,1,0:T(8,128)(2,1)S(1)}, bf16[5,6,512]{2,1,0:T(8,128)(2,1)S(1)}, u32[]{:S(2)}, u32[]{:S(2)}) collective-permute-start(bf16[5,6,512]{2,1,0:T(8,128)(2,1)S(1)} %broadcast_select_fusion.7), channel_id=1, source_target_pairs={{0,4},{4,0},{8,12},{12,8},{1,5},{5,1},{9,13},{13,9},{2,6},{6,2},{1... | collective-permute-start | bytes 92168 | tf_op jit(solution)/shard_map/ppermute | solution.py:42
  12.1 5.2 %collective-permute-start.4 = (bf16[5,6,512]{2,1,0:T(8,128)(2,1)S(1)}, bf16[5,6,512]{2,1,0:T(8,128)(2,1)S(1)}, u32[]{:S(2)}, u32[]{:S(2)}) collective-permute-start(bf16[5,6,512]{2,1,0:T(8,128)(2,1)S(1)} %get-tuple-element.24), channel_id=1, source_target_pairs={{0,12},{4,8},{8,4},{12,0},{1,13},{5,9},{9,5},{13,1},{2,14},{6,10},... | collective-permute-start | bytes 92168 | tf_op jit(solution)/shard_map/ppermute | solution.py:41
  13.5 3.8 %copy-start = (bf16[1024,256]{1,0:T(8,128)(2,1)S(1)}, bf16[1024,256]{1,0:T(8,128)(2,1)}, u32[]{:S(2)}) copy-start(bf16[1024,256]{1,0:T(8,128)(2,1)} %constant.41.clone.refs_1_) | copy-start | bytes 1572868
  13.6 4.8 %collective-permute-start.9 = (bf16[5,8,512]{2,1,0:T(8,128)(2,1)S(1)}, bf16[5,8,512]{2,1,0:T(8,128)(2,1)S(1)}, u32[]{:S(2)}, u32[]{:S(2)}) collective-permute-start(bf16[5,8,512]{2,1,0:T(8,128)(2,1)S(1)} %broadcast_select_fusion.5), channel_id=1, source_target_pairs={{0,4},{4,0},{8,12},{12,8},{1,5},{5,1},{9,13},{13,9},{2,6},{6,2},{1... | collective-permute-start | bytes 122888 | tf_op jit(solution)/shard_map/ppermute | solution.py:42
  16.0 3.4 %collective-permute-start.10 = (bf16[5,8,512]{2,1,0:T(8,128)(2,1)S(1)}, bf16[5,8,512]{2,1,0:T(8,128)(2,1)S(1)}, u32[]{:S(2)}, u32[]{:S(2)}) collective-permute-start(bf16[5,8,512]{2,1,0:T(8,128)(2,1)S(1)} %get-tuple-element.21), channel_id=1, source_target_pairs={{0,12},{4,8},{8,4},{12,0},{1,13},{5,9},{9,5},{13,1},{2,14},{6,10},... | collective-permute-start | bytes 122888 | tf_op jit(solution)/shard_map/ppermute | solution.py:41

commit v9 on v8

--- a/solution.py
+++ b/solution.py
@@ -290,19 +290,26 @@
     return sources, row + 2 * ((len(narrow) + 1) // 2)
 
 
+def whereabouts():
+    def even(axis):
+        return lax.axis_index(axis) % 2 == 0 if lax.axis_size(axis) % 2 == 0 else jnp.bool_(True)
+
+    return even("gx"), even("gy"), lax.axis_index("sec") % min(4, lax.axis_size("sec"))
+
+
 def first_kernel(chain, corrected, rows, *refs):
-    flags, matrix, x_first, x_second, center, y_first, y_second, out, edges, *scratch = refs
-    even_x = flags[0] == 1
+    matrix, x_first, x_second, center, y_first, y_second, out, edges, *scratch = refs
+    even_x, even_y, _ = whereabouts()
     pieces, _ = edge_layout(edge_turns(chain, corrected)[0])
     unpack_edges(edges, x_first, x_second, even_x)
-    level = Level(rows, even_x, flags[1] == 1, matrix, scratch)
+    level = Level(rows, even_x, even_y, matrix, scratch)
     level.assemble(center, y_first, y_second, edges, pieces["state", 0])
     for field, tile, rate in level.rates(level.products(0)):
         out[field, tile - 1] = level.state[field, tile, level.window, :] + (0.5 * TIME_STEP) * rate
 
 
 def advance_kernel(chain, corrected, rows, *refs):
-    flags, matrix, begun, *refs = refs
+    matrix, begun, *refs = refs
     came, refs = refs[:4], refs[4:]
     inputs = []
     for link in range(chain):
@@ -310,10 +317,9 @@
         stored, refs = (refs[:3], refs[3:]) if corrected[link] else (None, refs)
         inputs.append((state, stored))
     out, fresh, terms, edges, *refs = refs
-    even_x = flags[0] == 1
-    position = flags[2]
+    even_x, even_y, position = whereabouts()
     levels = [
-        Level(rows, even_x, flags[1] == 1, matrix, refs[5 * link : 5 * link + 5]) for link in range(chain)
+        Level(rows, even_x, even_y, matrix, refs[5 * link : 5 * link + 5]) for link in range(chain)
     ]
     window = levels[0].window
     layout = {}
@@ -401,9 +407,7 @@
 
 def per_device(fields, stored_rates):
     levels = min(4, lax.axis_size("sec"))
-    position = lax.axis_index("sec") % levels
-    even_x = lax.axis_index("gx") % 2 == 0 if lax.axis_size("gx") % 2 == 0 else jnp.bool_(True)
-    even_y = lax.axis_index("gy") % 2 == 0 if lax.axis_size("gy") % 2 == 0 else jnp.bool_(True)
+    even_x, even_y, _ = whereabouts()
     block = fields[0]
     stored = stored_rates[0]
     rows, columns = block.shape[1:]
@@ -477,10 +481,8 @@
             if link:
                 padded["kept", link, 1] = link_padded[FIELDS:]
     came += over_x(late)
-    flags = jnp.stack([even_x.astype(jnp.int32), even_y.astype(jnp.int32), position])
     matrix = jnp.asarray(stencil_matrix(), jnp.bfloat16)
     high, tall = rows + WINDOW, rows + 2 * FIRST
-    smem = pl.BlockSpec(memory_space=pltpu.SMEM)
     vmem = pl.BlockSpec(memory_space=pltpu.VMEM)
     params = pltpu.CompilerParams(vmem_limit_bytes=48 * 1024 * 1024)
     taken = max(edge_layout(kinds)[1] for kinds in (early, late))
@@ -488,17 +490,18 @@
     begun = pl.pallas_call(
         functools.partial(first_kernel, chain, corrected, rows),
         out_shape=jax.ShapeDtypeStruct((FIELDS, 4, high, LANES), jnp.float32),
-        in_specs=[smem] + [vmem] * 6,
+        in_specs=[vmem] * 6,
         out_specs=vmem,
         scratch_shapes=[pltpu.VMEM(edges, jnp.float32), *scratch_of_level(rows)],
         compiler_params=params,
+        cost_estimate=pl.CostEstimate(flops=4 * 10**8, bytes_accessed=10**6, transcendentals=0),
         name="own_first_tick",
-    )(flags, matrix, *came[:2], whole, *own_y)
+    )(matrix, *came[:2], whole, *own_y)
     operands = [begun, *came, *operands]
     result = pl.pallas_call(
         functools.partial(advance_kernel, chain, corrected, rows),
         out_shape=jax.ShapeDtypeStruct((FIELDS, rows, columns), jnp.float32),
-        in_specs=[smem] + [vmem] * (len(operands) + 1),
+        in_specs=[vmem] * (len(operands) + 1),
         out_specs=vmem,
         scratch_shapes=[
             pltpu.VMEM((chain, TICKS, FIELDS, 4, high, LANES), jnp.float32),
@@ -508,7 +511,7 @@
         ],
         compiler_params=params,
         name="advance",
-    )(flags, matrix, *operands)
+    )(matrix, *operands)
     return result[None]
 
 

time: 23 us -> 22.4 us (0.974)
  Pallas kernels: 4.56 us -> 3.38 us
  waiting for transfers between devices: 1.79 us -> 2.42 us
    pallas_call x1, Pallas kernels: 3.45 us -> 2.81 us  [per_device(): pl.pallas_call(functools.partial(advance_kernel, chain, corrected, rows),...]
    ppermute x4, waiting for transfers between devices: 1.77 us -> 2.4 us  [neighbours(): second = lax.ppermute(inward, axis, far)]
    pallas_call x1, Pallas kernels: 1.12 us -> 0.57 us  [per_device(): pl.pallas_call(functools.partial(first_kernel, chain, corrected, rows), o...]
  transfers between devices with their start and end apart: 11 -> 11, of which waited for: 2 -> 2; matrix products, arithmetic and copies ran while one was open for 2% -> 2% of each run, Pallas kernels for 5% -> 3%
where the time goes in v9:
time: 22.4 us; the launch traced here: 22.2 us
  starting transfers between devices  14.7 us (66%)
  Pallas kernels  3.38 us (15%)
  waiting for transfers between devices  2.42 us (11%)
  other arithmetic  1.44 us (6%)
    ppermute x4, starting transfers between devices, neighbours(): first = lax.ppermute(outward, axis, near)  7 us
    ppermute x4, starting transfers between devices, neighbours(): second = lax.ppermute(inward, axis, far)  5.7 us
    pallas_call x1, Pallas kernels, per_device(): pl.pallas_call(functools.partial(advance_kernel, chain, corrected, rows),...  2.81 us
    ppermute x4, waiting for transfers between devices, neighbours(): second = lax.ppermute(inward, axis, far)  2.4 us
    ppermute x3, starting transfers between devices, from_lower(): return lax.ppermute(block, 'sec', route)  2.04 us
    convert_element_type x1, other arithmetic, per_device(): sent = block.astype(jnp.bfloat16)  1.07 us
    pallas_call x1, Pallas kernels, per_device(): pl.pallas_call(functools.partial(first_kernel, chain, corrected, rows), o...  0.57 us
  transfers between devices with their start and end apart: 11, of which 2 were waited for; matrix products, arithmetic and copies ran while one was open for 2% of the time, Pallas kernels for 3%

profile of v9, /device:TPU:3, one launch (start us, length us, event | category | flops | bytes accessed | tf_op | source)
XLA Modules:
  0.0 22.2 jit_solution(17960129897767779537)
XLA Ops:
  0.0 0.0 copy-start
  0.0 1.1 %convert_bitcast_fusion = (bf16[5,32,256]{2,1,0:T(8,128)(2,1)S(1)}, f32[5,32,256]{2,1,0:T(8,128)S(1)}) fusion(f32[1,5,32,256]{3,2,1,0:T(8,128)} %param.3), kind=kLoop, calls=%fused_computation.24 | loop fusion | flops 81920 | bytes 409600 | tf_op jit(solution)/shard_map/convert_element_type | solution.py:417
  1.1 1.4 %collective-permute-start.1 = (bf16[5,32,256]{2,1,0:T(8,128)(2,1)S(1)}, bf16[5,32,256]{2,1,0:T(8,128)(2,1)S(1)}, u32[]{:S(2)}, u32[]{:S(2)}) collective-permute-start(bf16[5,32,256]{2,1,0:T(8,128)(2,1)S(1)} %get-tuple-element.13), channel_id=1, source_target_pairs={{0,1},{1,0},{2,3},{3,2},{4,5},{5,4},{6,7},{7,6},{8,9},{9,8},{10,11... | collective-permute-start | bytes 245768 | tf_op jit(solution)/shard_map/ppermute | solution.py:42
  2.4 0.3 %collective-permute-start.2 = (bf16[5,32,256]{2,1,0:T(8,128)(2,1)S(1)}, bf16[5,32,256]{2,1,0:T(8,128)(2,1)S(1)}, u32[]{:S(2)}, u32[]{:S(2)}) collective-permute-start(bf16[5,32,256]{2,1,0:T(8,128)(2,1)S(1)} %get-tuple-element.13), channel_id=1, source_target_pairs={{0,16},{16,0},{1,17},{17,1},{2,18},{18,2},{3,19},{19,3},{4,20},{20... | collective-permute-start | bytes 245768 | tf_op jit(solution)/shard_map/ppermute | solution.py:51
  2.7 2.2 %collective-permute-start = (bf16[5,32,256]{2,1,0:T(8,128)(2,1)S(1)}, bf16[5,32,256]{2,1,0:T(8,128)(2,1)S(1)}, u32[]{:S(2)}, u32[]{:S(2)}) collective-permute-start(bf16[5,32,256]{2,1,0:T(8,128)(2,1)S(1)} %get-tuple-element.13), channel_id=1, source_target_pairs={{0,3},{1,2},{2,1},{3,0},{4,7},{5,6},{6,5},{7,4},{8,11},{9,10},{10,... | collective-permute-start | bytes 245768 | tf_op jit(solution)/shard_map/ppermute | solution.py:41
  4.9 0.0 copy-done
  4.9 0.1 fusion.5
  5.0 0.5 %collective-permute-start.5 = (bf16[10,32,128]{2,1,0:T(8,128)(2,1)S(1)}, bf16[10,32,128]{2,1,0:T(8,128)(2,1)S(1)}, u32[]{:S(2)}, u32[]{:S(2)}) collective-permute-start(bf16[10,32,128]{2,1,0:T(8,128)(2,1)S(1)} %get-tuple-element.34), channel_id=1, source_target_pairs={{0,1},{1,0},{2,3},{3,2},{4,5},{5,4},{6,7},{7,6},{8,9},{9,8},{10,11... | collective-permute-start | bytes 245768 | tf_op jit(solution)/shard_map/ppermute | solution.py:42
  5.5 0.9 %collective-permute-start.6 = (bf16[10,32,128]{2,1,0:T(8,128)(2,1)S(1)}, bf16[10,32,128]{2,1,0:T(8,128)(2,1)S(1)}, u32[]{:S(2)}, u32[]{:S(2)}) collective-permute-start(bf16[10,32,128]{2,1,0:T(8,128)(2,1)S(1)} %get-tuple-element.33), channel_id=1, source_target_pairs={{0,3},{1,2},{2,1},{3,0},{4,7},{5,6},{6,5},{7,4},{8,11},{9,10},{10,... | collective-permute-start | bytes 245768 | tf_op jit(solution)/shard_map/ppermute | solution.py:41
  6.5 0.0 collective-permute-done.1.refs_4_
  6.5 0.0 collective-permute-done.2.refs_9_
  6.5 1.3 %collective-permute-start.7 = (bf16[5,32,256]{2,1,0:T(8,128)(2,1)S(1)}, bf16[5,32,256]{2,1,0:T(8,128)(2,1)S(1)}, u32[]{:S(2)}, u32[]{:S(2)}) collective-permute-start(bf16[5,32,256]{2,1,0:T(8,128)(2,1)S(1)} %collective-permute-done.1.refs_4_), channel_id=1, source_target_pairs={{0,16},{16,0},{1,17},{17,1},{2,18},{18,2},{3,19},{19,3},{4,20},{20... | collective-permute-start | bytes 245768 | tf_op jit(solution)/shard_map/ppermute | solution.py:51
  7.8 0.8 %collective-permute-done.refs_5_ = bf16[5,32,256]{2,1,0:T(8,128)(2,1)S(1)} collective-permute-done((bf16[5,32,256]{2,1,0:T(8,128)(2,1)S(1)}, bf16[5,32,256]{2,1,0:T(8,128)(2,1)S(1)}, u32[]{:S(2)}, u32[]{:S(2)}) %collective-permute-start) | collective-permute-done | bytes 81952 | tf_op jit(solution)/shard_map/ppermute | solution.py:41
  8.6 0.1 broadcast_select_fusion.6
  8.7 0.5 %collective-permute-start.8 = (bf16[5,32,256]{2,1,0:T(8,128)(2,1)S(1)}, bf16[5,32,256]{2,1,0:T(8,128)(2,1)S(1)}, u32[]{:S(2)}, u32[]{:S(2)}) collective-permute-start(bf16[5,32,256]{2,1,0:T(8,128)(2,1)S(1)} %collective-permute-done.refs_5_), channel_id=1, source_target_pairs={{0,16},{16,0},{1,17},{17,1},{2,18},{18,2},{3,19},{19,3},{4,20},{20... | collective-permute-start | bytes 245768 | tf_op jit(solution)/shard_map/ppermute | solution.py:51
  9.2 2.8 %collective-permute-start.3 = (bf16[5,6,512]{2,1,0:T(8,128)(2,1)S(1)}, bf16[5,6,512]{2,1,0:T(8,128)(2,1)S(1)}, u32[]{:S(2)}, u32[]{:S(2)}) collective-permute-start(bf16[5,6,512]{2,1,0:T(8,128)(2,1)S(1)} %broadcast_select_fusion.7), channel_id=1, source_target_pairs={{0,4},{4,0},{8,12},{12,8},{1,5},{5,1},{9,13},{13,9},{2,6},{6,2},{1... | collective-permute-start | bytes 92168 | tf_op jit(solution)/shard_map/ppermute | solution.py:42
  12.1 0.0 collective-permute-done.5.refs_7_
  12.1 1.4 %collective-permute-start.4 = (bf16[5,6,512]{2,1,0:T(8,128)(2,1)S(1)}, bf16[5,6,512]{2,1,0:T(8,128)(2,1)S(1)}, u32[]{:S(2)}, u32[]{:S(2)}) collective-permute-start(bf16[5,6,512]{2,1,0:T(8,128)(2,1)S(1)} %get-tuple-element.24), channel_id=1, source_target_pairs={{0,12},{4,8},{8,4},{12,0},{1,13},{5,9},{9,5},{13,1},{2,14},{6,10},... | collective-permute-start | bytes 92168 | tf_op jit(solution)/shard_map/ppermute | solution.py:41
  13.5 0.0 collective-permute-done.6.refs_8_
  13.5 0.0 collective-permute-done.7.refs_10_
  13.5 0.0 collective-permute-done.8.refs_11_
  13.5 0.0 copy-start.1
  13.5 0.1 broadcast_select_fusion.4
  13.6 2.3 %collective-permute-start.9 = (bf16[5,8,512]{2,1,0:T(8,128)(2,1)S(1)}, bf16[5,8,512]{2,1,0:T(8,128)(2,1)S(1)}, u32[]{:S(2)}, u32[]{:S(2)}) collective-permute-start(bf16[5,8,512]{2,1,0:T(8,128)(2,1)S(1)} %broadcast_select_fusion.5), channel_id=1, source_target_pairs={{0,4},{4,0},{8,12},{12,8},{1,5},{5,1},{9,13},{13,9},{2,6},{6,2},{1... | collective-permute-start | bytes 122888 | tf_op jit(solution)/shard_map/ppermute | solution.py:42
  16.0 1.2 %collective-permute-start.10 = (bf16[5,8,512]{2,1,0:T(8,128)(2,1)S(1)}, bf16[5,8,512]{2,1,0:T(8,128)(2,1)S(1)}, u32[]{:S(2)}, u32[]{:S(2)}) collective-permute-start(bf16[5,8,512]{2,1,0:T(8,128)(2,1)S(1)} %get-tuple-element.21), channel_id=1, source_target_pairs={{0,12},{4,8},{8,4},{12,0},{1,13},{5,9},{9,5},{13,1},{2,14},{6,10},... | collective-permute-start | bytes 122888 | tf_op jit(solution)/shard_map/ppermute | solution.py:41
  17.2 0.0 collective-permute-done.3
  17.2 0.0 collective-permute-done.4
  17.2 0.0 copy-done.1
  17.2 0.6 %own_first_tick.1.refs_1_ = f32[5,4,40,128]{3,2,1,0:T(8,128)S(1)} custom-call(bf16[1024,256]{1,0:T(8,128)(2,1)S(1)} %copy-done.1, f32[5,6,512]{2,1,0:T(8,128)S(1)} %convert_element_type.27.refs_1_.refs_2_, f32[5,6,512]{2,1,0:T(8,128)S(1)} %convert_element_type.28.refs_2_.refs_3_, f32[5,32,256]{2,1,0:T(8,128)S(1)} %get-tuple-element.15.refs_3_, ...), custom_call_target="tpu_custom_call" | custom-call | flops 400000000 | bytes 1000000 | tf_op jit(solution)/shard_map/own_first_tick/pallas_call | solution.py:490
  17.8 0.0 collective-permute-done.9
  17.8 1.6 %collective-permute-done.10 = bf16[5,8,512]{2,1,0:T(8,128)(2,1)S(1)} collective-permute-done((bf16[5,8,512]{2,1,0:T(8,128)(2,1)S(1)}, bf16[5,8,512]{2,1,0:T(8,128)(2,1)S(1)}, u32[]{:S(2)}, u32[]{:S(2)}) %collective-permute-start.10) | collective-permute-done | bytes 40992 | tf_op jit(solution)/shard_map/ppermute | solution.py:41
  19.4 2.8 %advance.1 = f32[5,32,256]{2,1,0:T(8,128)} custom-call(bf16[1024,256]{1,0:T(8,128)(2,1)S(1)} %copy-done.1, f32[5,4,40,128]{3,2,1,0:T(8,128)S(1)} %own_first_tick.1.refs_1_, f32[5,6,512]{2,1,0:T(8,128)S(1)} %convert_element_type.27.refs_1_.refs_2_, f32[5,6,512]{2,1,0:T(8,128)S(1)} %convert_element_type.28.refs_2_.refs_3_, ...), custom_call_target="tpu_custom_call" | custom-call | tf_op jit(solution)/shard_map/advance/pallas_call | solution.py:501
  (15 shorter events, 0.2 us)
Async XLA Ops:
  0.0 4.9 %copy-start = (bf16[1,3,5,32,256]{4,3,2,1,0:T(8,128)(2,1)S(1)}, bf16[1,3,5,32,256]{4,3,2,1,0:T(8,128)(2,1)}, u32[]{:S(2)}) copy-start(bf16[1,3,5,32,256]{4,3,2,1,0:T(8,128)(2,1)} %param.4) | copy-start | bytes 737284
  1.1 5.4 %collective-permute-start.1 = (bf16[5,32,256]{2,1,0:T(8,128)(2,1)S(1)}, bf16[5,32,256]{2,1,0:T(8,128)(2,1)S(1)}, u32[]{:S(2)}, u32[]{:S(2)}) collective-permute-start(bf16[5,32,256]{2,1,0:T(8,128)(2,1)S(1)} %get-tuple-element.13), channel_id=1, source_target_pairs={{0,1},{1,0},{2,3},{3,2},{4,5},{5,4},{6,7},{7,6},{8,9},{9,8},{10,11... | collective-permute-start | bytes 245768 | tf_op jit(solution)/shard_map/ppermute | solution.py:42
  2.4 4.1 %collective-permute-start.2 = (bf16[5,32,256]{2,1,0:T(8,128)(2,1)S(1)}, bf16[5,32,256]{2,1,0:T(8,128)(2,1)S(1)}, u32[]{:S(2)}, u32[]{:S(2)}) collective-permute-start(bf16[5,32,256]{2,1,0:T(8,128)(2,1)S(1)} %get-tuple-element.13), channel_id=1, source_target_pairs={{0,16},{16,0},{1,17},{17,1},{2,18},{18,2},{3,19},{19,3},{4,20},{20... | collective-permute-start | bytes 245768 | tf_op jit(solution)/shard_map/ppermute | solution.py:51
  2.7 5.9 %collective-permute-start = (bf16[5,32,256]{2,1,0:T(8,128)(2,1)S(1)}, bf16[5,32,256]{2,1,0:T(8,128)(2,1)S(1)}, u32[]{:S(2)}, u32[]{:S(2)}) collective-permute-start(bf16[5,32,256]{2,1,0:T(8,128)(2,1)S(1)} %get-tuple-element.13), channel_id=1, source_target_pairs={{0,3},{1,2},{2,1},{3,0},{4,7},{5,6},{6,5},{7,4},{8,11},{9,10},{10,... | collective-permute-start | bytes 245768 | tf_op jit(solution)/shard_map/ppermute | solution.py:41
  5.0 7.0 %collective-permute-start.5 = (bf16[10,32,128]{2,1,0:T(8,128)(2,1)S(1)}, bf16[10,32,128]{2,1,0:T(8,128)(2,1)S(1)}, u32[]{:S(2)}, u32[]{:S(2)}) collective-permute-start(bf16[10,32,128]{2,1,0:T(8,128)(2,1)S(1)} %get-tuple-element.34), channel_id=1, source_target_pairs={{0,1},{1,0},{2,3},{3,2},{4,5},{5,4},{6,7},{7,6},{8,9},{9,8},{10,11... | collective-permute-start | bytes 245768 | tf_op jit(solution)/shard_map/ppermute | solution.py:42
  5.5 8.0 %collective-permute-start.6 = (bf16[10,32,128]{2,1,0:T(8,128)(2,1)S(1)}, bf16[10,32,128]{2,1,0:T(8,128)(2,1)S(1)}, u32[]{:S(2)}, u32[]{:S(2)}) collective-permute-start(bf16[10,32,128]{2,1,0:T(8,128)(2,1)S(1)} %get-tuple-element.33), channel_id=1, source_target_pairs={{0,3},{1,2},{2,1},{3,0},{4,7},{5,6},{6,5},{7,4},{8,11},{9,10},{10,... | collective-permute-start | bytes 245768 | tf_op jit(solution)/shard_map/ppermute | solution.py:41
  6.5 7.0 %collective-permute-start.7 = (bf16[5,32,256]{2,1,0:T(8,128)(2,1)S(1)}, bf16[5,32,256]{2,1,0:T(8,128)(2,1)S(1)}, u32[]{:S(2)}, u32[]{:S(2)}) collective-permute-start(bf16[5,32,256]{2,1,0:T(8,128)(2,1)S(1)} %collective-permute-done.1.refs_4_), channel_id=1, source_target_pairs={{0,16},{16,0},{1,17},{17,1},{2,18},{18,2},{3,19},{19,3},{4,20},{20... | collective-permute-start | bytes 245768 | tf_op jit(solution)/shard_map/ppermute | solution.py:51
  8.7 4.8 %collective-permute-start.8 = (bf16[5,32,256]{2,1,0:T(8,128)(2,1)S(1)}, bf16[5,32,256]{2,1,0:T(8,128)(2,1)S(1)}, u32[]{:S(2)}, u32[]{:S(2)}) collective-permute-start(bf16[5,32,256]{2,1,0:T(8,128)(2,1)S(1)} %collective-permute-done.refs_5_), channel_id=1, source_target_pairs={{0,16},{16,0},{1,17},{17,1},{2,18},{18,2},{3,19},{19,3},{4,20},{20... | collective-permute-start | bytes 245768 | tf_op jit(solution)/shard_map/ppermute | solution.py:51
  9.2 8.0 %collective-permute-start.3 = (bf16[5,6,512]{2,1,0:T(8,128)(2,1)S(1)}, bf16[5,6,512]{2,1,0:T(8,128)(2,1)S(1)}, u32[]{:S(2)}, u32[]{:S(2)}) collective-permute-start(bf16[5,6,512]{2,1,0:T(8,128)(2,1)S(1)} %broadcast_select_fusion.7), channel_id=1, source_target_pairs={{0,4},{4,0},{8,12},{12,8},{1,5},{5,1},{9,13},{13,9},{2,6},{6,2},{1... | collective-permute-start | bytes 92168 | tf_op jit(solution)/shard_map/ppermute | solution.py:42
  12.1 5.1 %collective-permute-start.4 = (bf16[5,6,512]{2,1,0:T(8,128)(2,1)S(1)}, bf16[5,6,512]{2,1,0:T(8,128)(2,1)S(1)}, u32[]{:S(2)}, u32[]{:S(2)}) collective-permute-start(bf16[5,6,512]{2,1,0:T(8,128)(2,1)S(1)} %get-tuple-element.24), channel_id=1, source_target_pairs={{0,12},{4,8},{8,4},{12,0},{1,13},{5,9},{9,5},{13,1},{2,14},{6,10},... | collective-permute-start | bytes 92168 | tf_op jit(solution)/shard_map/ppermute | solution.py:41
  13.5 3.7 %copy-start.1 = (bf16[1024,256]{1,0:T(8,128)(2,1)S(1)}, bf16[1024,256]{1,0:T(8,128)(2,1)}, u32[]{:S(2)}) copy-start(bf16[1024,256]{1,0:T(8,128)(2,1)} %constant.31.clone.refs_0_) | copy-start | bytes 1572868
  13.6 4.2 %collective-permute-start.9 = (bf16[5,8,512]{2,1,0:T(8,128)(2,1)S(1)}, bf16[5,8,512]{2,1,0:T(8,128)(2,1)S(1)}, u32[]{:S(2)}, u32[]{:S(2)}) collective-permute-start(bf16[5,8,512]{2,1,0:T(8,128)(2,1)S(1)} %broadcast_select_fusion.5), channel_id=1, source_target_pairs={{0,4},{4,0},{8,12},{12,8},{1,5},{5,1},{9,13},{13,9},{2,6},{6,2},{1... | collective-permute-start | bytes 122888 | tf_op jit(solution)/shard_map/ppermute | solution.py:42
  16.0 3.4 %collective-permute-start.10 = (bf16[5,8,512]{2,1,0:T(8,128)(2,1)S(1)}, bf16[5,8,512]{2,1,0:T(8,128)(2,1)S(1)}, u32[]{:S(2)}, u32[]{:S(2)}) collective-permute-start(bf16[5,8,512]{2,1,0:T(8,128)(2,1)S(1)} %get-tuple-element.21), channel_id=1, source_target_pairs={{0,12},{4,8},{8,4},{12,0},{1,13},{5,9},{9,5},{13,1},{2,14},{6,10},... | collective-permute-start | bytes 122888 | tf_op jit(solution)/shard_map/ppermute | solution.py:41

commit v10 on v9

--- a/solution.py
+++ b/solution.py
@@ -462,7 +462,9 @@
 
     early, late = edge_turns(chain, corrected)
     came = over_x(early)
-    kept_y, forwarded = lax.optimization_barrier((kept_y, forwarded))
+    if chain > 1:
+        kept_y, from_far = lax.optimization_barrier((kept_y, [pair[1] for pair in forwarded]))
+        forwarded = [(pair[0], far) for pair, far in zip(forwarded, from_far)]
     operands = []
     for link in range(chain):
         if link:

time: 22.4 us -> 22.4 us (level)
  no operation moved by 1% of the time
where the time goes in v10:
time: 22.4 us; the launch traced here: 22.2 us
  starting transfers between devices  14.7 us (66%)
  Pallas kernels  3.38 us (15%)
  waiting for transfers between devices  2.42 us (11%)
  other arithmetic  1.44 us (6%)
    ppermute x4, starting transfers between devices, neighbours(): first = lax.ppermute(outward, axis, near)  7 us
    ppermute x4, starting transfers between devices, neighbours(): second = lax.ppermute(inward, axis, far)  5.7 us
    pallas_call x1, Pallas kernels, per_device(): pl.pallas_call(functools.partial(advance_kernel, chain, corrected, rows),...  2.81 us
    ppermute x4, waiting for transfers between devices, neighbours(): second = lax.ppermute(inward, axis, far)  2.4 us
    ppermute x3, starting transfers between devices, from_lower(): return lax.ppermute(block, 'sec', route)  2.04 us
    convert_element_type x1, other arithmetic, per_device(): sent = block.astype(jnp.bfloat16)  1.07 us
    pallas_call x1, Pallas kernels, per_device(): pl.pallas_call(functools.partial(first_kernel, chain, corrected, rows), o...  0.57 us
  transfers between devices with their start and end apart: 11, of which 2 were waited for; matrix products, arithmetic and copies ran while one was open for 2% of the time, Pallas kernels for 3%

profile of v10, /device:TPU:3, one launch (start us, length us, event | category | flops | bytes accessed | tf_op | source)
XLA Modules:
  0.0 22.2 jit_solution(17960129897767779537)
XLA Ops:
  0.0 0.0 copy-start
  0.0 1.1 %convert_bitcast_fusion = (bf16[5,32,256]{2,1,0:T(8,128)(2,1)S(1)}, f32[5,32,256]{2,1,0:T(8,128)S(1)}) fusion(f32[1,5,32,256]{3,2,1,0:T(8,128)} %param.3), kind=kLoop, calls=%fused_computation.24 | loop fusion | flops 81920 | bytes 409600 | tf_op jit(solution)/shard_map/convert_element_type | solution.py:417
  1.1 1.4 %collective-permute-start.1 = (bf16[5,32,256]{2,1,0:T(8,128)(2,1)S(1)}, bf16[5,32,256]{2,1,0:T(8,128)(2,1)S(1)}, u32[]{:S(2)}, u32[]{:S(2)}) collective-permute-start(bf16[5,32,256]{2,1,0:T(8,128)(2,1)S(1)} %get-tuple-element.16), channel_id=1, source_target_pairs={{0,1},{1,0},{2,3},{3,2},{4,5},{5,4},{6,7},{7,6},{8,9},{9,8},{10,11... | collective-permute-start | bytes 245768 | tf_op jit(solution)/shard_map/ppermute | solution.py:42
  2.4 0.3 %collective-permute-start.2 = (bf16[5,32,256]{2,1,0:T(8,128)(2,1)S(1)}, bf16[5,32,256]{2,1,0:T(8,128)(2,1)S(1)}, u32[]{:S(2)}, u32[]{:S(2)}) collective-permute-start(bf16[5,32,256]{2,1,0:T(8,128)(2,1)S(1)} %get-tuple-element.16), channel_id=1, source_target_pairs={{0,16},{16,0},{1,17},{17,1},{2,18},{18,2},{3,19},{19,3},{4,20},{20... | collective-permute-start | bytes 245768 | tf_op jit(solution)/shard_map/ppermute | solution.py:51
  2.7 2.2 %collective-permute-start = (bf16[5,32,256]{2,1,0:T(8,128)(2,1)S(1)}, bf16[5,32,256]{2,1,0:T(8,128)(2,1)S(1)}, u32[]{:S(2)}, u32[]{:S(2)}) collective-permute-start(bf16[5,32,256]{2,1,0:T(8,128)(2,1)S(1)} %get-tuple-element.16), channel_id=1, source_target_pairs={{0,3},{1,2},{2,1},{3,0},{4,7},{5,6},{6,5},{7,4},{8,11},{9,10},{10,... | collective-permute-start | bytes 245768 | tf_op jit(solution)/shard_map/ppermute | solution.py:41
  4.9 0.0 copy-done
  4.9 0.1 fusion.5
  5.0 0.5 %collective-permute-start.5 = (bf16[10,32,128]{2,1,0:T(8,128)(2,1)S(1)}, bf16[10,32,128]{2,1,0:T(8,128)(2,1)S(1)}, u32[]{:S(2)}, u32[]{:S(2)}) collective-permute-start(bf16[10,32,128]{2,1,0:T(8,128)(2,1)S(1)} %get-tuple-element.40), channel_id=1, source_target_pairs={{0,1},{1,0},{2,3},{3,2},{4,5},{5,4},{6,7},{7,6},{8,9},{9,8},{10,11... | collective-permute-start | bytes 245768 | tf_op jit(solution)/shard_map/ppermute | solution.py:42
  5.5 0.9 %collective-permute-start.6 = (bf16[10,32,128]{2,1,0:T(8,128)(2,1)S(1)}, bf16[10,32,128]{2,1,0:T(8,128)(2,1)S(1)}, u32[]{:S(2)}, u32[]{:S(2)}) collective-permute-start(bf16[10,32,128]{2,1,0:T(8,128)(2,1)S(1)} %get-tuple-element.39), channel_id=1, source_target_pairs={{0,3},{1,2},{2,1},{3,0},{4,7},{5,6},{6,5},{7,4},{8,11},{9,10},{10,... | collective-permute-start | bytes 245768 | tf_op jit(solution)/shard_map/ppermute | solution.py:41
  6.5 0.0 collective-permute-done.1.refs_4_
  6.5 0.0 collective-permute-done.2.refs_9_
  6.5 1.3 %collective-permute-start.7 = (bf16[5,32,256]{2,1,0:T(8,128)(2,1)S(1)}, bf16[5,32,256]{2,1,0:T(8,128)(2,1)S(1)}, u32[]{:S(2)}, u32[]{:S(2)}) collective-permute-start(bf16[5,32,256]{2,1,0:T(8,128)(2,1)S(1)} %collective-permute-done.1.refs_4_), channel_id=1, source_target_pairs={{0,16},{16,0},{1,17},{17,1},{2,18},{18,2},{3,19},{19,3},{4,20},{20... | collective-permute-start | bytes 245768 | tf_op jit(solution)/shard_map/ppermute | solution.py:51
  7.8 0.8 %collective-permute-done.refs_5_ = bf16[5,32,256]{2,1,0:T(8,128)(2,1)S(1)} collective-permute-done((bf16[5,32,256]{2,1,0:T(8,128)(2,1)S(1)}, bf16[5,32,256]{2,1,0:T(8,128)(2,1)S(1)}, u32[]{:S(2)}, u32[]{:S(2)}) %collective-permute-start) | collective-permute-done | bytes 81952 | tf_op jit(solution)/shard_map/ppermute | solution.py:41
  8.6 0.1 broadcast_select_fusion.6
  8.7 0.5 %collective-permute-start.8 = (bf16[5,32,256]{2,1,0:T(8,128)(2,1)S(1)}, bf16[5,32,256]{2,1,0:T(8,128)(2,1)S(1)}, u32[]{:S(2)}, u32[]{:S(2)}) collective-permute-start(bf16[5,32,256]{2,1,0:T(8,128)(2,1)S(1)} %collective-permute-done.refs_5_), channel_id=1, source_target_pairs={{0,16},{16,0},{1,17},{17,1},{2,18},{18,2},{3,19},{19,3},{4,20},{20... | collective-permute-start | bytes 245768 | tf_op jit(solution)/shard_map/ppermute | solution.py:51
  9.2 2.8 %collective-permute-start.3 = (bf16[5,6,512]{2,1,0:T(8,128)(2,1)S(1)}, bf16[5,6,512]{2,1,0:T(8,128)(2,1)S(1)}, u32[]{:S(2)}, u32[]{:S(2)}) collective-permute-start(bf16[5,6,512]{2,1,0:T(8,128)(2,1)S(1)} %broadcast_select_fusion.7), channel_id=1, source_target_pairs={{0,4},{4,0},{8,12},{12,8},{1,5},{5,1},{9,13},{13,9},{2,6},{6,2},{1... | collective-permute-start | bytes 92168 | tf_op jit(solution)/shard_map/ppermute | solution.py:42
  12.1 0.0 collective-permute-done.5.refs_7_
  12.1 1.4 %collective-permute-start.4 = (bf16[5,6,512]{2,1,0:T(8,128)(2,1)S(1)}, bf16[5,6,512]{2,1,0:T(8,128)(2,1)S(1)}, u32[]{:S(2)}, u32[]{:S(2)}) collective-permute-start(bf16[5,6,512]{2,1,0:T(8,128)(2,1)S(1)} %get-tuple-element.30), channel_id=1, source_target_pairs={{0,12},{4,8},{8,4},{12,0},{1,13},{5,9},{9,5},{13,1},{2,14},{6,10},... | collective-permute-start | bytes 92168 | tf_op jit(solution)/shard_map/ppermute | solution.py:41
  13.5 0.0 collective-permute-done.6.refs_8_
  13.5 0.0 collective-permute-done.7.refs_10_
  13.5 0.0 collective-permute-done.8.refs_11_
  13.5 0.0 copy-start.1
  13.5 0.1 broadcast_select_fusion.4
  13.6 2.3 %collective-permute-start.9 = (bf16[5,8,512]{2,1,0:T(8,128)(2,1)S(1)}, bf16[5,8,512]{2,1,0:T(8,128)(2,1)S(1)}, u32[]{:S(2)}, u32[]{:S(2)}) collective-permute-start(bf16[5,8,512]{2,1,0:T(8,128)(2,1)S(1)} %broadcast_select_fusion.5), channel_id=1, source_target_pairs={{0,4},{4,0},{8,12},{12,8},{1,5},{5,1},{9,13},{13,9},{2,6},{6,2},{1... | collective-permute-start | bytes 122888 | tf_op jit(solution)/shard_map/ppermute | solution.py:42
  16.0 1.2 %collective-permute-start.10 = (bf16[5,8,512]{2,1,0:T(8,128)(2,1)S(1)}, bf16[5,8,512]{2,1,0:T(8,128)(2,1)S(1)}, u32[]{:S(2)}, u32[]{:S(2)}) collective-permute-start(bf16[5,8,512]{2,1,0:T(8,128)(2,1)S(1)} %get-tuple-element.27), channel_id=1, source_target_pairs={{0,12},{4,8},{8,4},{12,0},{1,13},{5,9},{9,5},{13,1},{2,14},{6,10},... | collective-permute-start | bytes 122888 | tf_op jit(solution)/shard_map/ppermute | solution.py:41
  17.2 0.0 collective-permute-done.3
  17.2 0.0 collective-permute-done.4
  17.2 0.0 copy-done.1
  17.2 0.6 %own_first_tick.1.refs_1_ = f32[5,4,40,128]{3,2,1,0:T(8,128)S(1)} custom-call(bf16[1024,256]{1,0:T(8,128)(2,1)S(1)} %copy-done.1, f32[5,6,512]{2,1,0:T(8,128)S(1)} %convert_element_type.27.refs_1_.refs_2_, f32[5,6,512]{2,1,0:T(8,128)S(1)} %convert_element_type.28.refs_2_.refs_3_, f32[5,32,256]{2,1,0:T(8,128)S(1)} %get-tuple-element.18.refs_3_, ...), custom_call_target="tpu_custom_call" | custom-call | flops 400000000 | bytes 1000000 | tf_op jit(solution)/shard_map/own_first_tick/pallas_call | solution.py:492
  17.8 0.0 collective-permute-done.9
  17.8 1.6 %collective-permute-done.10 = bf16[5,8,512]{2,1,0:T(8,128)(2,1)S(1)} collective-permute-done((bf16[5,8,512]{2,1,0:T(8,128)(2,1)S(1)}, bf16[5,8,512]{2,1,0:T(8,128)(2,1)S(1)}, u32[]{:S(2)}, u32[]{:S(2)}) %collective-permute-start.10) | collective-permute-done | bytes 40992 | tf_op jit(solution)/shard_map/ppermute | solution.py:41
  19.4 2.8 %advance.1 = f32[5,32,256]{2,1,0:T(8,128)} custom-call(bf16[1024,256]{1,0:T(8,128)(2,1)S(1)} %copy-done.1, f32[5,4,40,128]{3,2,1,0:T(8,128)S(1)} %own_first_tick.1.refs_1_, f32[5,6,512]{2,1,0:T(8,128)S(1)} %convert_element_type.27.refs_1_.refs_2_, f32[5,6,512]{2,1,0:T(8,128)S(1)} %convert_element_type.28.refs_2_.refs_3_, ...), custom_call_target="tpu_custom_call" | custom-call | tf_op jit(solution)/shard_map/advance/pallas_call | solution.py:503
  (15 shorter events, 0.2 us)
Async XLA Ops:
  0.0 4.9 %copy-start = (bf16[1,3,5,32,256]{4,3,2,1,0:T(8,128)(2,1)S(1)}, bf16[1,3,5,32,256]{4,3,2,1,0:T(8,128)(2,1)}, u32[]{:S(2)}) copy-start(bf16[1,3,5,32,256]{4,3,2,1,0:T(8,128)(2,1)} %param.4) | copy-start | bytes 737284
  1.1 5.4 %collective-permute-start.1 = (bf16[5,32,256]{2,1,0:T(8,128)(2,1)S(1)}, bf16[5,32,256]{2,1,0:T(8,128)(2,1)S(1)}, u32[]{:S(2)}, u32[]{:S(2)}) collective-permute-start(bf16[5,32,256]{2,1,0:T(8,128)(2,1)S(1)} %get-tuple-element.16), channel_id=1, source_target_pairs={{0,1},{1,0},{2,3},{3,2},{4,5},{5,4},{6,7},{7,6},{8,9},{9,8},{10,11... | collective-permute-start | bytes 245768 | tf_op jit(solution)/shard_map/ppermute | solution.py:42
  2.4 4.1 %collective-permute-start.2 = (bf16[5,32,256]{2,1,0:T(8,128)(2,1)S(1)}, bf16[5,32,256]{2,1,0:T(8,128)(2,1)S(1)}, u32[]{:S(2)}, u32[]{:S(2)}) collective-permute-start(bf16[5,32,256]{2,1,0:T(8,128)(2,1)S(1)} %get-tuple-element.16), channel_id=1, source_target_pairs={{0,16},{16,0},{1,17},{17,1},{2,18},{18,2},{3,19},{19,3},{4,20},{20... | collective-permute-start | bytes 245768 | tf_op jit(solution)/shard_map/ppermute | solution.py:51
  2.7 5.9 %collective-permute-start = (bf16[5,32,256]{2,1,0:T(8,128)(2,1)S(1)}, bf16[5,32,256]{2,1,0:T(8,128)(2,1)S(1)}, u32[]{:S(2)}, u32[]{:S(2)}) collective-permute-start(bf16[5,32,256]{2,1,0:T(8,128)(2,1)S(1)} %get-tuple-element.16), channel_id=1, source_target_pairs={{0,3},{1,2},{2,1},{3,0},{4,7},{5,6},{6,5},{7,4},{8,11},{9,10},{10,... | collective-permute-start | bytes 245768 | tf_op jit(solution)/shard_map/ppermute | solution.py:41
  5.0 7.0 %collective-permute-start.5 = (bf16[10,32,128]{2,1,0:T(8,128)(2,1)S(1)}, bf16[10,32,128]{2,1,0:T(8,128)(2,1)S(1)}, u32[]{:S(2)}, u32[]{:S(2)}) collective-permute-start(bf16[10,32,128]{2,1,0:T(8,128)(2,1)S(1)} %get-tuple-element.40), channel_id=1, source_target_pairs={{0,1},{1,0},{2,3},{3,2},{4,5},{5,4},{6,7},{7,6},{8,9},{9,8},{10,11... | collective-permute-start | bytes 245768 | tf_op jit(solution)/shard_map/ppermute | solution.py:42
  5.5 8.0 %collective-permute-start.6 = (bf16[10,32,128]{2,1,0:T(8,128)(2,1)S(1)}, bf16[10,32,128]{2,1,0:T(8,128)(2,1)S(1)}, u32[]{:S(2)}, u32[]{:S(2)}) collective-permute-start(bf16[10,32,128]{2,1,0:T(8,128)(2,1)S(1)} %get-tuple-element.39), channel_id=1, source_target_pairs={{0,3},{1,2},{2,1},{3,0},{4,7},{5,6},{6,5},{7,4},{8,11},{9,10},{10,... | collective-permute-start | bytes 245768 | tf_op jit(solution)/shard_map/ppermute | solution.py:41
  6.5 7.0 %collective-permute-start.7 = (bf16[5,32,256]{2,1,0:T(8,128)(2,1)S(1)}, bf16[5,32,256]{2,1,0:T(8,128)(2,1)S(1)}, u32[]{:S(2)}, u32[]{:S(2)}) collective-permute-start(bf16[5,32,256]{2,1,0:T(8,128)(2,1)S(1)} %collective-permute-done.1.refs_4_), channel_id=1, source_target_pairs={{0,16},{16,0},{1,17},{17,1},{2,18},{18,2},{3,19},{19,3},{4,20},{20... | collective-permute-start | bytes 245768 | tf_op jit(solution)/shard_map/ppermute | solution.py:51
  8.7 4.8 %collective-permute-start.8 = (bf16[5,32,256]{2,1,0:T(8,128)(2,1)S(1)}, bf16[5,32,256]{2,1,0:T(8,128)(2,1)S(1)}, u32[]{:S(2)}, u32[]{:S(2)}) collective-permute-start(bf16[5,32,256]{2,1,0:T(8,128)(2,1)S(1)} %collective-permute-done.refs_5_), channel_id=1, source_target_pairs={{0,16},{16,0},{1,17},{17,1},{2,18},{18,2},{3,19},{19,3},{4,20},{20... | collective-permute-start | bytes 245768 | tf_op jit(solution)/shard_map/ppermute | solution.py:51
  9.2 8.0 %collective-permute-start.3 = (bf16[5,6,512]{2,1,0:T(8,128)(2,1)S(1)}, bf16[5,6,512]{2,1,0:T(8,128)(2,1)S(1)}, u32[]{:S(2)}, u32[]{:S(2)}) collective-permute-start(bf16[5,6,512]{2,1,0:T(8,128)(2,1)S(1)} %broadcast_select_fusion.7), channel_id=1, source_target_pairs={{0,4},{4,0},{8,12},{12,8},{1,5},{5,1},{9,13},{13,9},{2,6},{6,2},{1... | collective-permute-start | bytes 92168 | tf_op jit(solution)/shard_map/ppermute | solution.py:42
  12.1 5.1 %collective-permute-start.4 = (bf16[5,6,512]{2,1,0:T(8,128)(2,1)S(1)}, bf16[5,6,512]{2,1,0:T(8,128)(2,1)S(1)}, u32[]{:S(2)}, u32[]{:S(2)}) collective-permute-start(bf16[5,6,512]{2,1,0:T(8,128)(2,1)S(1)} %get-tuple-element.30), channel_id=1, source_target_pairs={{0,12},{4,8},{8,4},{12,0},{1,13},{5,9},{9,5},{13,1},{2,14},{6,10},... | collective-permute-start | bytes 92168 | tf_op jit(solution)/shard_map/ppermute | solution.py:41
  13.5 3.7 %copy-start.1 = (bf16[1024,256]{1,0:T(8,128)(2,1)S(1)}, bf16[1024,256]{1,0:T(8,128)(2,1)}, u32[]{:S(2)}) copy-start(bf16[1024,256]{1,0:T(8,128)(2,1)} %constant.31.clone.refs_0_) | copy-start | bytes 1572868
  13.6 4.2 %collective-permute-start.9 = (bf16[5,8,512]{2,1,0:T(8,128)(2,1)S(1)}, bf16[5,8,512]{2,1,0:T(8,128)(2,1)S(1)}, u32[]{:S(2)}, u32[]{:S(2)}) collective-permute-start(bf16[5,8,512]{2,1,0:T(8,128)(2,1)S(1)} %broadcast_select_fusion.5), channel_id=1, source_target_pairs={{0,4},{4,0},{8,12},{12,8},{1,5},{5,1},{9,13},{13,9},{2,6},{6,2},{1... | collective-permute-start | bytes 122888 | tf_op jit(solution)/shard_map/ppermute | solution.py:42
  16.0 3.4 %collective-permute-start.10 = (bf16[5,8,512]{2,1,0:T(8,128)(2,1)S(1)}, bf16[5,8,512]{2,1,0:T(8,128)(2,1)S(1)}, u32[]{:S(2)}, u32[]{:S(2)}) collective-permute-start(bf16[5,8,512]{2,1,0:T(8,128)(2,1)S(1)} %get-tuple-element.27), channel_id=1, source_target_pairs={{0,12},{4,8},{8,4},{12,0},{1,13},{5,9},{9,5},{13,1},{2,14},{6,10},... | collective-permute-start | bytes 122888 | tf_op jit(solution)/shard_map/ppermute | solution.py:41

commit v11 on v10

--- a/solution.py
+++ b/solution.py
@@ -97,10 +97,10 @@
     ]
 
 
-def unpack_edges(edges, first, second, even_x):
+def unpack_edges(edges, first, second, even_x, tiles=range(4)):
     count = first.shape[1]
     for field in range(FIELDS):
-        for tile in range(4):
+        for tile in tiles:
             one = first[field, :, lanes(tile)]
             two = second[field, :, lanes(tile)]
             edges[0, field, tile, pl.ds(0, count), :] = jnp.where(even_x, two, one)
@@ -376,8 +376,10 @@
                 update(link, tick, waiting.pop((link, tick)))
 
         if links > 1:
-            for turn in range(2):
-                unpack_edges(edges.at[turn], *came[2 * turn : 2 * turn + 2], even_x)
+            parts = layout["kept", 0, 1][1]
+            used = [first + tile for _, _, tiles, _, first in parts for tile in range(tiles)]
+            unpack_edges(edges.at[0], *came[:2], even_x, used)
+            unpack_edges(edges.at[1], *came[2:], even_x)
         for tick in range(TICKS):
             for link in reversed(range(min(links, TICKS - tick + 1))):
                 if tick == 0:
@@ -512,6 +514,7 @@
             *(scratch_of_level(rows) * chain),
         ],
         compiler_params=params,
+        cost_estimate=pl.CostEstimate(flops=10**9, bytes_accessed=10**6, transcendentals=0),
         name="advance",
     )(matrix, *operands)
     return result[None]

time: 22.4 us -> 22.4 us (level)
  no operation moved by 1% of the time
where the time goes in v11:
time: 22.4 us; the launch traced here: 22.2 us
  starting transfers between devices  14.7 us (66%)
  Pallas kernels  3.38 us (15%)
  waiting for transfers between devices  2.42 us (11%)
  other arithmetic  1.44 us (6%)
    ppermute x4, starting transfers between devices, neighbours(): first = lax.ppermute(outward, axis, near)  7 us
    ppermute x4, starting transfers between devices, neighbours(): second = lax.ppermute(inward, axis, far)  5.7 us
    pallas_call x1, Pallas kernels, per_device(): pl.pallas_call(functools.partial(advance_kernel, chain, corrected, rows),...  2.81 us
    ppermute x4, waiting for transfers between devices, neighbours(): second = lax.ppermute(inward, axis, far)  2.4 us
    ppermute x3, starting transfers between devices, from_lower(): return lax.ppermute(block, 'sec', route)  2.04 us
    convert_element_type x1, other arithmetic, per_device(): sent = block.astype(jnp.bfloat16)  1.07 us
    pallas_call x1, Pallas kernels, per_device(): pl.pallas_call(functools.partial(first_kernel, chain, corrected, rows), o...  0.57 us
  transfers between devices with their start and end apart: 11, of which 2 were waited for; matrix products, arithmetic and copies ran while one was open for 2% of the time, Pallas kernels for 3%

profile of v11, /device:TPU:3, one launch (start us, length us, event | category | flops | bytes accessed | tf_op | source)
XLA Modules:
  0.0 22.2 jit_solution(4223716691094439491)
XLA Ops:
  0.0 0.0 copy-start
  0.0 1.1 %convert_bitcast_fusion = (bf16[5,32,256]{2,1,0:T(8,128)(2,1)S(1)}, f32[5,32,256]{2,1,0:T(8,128)S(1)}) fusion(f32[1,5,32,256]{3,2,1,0:T(8,128)} %param.3), kind=kLoop, calls=%fused_computation.24 | loop fusion | flops 81920 | bytes 409600 | tf_op jit(solution)/shard_map/convert_element_type | solution.py:419
  1.1 1.4 %collective-permute-start.1 = (bf16[5,32,256]{2,1,0:T(8,128)(2,1)S(1)}, bf16[5,32,256]{2,1,0:T(8,128)(2,1)S(1)}, u32[]{:S(2)}, u32[]{:S(2)}) collective-permute-start(bf16[5,32,256]{2,1,0:T(8,128)(2,1)S(1)} %get-tuple-element.16), channel_id=1, source_target_pairs={{0,1},{1,0},{2,3},{3,2},{4,5},{5,4},{6,7},{7,6},{8,9},{9,8},{10,11... | collective-permute-start | bytes 245768 | tf_op jit(solution)/shard_map/ppermute | solution.py:42
  2.4 0.3 %collective-permute-start.2 = (bf16[5,32,256]{2,1,0:T(8,128)(2,1)S(1)}, bf16[5,32,256]{2,1,0:T(8,128)(2,1)S(1)}, u32[]{:S(2)}, u32[]{:S(2)}) collective-permute-start(bf16[5,32,256]{2,1,0:T(8,128)(2,1)S(1)} %get-tuple-element.16), channel_id=1, source_target_pairs={{0,16},{16,0},{1,17},{17,1},{2,18},{18,2},{3,19},{19,3},{4,20},{20... | collective-permute-start | bytes 245768 | tf_op jit(solution)/shard_map/ppermute | solution.py:51
  2.7 2.2 %collective-permute-start = (bf16[5,32,256]{2,1,0:T(8,128)(2,1)S(1)}, bf16[5,32,256]{2,1,0:T(8,128)(2,1)S(1)}, u32[]{:S(2)}, u32[]{:S(2)}) collective-permute-start(bf16[5,32,256]{2,1,0:T(8,128)(2,1)S(1)} %get-tuple-element.16), channel_id=1, source_target_pairs={{0,3},{1,2},{2,1},{3,0},{4,7},{5,6},{6,5},{7,4},{8,11},{9,10},{10,... | collective-permute-start | bytes 245768 | tf_op jit(solution)/shard_map/ppermute | solution.py:41
  4.9 0.0 copy-done
  4.9 0.1 fusion.5
  5.0 0.5 %collective-permute-start.5 = (bf16[10,32,128]{2,1,0:T(8,128)(2,1)S(1)}, bf16[10,32,128]{2,1,0:T(8,128)(2,1)S(1)}, u32[]{:S(2)}, u32[]{:S(2)}) collective-permute-start(bf16[10,32,128]{2,1,0:T(8,128)(2,1)S(1)} %get-tuple-element.40), channel_id=1, source_target_pairs={{0,1},{1,0},{2,3},{3,2},{4,5},{5,4},{6,7},{7,6},{8,9},{9,8},{10,11... | collective-permute-start | bytes 245768 | tf_op jit(solution)/shard_map/ppermute | solution.py:42
  5.5 0.9 %collective-permute-start.6 = (bf16[10,32,128]{2,1,0:T(8,128)(2,1)S(1)}, bf16[10,32,128]{2,1,0:T(8,128)(2,1)S(1)}, u32[]{:S(2)}, u32[]{:S(2)}) collective-permute-start(bf16[10,32,128]{2,1,0:T(8,128)(2,1)S(1)} %get-tuple-element.39), channel_id=1, source_target_pairs={{0,3},{1,2},{2,1},{3,0},{4,7},{5,6},{6,5},{7,4},{8,11},{9,10},{10,... | collective-permute-start | bytes 245768 | tf_op jit(solution)/shard_map/ppermute | solution.py:41
  6.5 0.0 collective-permute-done.1.refs_4_
  6.5 0.0 collective-permute-done.2.refs_9_
  6.5 1.3 %collective-permute-start.7 = (bf16[5,32,256]{2,1,0:T(8,128)(2,1)S(1)}, bf16[5,32,256]{2,1,0:T(8,128)(2,1)S(1)}, u32[]{:S(2)}, u32[]{:S(2)}) collective-permute-start(bf16[5,32,256]{2,1,0:T(8,128)(2,1)S(1)} %collective-permute-done.1.refs_4_), channel_id=1, source_target_pairs={{0,16},{16,0},{1,17},{17,1},{2,18},{18,2},{3,19},{19,3},{4,20},{20... | collective-permute-start | bytes 245768 | tf_op jit(solution)/shard_map/ppermute | solution.py:51
  7.8 0.8 %collective-permute-done.refs_5_ = bf16[5,32,256]{2,1,0:T(8,128)(2,1)S(1)} collective-permute-done((bf16[5,32,256]{2,1,0:T(8,128)(2,1)S(1)}, bf16[5,32,256]{2,1,0:T(8,128)(2,1)S(1)}, u32[]{:S(2)}, u32[]{:S(2)}) %collective-permute-start) | collective-permute-done | bytes 81952 | tf_op jit(solution)/shard_map/ppermute | solution.py:41
  8.6 0.1 broadcast_select_fusion.6
  8.7 0.5 %collective-permute-start.8 = (bf16[5,32,256]{2,1,0:T(8,128)(2,1)S(1)}, bf16[5,32,256]{2,1,0:T(8,128)(2,1)S(1)}, u32[]{:S(2)}, u32[]{:S(2)}) collective-permute-start(bf16[5,32,256]{2,1,0:T(8,128)(2,1)S(1)} %collective-permute-done.refs_5_), channel_id=1, source_target_pairs={{0,16},{16,0},{1,17},{17,1},{2,18},{18,2},{3,19},{19,3},{4,20},{20... | collective-permute-start | bytes 245768 | tf_op jit(solution)/shard_map/ppermute | solution.py:51
  9.2 2.8 %collective-permute-start.3 = (bf16[5,6,512]{2,1,0:T(8,128)(2,1)S(1)}, bf16[5,6,512]{2,1,0:T(8,128)(2,1)S(1)}, u32[]{:S(2)}, u32[]{:S(2)}) collective-permute-start(bf16[5,6,512]{2,1,0:T(8,128)(2,1)S(1)} %broadcast_select_fusion.7), channel_id=1, source_target_pairs={{0,4},{4,0},{8,12},{12,8},{1,5},{5,1},{9,13},{13,9},{2,6},{6,2},{1... | collective-permute-start | bytes 92168 | tf_op jit(solution)/shard_map/ppermute | solution.py:42
  12.1 0.0 collective-permute-done.5.refs_7_
  12.1 1.4 %collective-permute-start.4 = (bf16[5,6,512]{2,1,0:T(8,128)(2,1)S(1)}, bf16[5,6,512]{2,1,0:T(8,128)(2,1)S(1)}, u32[]{:S(2)}, u32[]{:S(2)}) collective-permute-start(bf16[5,6,512]{2,1,0:T(8,128)(2,1)S(1)} %get-tuple-element.30), channel_id=1, source_target_pairs={{0,12},{4,8},{8,4},{12,0},{1,13},{5,9},{9,5},{13,1},{2,14},{6,10},... | collective-permute-start | bytes 92168 | tf_op jit(solution)/shard_map/ppermute | solution.py:41
  13.5 0.0 collective-permute-done.6.refs_8_
  13.5 0.0 collective-permute-done.7.refs_10_
  13.5 0.0 collective-permute-done.8.refs_11_
  13.5 0.0 copy-start.1
  13.5 0.1 broadcast_select_fusion.4
  13.6 2.3 %collective-permute-start.9 = (bf16[5,8,512]{2,1,0:T(8,128)(2,1)S(1)}, bf16[5,8,512]{2,1,0:T(8,128)(2,1)S(1)}, u32[]{:S(2)}, u32[]{:S(2)}) collective-permute-start(bf16[5,8,512]{2,1,0:T(8,128)(2,1)S(1)} %broadcast_select_fusion.5), channel_id=1, source_target_pairs={{0,4},{4,0},{8,12},{12,8},{1,5},{5,1},{9,13},{13,9},{2,6},{6,2},{1... | collective-permute-start | bytes 122888 | tf_op jit(solution)/shard_map/ppermute | solution.py:42
  16.0 1.2 %collective-permute-start.10 = (bf16[5,8,512]{2,1,0:T(8,128)(2,1)S(1)}, bf16[5,8,512]{2,1,0:T(8,128)(2,1)S(1)}, u32[]{:S(2)}, u32[]{:S(2)}) collective-permute-start(bf16[5,8,512]{2,1,0:T(8,128)(2,1)S(1)} %get-tuple-element.27), channel_id=1, source_target_pairs={{0,12},{4,8},{8,4},{12,0},{1,13},{5,9},{9,5},{13,1},{2,14},{6,10},... | collective-permute-start | bytes 122888 | tf_op jit(solution)/shard_map/ppermute | solution.py:41
  17.2 0.0 collective-permute-done.3
  17.2 0.0 collective-permute-done.4
  17.2 0.0 copy-done.1
  17.2 0.6 %own_first_tick.1.refs_1_ = f32[5,4,40,128]{3,2,1,0:T(8,128)S(1)} custom-call(bf16[1024,256]{1,0:T(8,128)(2,1)S(1)} %copy-done.1, f32[5,6,512]{2,1,0:T(8,128)S(1)} %convert_element_type.27.refs_1_.refs_2_, f32[5,6,512]{2,1,0:T(8,128)S(1)} %convert_element_type.28.refs_2_.refs_3_, f32[5,32,256]{2,1,0:T(8,128)S(1)} %get-tuple-element.18.refs_3_, ...), custom_call_target="tpu_custom_call" | custom-call | flops 400000000 | bytes 1000000 | tf_op jit(solution)/shard_map/own_first_tick/pallas_call | solution.py:494
  17.8 0.0 collective-permute-done.9
  17.8 1.6 %collective-permute-done.10 = bf16[5,8,512]{2,1,0:T(8,128)(2,1)S(1)} collective-permute-done((bf16[5,8,512]{2,1,0:T(8,128)(2,1)S(1)}, bf16[5,8,512]{2,1,0:T(8,128)(2,1)S(1)}, u32[]{:S(2)}, u32[]{:S(2)}) %collective-permute-start.10) | collective-permute-done | bytes 40992 | tf_op jit(solution)/shard_map/ppermute | solution.py:41
  19.4 2.8 %advance.1 = f32[5,32,256]{2,1,0:T(8,128)} custom-call(bf16[1024,256]{1,0:T(8,128)(2,1)S(1)} %copy-done.1, f32[5,4,40,128]{3,2,1,0:T(8,128)S(1)} %own_first_tick.1.refs_1_, f32[5,6,512]{2,1,0:T(8,128)S(1)} %convert_element_type.27.refs_1_.refs_2_, f32[5,6,512]{2,1,0:T(8,128)S(1)} %convert_element_type.28.refs_2_.refs_3_, ...), custom_call_target="tpu_custom_call" | custom-call | flops 1000000000 | bytes 1000000 | tf_op jit(solution)/shard_map/advance/pallas_call | solution.py:505
  (15 shorter events, 0.2 us)
Async XLA Ops:
  0.0 4.9 %copy-start = (bf16[1,3,5,32,256]{4,3,2,1,0:T(8,128)(2,1)S(1)}, bf16[1,3,5,32,256]{4,3,2,1,0:T(8,128)(2,1)}, u32[]{:S(2)}) copy-start(bf16[1,3,5,32,256]{4,3,2,1,0:T(8,128)(2,1)} %param.4) | copy-start | bytes 737284
  1.1 5.4 %collective-permute-start.1 = (bf16[5,32,256]{2,1,0:T(8,128)(2,1)S(1)}, bf16[5,32,256]{2,1,0:T(8,128)(2,1)S(1)}, u32[]{:S(2)}, u32[]{:S(2)}) collective-permute-start(bf16[5,32,256]{2,1,0:T(8,128)(2,1)S(1)} %get-tuple-element.16), channel_id=1, source_target_pairs={{0,1},{1,0},{2,3},{3,2},{4,5},{5,4},{6,7},{7,6},{8,9},{9,8},{10,11... | collective-permute-start | bytes 245768 | tf_op jit(solution)/shard_map/ppermute | solution.py:42
  2.4 4.1 %collective-permute-start.2 = (bf16[5,32,256]{2,1,0:T(8,128)(2,1)S(1)}, bf16[5,32,256]{2,1,0:T(8,128)(2,1)S(1)}, u32[]{:S(2)}, u32[]{:S(2)}) collective-permute-start(bf16[5,32,256]{2,1,0:T(8,128)(2,1)S(1)} %get-tuple-element.16), channel_id=1, source_target_pairs={{0,16},{16,0},{1,17},{17,1},{2,18},{18,2},{3,19},{19,3},{4,20},{20... | collective-permute-start | bytes 245768 | tf_op jit(solution)/shard_map/ppermute | solution.py:51
  2.7 5.9 %collective-permute-start = (bf16[5,32,256]{2,1,0:T(8,128)(2,1)S(1)}, bf16[5,32,256]{2,1,0:T(8,128)(2,1)S(1)}, u32[]{:S(2)}, u32[]{:S(2)}) collective-permute-start(bf16[5,32,256]{2,1,0:T(8,128)(2,1)S(1)} %get-tuple-element.16), channel_id=1, source_target_pairs={{0,3},{1,2},{2,1},{3,0},{4,7},{5,6},{6,5},{7,4},{8,11},{9,10},{10,... | collective-permute-start | bytes 245768 | tf_op jit(solution)/shard_map/ppermute | solution.py:41
  5.0 7.0 %collective-permute-start.5 = (bf16[10,32,128]{2,1,0:T(8,128)(2,1)S(1)}, bf16[10,32,128]{2,1,0:T(8,128)(2,1)S(1)}, u32[]{:S(2)}, u32[]{:S(2)}) collective-permute-start(bf16[10,32,128]{2,1,0:T(8,128)(2,1)S(1)} %get-tuple-element.40), channel_id=1, source_target_pairs={{0,1},{1,0},{2,3},{3,2},{4,5},{5,4},{6,7},{7,6},{8,9},{9,8},{10,11... | collective-permute-start | bytes 245768 | tf_op jit(solution)/shard_map/ppermute | solution.py:42
  5.5 8.0 %collective-permute-start.6 = (bf16[10,32,128]{2,1,0:T(8,128)(2,1)S(1)}, bf16[10,32,128]{2,1,0:T(8,128)(2,1)S(1)}, u32[]{:S(2)}, u32[]{:S(2)}) collective-permute-start(bf16[10,32,128]{2,1,0:T(8,128)(2,1)S(1)} %get-tuple-element.39), channel_id=1, source_target_pairs={{0,3},{1,2},{2,1},{3,0},{4,7},{5,6},{6,5},{7,4},{8,11},{9,10},{10,... | collective-permute-start | bytes 245768 | tf_op jit(solution)/shard_map/ppermute | solution.py:41
  6.5 7.0 %collective-permute-start.7 = (bf16[5,32,256]{2,1,0:T(8,128)(2,1)S(1)}, bf16[5,32,256]{2,1,0:T(8,128)(2,1)S(1)}, u32[]{:S(2)}, u32[]{:S(2)}) collective-permute-start(bf16[5,32,256]{2,1,0:T(8,128)(2,1)S(1)} %collective-permute-done.1.refs_4_), channel_id=1, source_target_pairs={{0,16},{16,0},{1,17},{17,1},{2,18},{18,2},{3,19},{19,3},{4,20},{20... | collective-permute-start | bytes 245768 | tf_op jit(solution)/shard_map/ppermute | solution.py:51
  8.7 4.8 %collective-permute-start.8 = (bf16[5,32,256]{2,1,0:T(8,128)(2,1)S(1)}, bf16[5,32,256]{2,1,0:T(8,128)(2,1)S(1)}, u32[]{:S(2)}, u32[]{:S(2)}) collective-permute-start(bf16[5,32,256]{2,1,0:T(8,128)(2,1)S(1)} %collective-permute-done.refs_5_), channel_id=1, source_target_pairs={{0,16},{16,0},{1,17},{17,1},{2,18},{18,2},{3,19},{19,3},{4,20},{20... | collective-permute-start | bytes 245768 | tf_op jit(solution)/shard_map/ppermute | solution.py:51
  9.2 8.0 %collective-permute-start.3 = (bf16[5,6,512]{2,1,0:T(8,128)(2,1)S(1)}, bf16[5,6,512]{2,1,0:T(8,128)(2,1)S(1)}, u32[]{:S(2)}, u32[]{:S(2)}) collective-permute-start(bf16[5,6,512]{2,1,0:T(8,128)(2,1)S(1)} %broadcast_select_fusion.7), channel_id=1, source_target_pairs={{0,4},{4,0},{8,12},{12,8},{1,5},{5,1},{9,13},{13,9},{2,6},{6,2},{1... | collective-permute-start | bytes 92168 | tf_op jit(solution)/shard_map/ppermute | solution.py:42
  12.1 5.1 %collective-permute-start.4 = (bf16[5,6,512]{2,1,0:T(8,128)(2,1)S(1)}, bf16[5,6,512]{2,1,0:T(8,128)(2,1)S(1)}, u32[]{:S(2)}, u32[]{:S(2)}) collective-permute-start(bf16[5,6,512]{2,1,0:T(8,128)(2,1)S(1)} %get-tuple-element.30), channel_id=1, source_target_pairs={{0,12},{4,8},{8,4},{12,0},{1,13},{5,9},{9,5},{13,1},{2,14},{6,10},... | collective-permute-start | bytes 92168 | tf_op jit(solution)/shard_map/ppermute | solution.py:41
  13.5 3.7 %copy-start.1 = (bf16[1024,256]{1,0:T(8,128)(2,1)S(1)}, bf16[1024,256]{1,0:T(8,128)(2,1)}, u32[]{:S(2)}) copy-start(bf16[1024,256]{1,0:T(8,128)(2,1)} %constant.31.clone.refs_0_) | copy-start | bytes 1572868
  13.6 4.2 %collective-permute-start.9 = (bf16[5,8,512]{2,1,0:T(8,128)(2,1)S(1)}, bf16[5,8,512]{2,1,0:T(8,128)(2,1)S(1)}, u32[]{:S(2)}, u32[]{:S(2)}) collective-permute-start(bf16[5,8,512]{2,1,0:T(8,128)(2,1)S(1)} %broadcast_select_fusion.5), channel_id=1, source_target_pairs={{0,4},{4,0},{8,12},{12,8},{1,5},{5,1},{9,13},{13,9},{2,6},{6,2},{1... | collective-permute-start | bytes 122888 | tf_op jit(solution)/shard_map/ppermute | solution.py:42
  16.0 3.4 %collective-permute-start.10 = (bf16[5,8,512]{2,1,0:T(8,128)(2,1)S(1)}, bf16[5,8,512]{2,1,0:T(8,128)(2,1)S(1)}, u32[]{:S(2)}, u32[]{:S(2)}) collective-permute-start(bf16[5,8,512]{2,1,0:T(8,128)(2,1)S(1)} %get-tuple-element.27), channel_id=1, source_target_pairs={{0,12},{4,8},{8,4},{12,0},{1,13},{5,9},{9,5},{13,1},{2,14},{6,10},... | collective-permute-start | bytes 122888 | tf_op jit(solution)/shard_map/ppermute | solution.py:41
